TPU v7x, 32 devices: a whole 2x2x4 slice. The times are simulated.
32 devices in a mesh: groups: 2 (over y), seq: 4 (over z), chan: 4 (over x, core).
Axes of the slice: x: 2, y: 2, z: 4, core: 2. Of those that a mesh axis runs over, the one named last changes fastest.
Arguments:
- se_qkv: bfloat16 [3, 2560, 8192], P(None, ('groups', 'seq'), 'chan'), parts along dimension 1, may hold values from -6 to 6
- se_short: float32 [3, 3, 8192], P(None, None, 'chan'), may hold values from -3.5 to 3.5
- se_filter: float32 [7, 8192], P(None, 'chan'), may hold values from -2 to 2
- mr_qkv: bfloat16 [3, 2560, 8192], P(None, ('groups', 'seq'), 'chan'), parts along dimension 1, may hold values from -6 to 6
- mr_short: float32 [3, 3, 8192], P(None, None, 'chan'), may hold values from -3.5 to 3.5
- mr_filter: float32 [128, 8192], P(None, 'chan'), may hold values from -1 to 1
- mr_decay: float32 [8192], P('chan'), may hold values from 0.004 to 0.1
- attn_qkv: bfloat16 [3, 2560, 8192], P(None, ('groups', 'seq'), 'chan'), parts along dimension 1, may hold values from -140 to 140, as said below
Outputs:
- se_out: bfloat16 [2560, 8192], P(('groups', 'seq'), 'chan'), parts along dimension 0
- mr_out: bfloat16 [2560, 8192], P(('groups', 'seq'), 'chan'), parts along dimension 0
- attn_out: bfloat16 [2560, 8192], P(('groups', 'seq'), 'chan'), parts along dimension 0
There are 2 independent parts, one for each index of `groups`. A program takes and returns all parts, laid end to end along the dimension named above; an argument that names none is the same for every part. Nothing has to cross between parts.
Inputs may be any that keep to these rules, and one draw needn't show every extreme that they name: `attn_qkv`: Queries, keys and values of attention as bfloat16 numbers of order one; some queries may be large.
All inputs are finite; a program needn't handle non-finite values.
Results may differ from a plain program's by a relative error of at most 0.0035.
Values may be sent and summed in bfloat16 or wider, within the bound.
No kernel may reach another device: no remote copies, remote signals or barrier semaphores. Data moves between devices by JAX's collectives and lax.ppermute only.
A program may use at most 128 MiB of HBM per device.

v0:
```python
import jax
import jax.numpy as jnp
from jax import lax
from jax.sharding import PartitionSpec as P

HD = 128


def passed_along(value, axis, steps):
    count = lax.axis_size(axis)
    initial, last = (max(0, -steps), min(count, count - steps))
    return lax.ppermute(value, axis, [(source, source + steps) for source in range(initial, last)])


def causal_valid(extended, taps):
    width = extended.shape[1]
    flipped = taps[::-1][:, None, :]
    result = lax.conv_general_dilated(
        extended[None],
        flipped,
        (1,),
        "VALID",
        dimension_numbers=("NHC", "HIO", "NHC"),
        feature_group_count=width,
        precision=lax.Precision.HIGHEST,
    )
    return result[0]


def hyena_local(query_ext, keys_ext, short_taps, filter_taps):
    query_f = causal_valid(query_ext.astype(jnp.float32), short_taps[:, 0])
    key_f = causal_valid(keys_ext[0].astype(jnp.float32), short_taps[:, 1])
    val_f = causal_valid(keys_ext[1].astype(jnp.float32), short_taps[:, 2])
    return (query_f * causal_valid(key_f * val_f, filter_taps)).astype(jnp.bfloat16)


def attend(state, query, positions, pair, start):
    count = pair.shape[1]
    heads = query.shape[1]
    keyrows = pair[0].reshape(count, heads, HD)
    valrows = pair[1].reshape(count, heads, HD)

    def compute(inner):
        peak, total, accum = inner
        scores = jnp.einsum(
            "qhd,khd->hqk", query, keyrows, preferred_element_type=jnp.float32
        ) / jnp.sqrt(jnp.float32(HD))
        key_pos = jnp.arange(count)
        visible = (key_pos[None, :] <= positions[:, None])[None]
        scores = jnp.where(visible, scores, jnp.float32(-1e30))
        fresh = jnp.maximum(peak, jnp.max(scores, axis=2))
        weights = jnp.where(visible, jnp.exp(scores - fresh[:, :, None]), jnp.float32(0.0))
        factor = jnp.exp(peak - fresh)
        total = jnp.sum(weights, axis=2)
        update = jnp.einsum(
            "hqk,khd->qhd",
            weights.astype(jnp.bfloat16),
            valrows,
            preferred_element_type=jnp.float32,
        )
        accum = accum * factor.T[:, :, None] + update
        return (fresh, total, accum)

    return lax.cond(start <= jnp.max(positions), compute, lambda inner: inner, state)


def start_state(query):
    rows, heads = (query.shape[0], query.shape[1])
    return (
        jnp.full((heads, rows), -1e30, jnp.float32),
        jnp.zeros((heads, rows), jnp.float32),
        jnp.zeros((rows, heads, HD), jnp.float32),
    )


def finish(state):
    peak, total, accum = state
    rows, heads = (accum.shape[0], accum.shape[1])
    return (accum / total.T[:, :, None]).reshape(rows, heads * HD).astype(jnp.bfloat16)


def on_device(se_qkv, se_short, se_filter, mr_qkv, mr_short, mr_filter, mr_decay, attn_qkv):
    rows = se_qkv.shape[1]
    lead = se_short.shape[0] - 1
    se_reach = lead + se_filter.shape[0] - 1
    mr_reach = lead + mr_filter.shape[0] - 1
    tails = (
        se_qkv[0, rows - lead :],
        se_qkv[1:, rows - se_reach :],
        mr_qkv[0, rows - lead :],
        mr_qkv[1:, rows - mr_reach :],
    )
    se_qtail, se_kvtail, mr_qtail, mr_kvtail = passed_along(
        (tails[0], tails[1], tails[2], tails[3]), "seq", 1
    )
    steps_idx = jnp.arange(mr_filter.shape[0]).astype(jnp.float32)
    mr_taps = mr_filter * jnp.exp(-mr_decay[None, :] * steps_idx[:, None])
    index = lax.axis_index("seq")
    width = attn_qkv.shape[2]
    heads = width // HD
    query = attn_qkv[0].reshape(rows, heads, HD)
    base = index * rows
    pairs_local = attn_qkv[1:]
    groups = ((query, base + jnp.arange(rows)),)

    def fold_all(states, pair, start):
        return tuple(
            (attend(state, group[0], group[1], pair, start) for state, group in zip(states, groups))
        )

    initial = tuple((start_state(group[0]) for group in groups))
    se_out = hyena_local(
        jnp.concatenate([se_qtail, se_qkv[0]], axis=0),
        jnp.concatenate([se_kvtail, se_qkv[1:]], axis=1),
        se_short,
        se_filter,
    )
    mr_out = hyena_local(
        jnp.concatenate([mr_qtail, mr_qkv[0]], axis=0),
        jnp.concatenate([mr_kvtail, mr_qkv[1:]], axis=1),
        mr_short,
        mr_taps,
    )
    states = fold_all(initial, lax.all_gather(pairs_local, "seq", axis=1, tiled=True), jnp.int32(0))
    results = [finish(state) for state in states]
    attn_out = results[0]
    return (se_out, mr_out, attn_out)


def solution(mesh):
    in_specs = (
        P(None, ("groups", "seq"), "chan"),
        P(None, None, "chan"),
        P(None, "chan"),
        P(None, ("groups", "seq"), "chan"),
        P(None, None, "chan"),
        P(None, "chan"),
        P("chan"),
        P(None, ("groups", "seq"), "chan"),
    )
    out_specs = (
        P(("groups", "seq"), "chan"),
        P(("groups", "seq"), "chan"),
        P(("groups", "seq"), "chan"),
    )
    return jax.shard_map(
        on_device, mesh=mesh, in_specs=in_specs, out_specs=out_specs, check_vma=False
    )
```

profile of v0, /device:TPU:26, one launch (start us, length us, event | category | flops | bytes accessed | tf_op | source)
XLA Modules:
  0.0 305.1 jit_solution(69801989854182917)
XLA Ops:
  8.9 4.3 %copy.90 = bf16[2,320,2048]{2,0,1:T(2,128)(2,1)} copy(bf16[2,320,2048]{2,1,0:T(8,128)(2,1)S(1)} %slice-done) | data formatting | bytes 5242880
  17.5 2.5 slice.81
  25.1 3.2 %slice_bitcast_fusion.3 = bf16[320,2048]{1,0:T(8,128)(2,1)} fusion(bf16[3,320,2048]{2,1,0:T(8,128)(2,1)} %param.10), kind=kLoop, calls=%fused_computation.94 | loop fusion | bytes 2621440 | tf_op jit(solution)/shard_map/squeeze | solution.py:113
  35.6 8.9 %rev.31 = f32[128,2048]{1,0:T(8,128)} reverse(f32[128,2048]{1,0:T(8,128)} %exponential_multiply_fusion), dimensions={0} | reverse | bytes 2097152 | tf_op jit(solution)/shard_map/rev | solution.py:17
  45.2 51.7 %collective-permute-done.2 = bf16[2,2048]{1,0:T(2,128)(2,1)S(1)} collective-permute-done((bf16[2,2048]{1,0:T(2,128)(2,1)S(1)}, bf16[2,2048]{1,0:T(2,128)(2,1)S(1)}, u32[]{:S(2)}, u32[]{:S(2)}) %collective-permute-start.2) | collective-permute-done | bytes 8224 | tf_op jit(solution)/shard_map/ppermute | solution.py:12
  99.7 3.0 reshape.67
  102.7 2.2 copy.65
  104.9 2.8 convolution_select_fusion
  109.4 2.9 reshape.47
  112.3 2.3 copy.54
  115.7 3.2 %copy.67 = f32[8,41,2048]{2,1,0:T(8,128)} copy(f32[8,41,2048]{2,0,1:T(8,128)S(1)} %copy-done.5) | data formatting | bytes 5373952 | tf_op jit(solution)/shard_map/conv_general_dilated | solution.py:18
  118.9 6.1 %reshape.99 = f32[1,328,2048]{2,0,1:T(1,128)} reshape(f32[8,41,2048]{2,1,0:T(8,128)} %copy.67) | data formatting | bytes 5373952 | tf_op jit(solution)/shard_map/conv_general_dilated | solution.py:18
  125.0 3.5 %fusion.73 = (bf16[1,328,2048]{2,1,0:T(8,128)(2,1)}, bf16[1,328,2048]{2,1,0:T(8,128)(2,1)}) fusion(bf16[2,8,2048]{2,1,0:T(8,128)(2,1)S(1)} %collective-permute-done.1, bf16[2,320,2048]{2,1,0:T(8,128)(2,1)} %slice.73), kind=kLoop, calls=%fused_computation.86 | loop fusion | flops 5373952 | bytes 5373952 | tf_op jit(solution)/shard_map/concatenate | solution.py:114
  128.6 3.0 reshape.57
  131.5 2.2 copy.60
  134.8 3.0 reshape.52
  137.8 2.3 copy.57
  147.2 2.9 reshape.64
  150.1 2.5 slice_bitcast_fusion.1
  155.4 3.4 %reshape.72 = bf16[1,8,57,2048]{3,2,1,0:T(8,128)(2,1)} reshape(bf16[1,456,2048]{2,1,0:T(8,128)(2,1)} %pad.7) | data formatting | bytes 3735552 | tf_op jit(solution)/shard_map/conv_general_dilated | solution.py:18
  158.9 2.6 copy.70
  162.8 2.6 fusion.46
  171.7 4.2 %copy.75 = f32[8,57,2048]{2,1,0:T(8,128)} copy(f32[8,57,2048]{2,0,1:T(8,128)S(1)} %select_multiply_fusion) | data formatting | bytes 7471104 | tf_op jit(solution)/shard_map/mul | solution.py:34
  175.9 7.1 %reshape.100 = f32[1,456,2048]{2,0,1:T(1,128)} reshape(f32[8,57,2048]{2,1,0:T(8,128)} %copy.75) | data formatting | bytes 7471104 | tf_op jit(solution)/shard_map/mul | solution.py:34
  183.0 26.3 %fusion.31 = bf16[1,320,2048]{2,0,1:T(2,128)(2,1)S(1)} fusion(f32[1,328,2048]{2,0,1:T(1,128)S(1)} %copy-done.4, f32[1,456,2048]{2,0,1:T(1,128)} %reshape.100, f32[128,1,2048]{2,0,1:T(8,128)} %bitcast.85), kind=kOutput, calls=%fused_computation.49 | convolution fusion | flops 1007943680 | bytes 8716288 | tf_op jit(solution)/shard_map/conv_general_dilated | solution.py:18
  211.2 8.1 %all-gather.2.cloned.1.call-done = bf16[2,1280,2048]{2,0,1:T(2,128)(2,1)} async-done(((bf16[2,320,2048]{2,0,1:T(2,128)(2,1)}), bf16[2,1280,2048]{2,0,1:T(2,128)(2,1)}) %all-gather.2.cloned.1.call-update) | async-done | bytes 10485776 | tf_op jit(solution)/shard_map/all_gather | solution.py:124
  219.3 77.1 %conditional.1 = (f32[16,320]{1,0:T(8,128)S(1)}, f32[320,16,128]{2,0,1:T(8,128)S(1)}) conditional(s32[]{:T(128)} %convert_element_type.42, () %tuple.16, (s32[320]{0:T(512)S(1)}, bf16[3,320,2048]{2,1,0:T(8,128)(2,1)}, bf16[2,1280,2048]{2,0,1:T(2,128)(2,1)}) %tuple.34), branch_computations={%region_1.0_spmd, %region_2.5_spmd} | conditional | flops 3441710080 | bytes 163022128 | solution.py:64
  219.6 26.0 %copy.79 = bf16[2,1280,2048]{1,2,0:T(8,128)(2,1)} copy(bf16[2,1280,2048]{2,0,1:T(2,128)(2,1)} %get-tuple-element.25) | data formatting | bytes 20971520 | tf_op jit(solution)/shard_map
  245.6 8.7 %fusion.111 = (bf16[1,1280,2048]{1,2,0:T(8,128)(2,1)}, bf16[1,1280,2048]{1,2,0:T(8,128)(2,1)}) fusion(bf16[2,1280,2048]{1,2,0:T(8,128)(2,1)} %copy.79), kind=kLoop, calls=%fused_computation.143 | loop fusion | bytes 20971520 | tf_op jit(solution)/shard_map/slice | solution.py:41
  257.2 11.5 %fusion = (f32[16,320]{1,0:T(8,128)S(1)}, f32[16,320,1280]{2,1,0:T(8,128)}) fusion(pred[320,1280]{1,0:T(8,128)(4,1)S(1)} %iota_compare_fusion, bf16[1280,16,128]{0,2,1:T(8,128)(2,1)S(1)} %bitcast.81, bf16[320,16,128]{2,1,0:T(8,128)(2,1)S(1)} %bitcast.82), kind=kOutput, calls=%fused_computation.2 | convolution fusion | flops 1697377280 | bytes 33198080 | tf_op jit(solution)/shard_map/cond/branch_1_fun/qhd,khd->hqk/dot_general | solution.py:45
  268.7 13.8 %bitcast_add_fusion = f32[320,16,128]{2,0,1:T(8,128)S(1)} fusion(bf16[1280,16,128]{0,2,1:T(8,128)(2,1)} %bitcast.83, f32[16,320,1280]{2,1,0:T(8,128)} %get-tuple-element.31, f32[16,320]{1,0:T(8,128)S(1)} %get-tuple-element.29, pred[320,1280]{1,0:T(8,128)(4,1)S(1)} %iota_compare_fusion, f32[320,16]{0,1:T(8,128)S(1)} %get-tuple-element.28), kind=kOutput, calls=%fused_computation.7 | convolution fusion | flops 1711144960 | bytes 34529280 | tf_op jit(solution)/shard_map/cond/branch_1_fun/hqk,khd->qhd/dot_general | solution.py:55
  282.5 13.9 %fusion.2 = f32[16,320]{1,0:T(8,128)S(1)} fusion(f32[16,320,1280]{2,1,0:T(8,128)} %get-tuple-element.31, f32[16,320]{1,0:T(8,128)S(1)} %get-tuple-element.29, pred[320,1280]{1,0:T(8,128)(4,1)S(1)} %iota_compare_fusion), kind=kLoop, calls=%fused_computation.4 | loop fusion | flops 32762880 | bytes 26664960 | tf_op jit(solution)/shard_map/cond/branch_1_fun/reduce_sum | solution.py:54
  (105 shorter events, 49.0 us)
Async XLA Ops:
  7.2 1.7 slice-start
  7.2 212.1 %all-gather.2.cloned.1.call-start = ((), (), s32[]{:S(2)}) async-start(), calls=%async_computation | async-start | bytes 13107200 | tf_op jit(solution)/shard_map/all_gather | solution.py:124
  13.2 10.4 %copy-start.17 = (f32[2048]{0:T(1024)S(1)}, f32[2048]{0:T(1024)}, u32[]{:S(2)}) copy-start(f32[2048]{0:T(1024)} %param.16) | copy-start | bytes 24580
  13.2 10.5 %copy-start.14 = (f32[3,3,2048]{2,1,0:T(4,128)S(1)}, f32[3,3,2048]{2,1,0:T(4,128)}, u32[]{:S(2)}) copy-start(f32[3,3,2048]{2,1,0:T(4,128)} %param.11) | copy-start | bytes 221188
  13.2 10.6 %copy-start.15 = (f32[3,3,2048]{2,1,0:T(4,128)S(1)}, f32[3,3,2048]{2,1,0:T(4,128)}, u32[]{:S(2)}) copy-start(f32[3,3,2048]{2,1,0:T(4,128)} %param.14) | copy-start | bytes 221188
  13.2 10.7 %copy-start.12 = (f32[128,2048]{1,0:T(8,128)S(1)}, f32[128,2048]{1,0:T(8,128)}, u32[]{:S(2)}) copy-start(f32[128,2048]{1,0:T(8,128)} %param.15) | copy-start | bytes 3145732
  14.2 110.9 %collective-permute-start.1 = (bf16[2,8,2048]{2,1,0:T(8,128)(2,1)S(1)}, bf16[2,8,2048]{2,1,0:T(8,128)(2,1)S(1)}, u32[]{:S(2)}, u32[]{:S(2)}) collective-permute-start(bf16[2,8,2048]{2,1,0:T(8,128)(2,1)S(1)} %slice.72), channel_id=1, source_target_pairs={{0,4},{4,8},{8,12},{1,5},{5,9},{9,13},{2,6},{6,10},{10,14},{3,7},{... | collective-permute-start | bytes 196616 | tf_op jit(solution)/shard_map/ppermute | solution.py:12
  16.2 91.5 %collective-permute-start = (bf16[2,2048]{1,0:T(2,128)(2,1)S(1)}, bf16[2,2048]{1,0:T(2,128)(2,1)S(1)}, u32[]{:S(2)}, u32[]{:S(2)}) collective-permute-start(bf16[2,2048]{1,0:T(2,128)(2,1)S(1)} %slice_bitcast_fusion.5), channel_id=1, source_target_pairs={{0,4},{4,8},{8,12},{1,5},{5,9},{9,13},{2,6},{6,10},{10,14},{3,7},{... | collective-permute-start | bytes 24584 | tf_op jit(solution)/shard_map/ppermute | solution.py:12
  20.1 132.6 %collective-permute-start.3 = (bf16[2,129,2048]{2,1,0:T(8,128)(2,1)}, bf16[2,129,2048]{2,1,0:T(8,128)(2,1)}, u32[]{:S(2)}, u32[]{:S(2)}) collective-permute-start(bf16[2,129,2048]{2,1,0:T(8,128)(2,1)} %slice.81), channel_id=1, source_target_pairs={{0,4},{4,8},{8,12},{1,5},{5,9},{9,13},{2,6},{6,10},{10,14},{3,7},{... | collective-permute-start | bytes 3170312 | tf_op jit(solution)/shard_map/ppermute | solution.py:12
  22.1 74.8 %collective-permute-start.2 = (bf16[2,2048]{1,0:T(2,128)(2,1)S(1)}, bf16[2,2048]{1,0:T(2,128)(2,1)S(1)}, u32[]{:S(2)}, u32[]{:S(2)}) collective-permute-start(bf16[2,2048]{1,0:T(2,128)(2,1)S(1)} %slice_bitcast_fusion.4), channel_id=1, source_target_pairs={{0,4},{4,8},{8,12},{1,5},{5,9},{9,13},{2,6},{6,10},{10,14},{3,7},{... | collective-permute-start | bytes 24584 | tf_op jit(solution)/shard_map/ppermute | solution.py:12
  23.6 4.6 %copy-start.1 = (bf16[3,320,2048]{2,1,0:T(8,128)(2,1)S(1)}, bf16[3,320,2048]{2,1,0:T(8,128)(2,1)}, u32[]{:S(2)}) copy-start(bf16[3,320,2048]{2,1,0:T(8,128)(2,1)} %param.13) | copy-start | bytes 11796484
  25.1 5.0 %copy-start.3 = (bf16[3,320,2048]{2,1,0:T(8,128)(2,1)S(1)}, bf16[3,320,2048]{2,1,0:T(8,128)(2,1)}, u32[]{:S(2)}) copy-start(bf16[3,320,2048]{2,1,0:T(8,128)(2,1)} %param.10) | copy-start | bytes 11796484
  31.8 1.7 copy-start.13
  99.7 5.2 %copy-start.19 = (pred[8,41]{0,1:T(8,128)(4,1)S(1)}, pred[8,41]{0,1:T(8,128)(4,1)}, u32[]{:S(2)}) copy-start(pred[8,41]{0,1:T(8,128)(4,1)} %constant.66) | copy-start | bytes 988
  104.9 2.8 copy-start.2
  112.3 3.4 %copy-start.5 = (f32[8,41,2048]{2,0,1:T(8,128)S(1)}, f32[8,41,2048]{2,0,1:T(8,128)}, u32[]{:S(2)}) copy-start(f32[8,41,2048]{2,0,1:T(8,128)} %convolution_select_fusion) | copy-start | bytes 8060932
  114.6 1.1 copy-start.8
  133.7 1.1 copy-start.10
  134.8 5.3 %copy-start.20 = (pred[8,41]{0,1:T(8,128)(4,1)S(1)}, pred[8,41]{0,1:T(8,128)(4,1)}, u32[]{:S(2)}) copy-start(pred[8,41]{0,1:T(8,128)(4,1)} %constant.67) | copy-start | bytes 988
  137.8 2.3 copy-start.11
  141.8 1.6 copy-start.9
  161.5 1.3 copy-start.6
  167.5 1.5 copy-start.7
  169.1 1.4 copy-start.18
  175.9 7.1 %copy-start.4 = (f32[1,328,2048]{2,0,1:T(1,128)S(1)}, f32[1,328,2048]{2,0,1:T(1,128)}, u32[]{:S(2)}) copy-start(f32[1,328,2048]{2,0,1:T(1,128)} %reshape.99) | copy-start | bytes 8060932
  209.3 10.0 %copy-start.16 = (s32[320]{0:T(512)S(1)}, s32[320]{0:T(512)}, u32[]{:S(2)}) copy-start(s32[320]{0:T(512)} %iota_add_fusion) | copy-start | bytes 3844
  254.3 2.9 copy-start
Sparse Core Ops, SparseCore 0:
  13.3 205.9 all-gather.1
where the time goes:
time: 311 us; the launch traced here: 305 us
  local copies, waits for them, and re-layouts  135 us (43%)
  matrix products  62 us (20%)
  waiting for transfers between devices  59.8 us (19%)
  other arithmetic  27.9 us (9%)
  between operations  15.4 us (5%)
  starting transfers between devices  5.36 us (2%)
    ppermute x4, waiting for transfers between devices, passed_along(): lax.ppermute(value, axis, [(source, source + steps) for source in range(i...  51.7 us
    conv_general_dilated x20, local copies, waits for them, and re-layouts, causal_valid(): lax.conv_general_dilated(extended[None], flipped, (1,), 'VALID', dimensio...  39.4 us
    conv_general_dilated x8, matrix products, causal_valid(): lax.conv_general_dilated(extended[None], flipped, (1,), 'VALID', dimensio...  36.7 us
    another operation x1, local copies, waits for them, and re-layouts  26 us
    reduce_sum x1, other arithmetic, compute(): total = jnp.sum(weights, axis=2)  13.9 us
    dot_general x1, matrix products, compute(): jnp.einsum('hqk,khd->qhd', weights.astype(jnp.bfloat16), valrows, preferr...  13.8 us
    rev x8, local copies, waits for them, and re-layouts, causal_valid(): flipped = taps[::-1][:, None, :]  11.8 us
    dot_general x1, matrix products, compute(): jnp.einsum('qhd,khd->hqk', query, keyrows, preferred_element_type=jnp.flo...  11.5 us
  transfers between devices with their start and end apart: 5, of which 2 were waited for; matrix products, arithmetic and copies ran while one was open for 45% of the time, Pallas kernels for 0%

commit v1 on v0

v1 whole, which is shorter than its diff:
```python
import functools

import jax
import jax.numpy as jnp
import ml_dtypes
import numpy as np
from jax import lax
from jax.experimental import pallas as pl
from jax.experimental.pallas import tpu as pltpu
from jax.sharding import PartitionSpec as P

HD = 128
F32 = jnp.float32
BF16 = jnp.bfloat16
SCALE2 = float(np.log2(np.e) / np.sqrt(HD))
CHUNKS = (5, 5, 4, 2)
STAT_ROWS = 16
WINDOW = 256
BLOCK = 128
VMEM_LIMIT = 48 * 1024 * 1024


def split_np(value):
    high = value.astype(ml_dtypes.bfloat16)
    low = (value - high.astype(np.float64)).astype(ml_dtypes.bfloat16)
    return high, low


def transforms():
    bins = np.arange(WINDOW // 2)
    omega = 2.0 * np.pi * (bins + 0.5) / WINDOW
    place = np.arange(WINDOW)
    angle = omega[:, None] * place[None, :]
    forward = np.concatenate([np.cos(angle), -np.sin(angle)], axis=0)
    back = (2.0 / WINDOW) * np.concatenate(
        [np.cos(angle[:, BLOCK:]).T, -np.sin(angle[:, BLOCK:]).T], axis=1
    )
    f_high, f_low = split_np(forward)
    b_high, b_low = split_np(back)
    return np.concatenate([f_high, f_low], axis=0), np.concatenate([b_high, b_low], axis=0)


def halves(value):
    high = value.astype(BF16)
    return high, (value - high.astype(F32)).astype(BF16)


def dot(left, right):
    return jnp.dot(left, right, preferred_element_type=F32)


def forward_of(fwd, x_high):
    both = dot(fwd, x_high)
    return both[:WINDOW] + both[WINDOW:]


def spectral(u_spec, f_spec):
    half = WINDOW // 2
    ur, ui = u_spec[:half], u_spec[half:]
    fr, fi = f_spec[:half], f_spec[half:]
    return jnp.concatenate([ur * fr - ui * fi, ur * fi + ui * fr], axis=0)


def back_of(inv, y_spec):
    high, low = halves(y_spec)
    both = dot(inv, high)
    return both[:BLOCK] + both[BLOCK:] + dot(inv[:BLOCK], low)


def featurize(scratch, taps, first, count):
    return (
        taps[0] * scratch[first : first + count]
        + taps[1] * scratch[first - 1 : first - 1 + count]
        + taps[2] * scratch[first - 2 : first - 2 + count]
    )


def tap_rows(short_ref, which):
    return [short_ref[i, which : which + 1, :] for i in range(3)]


def se_kernel(qkv_ref, tail_ref, short_ref, filt_ref, out_ref, q_s, k_s, v_s, u_s):
    rows = qkv_ref.shape[1]
    width = qkv_ref.shape[2]
    tail = tail_ref[...].astype(F32)
    zero = jnp.zeros((8, width), F32)
    k_s[0:8] = zero
    v_s[0:8] = zero
    k_s[8:16] = tail[0:8]
    v_s[8:16] = tail[8:16]
    q_s[0:8] = jnp.concatenate([zero[:6], tail[16:18]], axis=0)
    q_s[8 : 8 + rows] = qkv_ref[0].astype(F32)
    k_s[16 : 16 + rows] = qkv_ref[1].astype(F32)
    v_s[16 : 16 + rows] = qkv_ref[2].astype(F32)
    tq, tk, tv = (tap_rows(short_ref, j) for j in range(3))
    taps = [filt_ref[i : i + 1, :] for i in range(filt_ref.shape[0])]
    u_s[0:8] = featurize(k_s, tk, 8, 8) * featurize(v_s, tv, 8, 8)
    step = 64
    for r in range(0, rows, step):
        u_s[8 + r : 8 + r + step] = featurize(k_s, tk, 16 + r, step) * featurize(
            v_s, tv, 16 + r, step
        )
    for r in range(0, rows, step):
        acc = taps[0] * u_s[8 + r : 8 + r + step]
        for i in range(1, len(taps)):
            acc = acc + taps[i] * u_s[8 + r - i : 8 + r - i + step]
        out_ref[r : r + step] = (featurize(q_s, tq, 8 + r, step) * acc).astype(BF16)


def mr_tail_kernel(k_ref, v_ref, short_ref, out_ref, k_s, v_s):
    half = k_ref.shape[1]
    k_s[...] = k_ref[0].astype(F32)
    v_s[...] = v_ref[0].astype(F32)
    tk, tv = tap_rows(short_ref, 1), tap_rows(short_ref, 2)
    first = half - BLOCK
    for r in range(0, BLOCK, 64):
        out_ref[r : r + 64] = (
            featurize(k_s, tk, first + r, 64) * featurize(v_s, tv, first + r, 64)
        ).astype(BF16)


def mr_main_kernel(
    qkv_ref, tail_ref, short_ref, filt_ref, decay_ref, fwd_ref, inv_ref,
    out_ref, spec_ref, lead_ref, q_s, k_s, v_s, u_s,
):
    rows = qkv_ref.shape[1]
    width = qkv_ref.shape[2]
    tail = tail_ref[...].astype(F32)
    zero = jnp.zeros((6, width), F32)
    q_s[0:8] = jnp.concatenate([zero, tail[18:20]], axis=0)
    k_s[0:8] = jnp.concatenate([zero, tail[20:22]], axis=0)
    v_s[0:8] = jnp.concatenate([zero, tail[22:24]], axis=0)
    q_s[8 : 8 + rows] = qkv_ref[0].astype(F32)
    k_s[8 : 8 + rows] = qkv_ref[1].astype(F32)
    v_s[8 : 8 + rows] = qkv_ref[2].astype(F32)
    tq, tk, tv = (tap_rows(short_ref, j) for j in range(3))
    step = 64
    for r in range(0, rows, step):
        u_s[r : r + step] = (
            featurize(k_s, tk, 8 + r, step) * featurize(v_s, tv, 8 + r, step)
        ).astype(BF16)
    lead_ref[...] = u_s[0:BLOCK]
    count = filt_ref.shape[0]
    place = lax.broadcasted_iota(jnp.int32, (count, 1), 0).astype(F32)
    taps = filt_ref[...] * jnp.exp(-decay_ref[...] * place)
    t_high, t_low = halves(taps)
    fwd = fwd_ref[...]
    inv = inv_ref[...]
    spec = forward_of(fwd[:, :count], t_high) + dot(fwd[:WINDOW, :count], t_low)
    spec_ref[...] = spec
    for start in range(BLOCK, rows, BLOCK):
        take = min(BLOCK, rows - start)
        window = BLOCK + take
        u_spec = forward_of(fwd[:, :window], u_s[start - BLOCK : start + take])
        mixed = back_of(inv, spectral(u_spec, spec))
        for r in range(0, take, step):
            out_ref[start + r : start + r + step] = (
                featurize(q_s, tq, 8 + start + r, step) * mixed[r : r + step]
            ).astype(BF16)


def mr_head_kernel(
    utail_ref, lead_ref, spec_ref, query_ref, tail_ref, short_ref, fwd_ref, inv_ref, part_ref,
    out_ref, q_s,
):
    del part_ref
    width = query_ref.shape[2]
    tail = tail_ref[...].astype(F32)
    q_s[0:8] = jnp.concatenate([jnp.zeros((6, width), F32), tail[18:20]], axis=0)
    q_s[8 : 8 + BLOCK] = query_ref[0].astype(F32)
    tq = tap_rows(short_ref, 0)
    window = jnp.concatenate([utail_ref[...], lead_ref[...]], axis=0)
    mixed = back_of(inv_ref[...], spectral(forward_of(fwd_ref[...], window), spec_ref[...]))
    for r in range(0, BLOCK, 64):
        out_ref[r : r + 64] = (featurize(q_s, tq, 8 + r, 64) * mixed[r : r + 64]).astype(BF16)


def nt_dot(left, right):
    return lax.dot_general(left, right, (((1,), (1,)), ((), ())), preferred_element_type=F32)


def tt_dot(left, right):
    return lax.dot_general(left, right, (((0,), (0,)), ((), ())), preferred_element_type=F32)


def partial_of(query, pairs, masked=False):
    scores = [nt_dot(keys, query) for keys, _ in pairs]
    if masked:
        shape = scores[0].shape
        below = lax.broadcasted_iota(jnp.int32, shape, 0) <= lax.broadcasted_iota(
            jnp.int32, shape, 1
        )
        scores = [jnp.where(below, scores[0], F32(-1e30))]
    peak = functools.reduce(jnp.maximum, [jnp.max(s, axis=0, keepdims=True) for s in scores])
    weights = [jnp.exp2((s - peak) * SCALE2) for s in scores]
    total = functools.reduce(jnp.add, [jnp.sum(w, axis=0, keepdims=True) for w in weights])
    mixed = functools.reduce(
        jnp.add, [tt_dot(vals, w.astype(BF16)) for w, (_, vals) in zip(weights, pairs)]
    )
    return mixed / total, peak * SCALE2 + jnp.log2(total)


def padded(rows):
    return -(-rows // 128) * 128


def pad_rows(value):
    extra = padded(value.shape[0]) - value.shape[0]
    if extra == 0:
        return value
    return jnp.concatenate([value, jnp.zeros((extra, value.shape[1]), value.dtype)], axis=0)


def stat_block(stat):
    high = stat.astype(BF16).astype(F32)
    mid = (stat - high).astype(BF16).astype(F32)
    low = (stat - high - mid).astype(BF16).astype(F32)
    lanes = stat.shape[1] // 128
    parts = [p[:, j * 128 : (j + 1) * 128] for p in (high, mid, low) for j in range(lanes)]
    parts.append(jnp.zeros((STAT_ROWS - len(parts), 128), F32))
    return jnp.concatenate(parts, axis=0).astype(BF16)


def stat_of(block, lanes):
    wide = block.astype(F32)
    total = wide[0:lanes] + wide[lanes : 2 * lanes] + wide[2 * lanes : 3 * lanes]
    return jnp.concatenate([total[j : j + 1] for j in range(lanes)], axis=1)


def put_payload(ref, mixed, stat, rows):
    ref[0, :rows] = mixed[:rows].astype(BF16)
    ref[0, rows : rows + STAT_ROWS] = stat_block(stat)


def local_kernel(q_ref, k_ref, v_ref, out_ref, stat_ref):
    rows = q_ref.shape[1]
    mixed, stat = partial_of(pad_rows(q_ref[0]), [(k_ref[0], v_ref[0])], masked=True)
    out_ref[0] = mixed.T[:rows]
    stat_ref[0] = jnp.broadcast_to(stat, stat_ref.shape[1:])


def cross_kernel(
    idx_ref, q_ref, k_ref, v_ref, first_ref, next_ref, last_ref, own_ref, up_ref, far_ref
):
    rows = q_ref.shape[1]
    index = idx_ref[0]

    @pl.when(index == 1)
    def _():
        early = (first_ref[0], first_ref[1])
        here = (k_ref[0], v_ref[0])
        both = jnp.concatenate([next_ref[...], last_ref[...]], axis=0)
        mixed, stat = partial_of(both, [early, here])
        mixed = mixed.T
        pad = jnp.zeros((1, padded(rows) - rows), F32)
        put_payload(up_ref, mixed[:rows], jnp.concatenate([stat[:, :rows], pad], axis=1), rows)
        put_payload(far_ref, mixed[rows:], jnp.concatenate([stat[:, rows:], pad], axis=1), rows)
        mixed, stat = partial_of(pad_rows(q_ref[0]), [early])
        put_payload(own_ref, mixed.T, stat, rows)

    @pl.when(index == 2)
    def _():
        mixed, stat = partial_of(pad_rows(next_ref[...]), [(k_ref[0], v_ref[0])])
        put_payload(up_ref, mixed.T, stat, rows)


def merge_kernel(idx_ref, loc_ref, stat_ref, own_ref, up_ref, far_ref, *rest):
    out_ref = rest[-1]
    rows = loc_ref.shape[1]
    lanes = padded(rows) // 128
    index = idx_ref[0]

    def merged(parts):
        stats = [stat_ref[0, 0:1]] + [stat_of(p[0, rows : rows + STAT_ROWS], lanes) for p in parts]
        values = [loc_ref[0]] + [p[0, :rows].astype(F32) for p in parts]
        top = functools.reduce(jnp.maximum, stats)
        weights = [jnp.exp2(s - top) for s in stats]
        total = functools.reduce(jnp.add, weights)
        result = 0.0
        for weight, value in zip(weights, values):
            column = jnp.broadcast_to(weight / total, (128, padded(rows))).T[:rows]
            result = result + column * value
        out_ref[...] = result.astype(BF16)

    @pl.when(index == 0)
    def _():
        out_ref[...] = loc_ref[0].astype(BF16)

    @pl.when(index == 1)
    def _():
        merged([own_ref])

    @pl.when(index == 2)
    def _():
        merged([up_ref])

    @pl.when(index == 3)
    def _():
        merged([up_ref, far_ref])


def params():
    return pltpu.CompilerParams(vmem_limit_bytes=VMEM_LIMIT)


def cost(flops, size):
    return pl.CostEstimate(flops=int(flops), bytes_accessed=int(size), transcendentals=0)


SMEM = pl.BlockSpec(memory_space=pltpu.SMEM)


def shape(dims, kind):
    return jax.ShapeDtypeStruct(dims, kind)


def full(array):
    return pl.BlockSpec(array.shape, lambda j: (0,) * array.ndim)


def se_mixer(qkv, tail, short, filt):
    rows, width = qkv.shape[1:]
    cols = 256
    return pl.pallas_call(
        se_kernel,
        grid=(width // cols,),
        in_specs=[
            pl.BlockSpec((3, rows, cols), lambda j: (0, 0, j)),
            pl.BlockSpec((tail.shape[0], cols), lambda j: (0, j)),
            pl.BlockSpec((3, 3, cols), lambda j: (0, 0, j)),
            pl.BlockSpec((filt.shape[0], cols), lambda j: (0, j)),
        ],
        out_specs=pl.BlockSpec((rows, cols), lambda j: (0, j)),
        out_shape=shape((rows, width), BF16),
        scratch_shapes=[
            pltpu.VMEM((8 + rows, cols), F32),
            pltpu.VMEM((16 + rows, cols), F32),
            pltpu.VMEM((16 + rows, cols), F32),
            pltpu.VMEM((8 + rows, cols), F32),
        ],
        compiler_params=params(),
        cost_estimate=cost(rows * width * 40, rows * width * 8),
        name="se_mixer",
    )(qkv, tail, short, filt)


def mr_tail(qkv, short):
    rows, width = qkv.shape[1:]
    cols = 512
    half = rows // 2
    return pl.pallas_call(
        mr_tail_kernel,
        grid=(width // cols,),
        in_specs=[
            pl.BlockSpec((1, half, cols), lambda j: (1, 1, j)),
            pl.BlockSpec((1, half, cols), lambda j: (2, 1, j)),
            pl.BlockSpec((3, 3, cols), lambda j: (0, 0, j)),
        ],
        out_specs=pl.BlockSpec((BLOCK, cols), lambda j: (0, j)),
        out_shape=shape((BLOCK, width), BF16),
        scratch_shapes=[pltpu.VMEM((half, cols), F32), pltpu.VMEM((half, cols), F32)],
        compiler_params=params(),
        cost_estimate=cost(BLOCK * width * 12, rows * width * 3),
        name="mr_tail",
    )(qkv, qkv, short)


def mr_main(qkv, tail, short, filt, decay, fwd, inv):
    rows, width = qkv.shape[1:]
    cols = 256
    col = lambda j: (0, j)
    return pl.pallas_call(
        mr_main_kernel,
        grid=(width // cols,),
        in_specs=[
            pl.BlockSpec((3, rows, cols), lambda j: (0, 0, j)),
            pl.BlockSpec((tail.shape[0], cols), col),
            pl.BlockSpec((3, 3, cols), lambda j: (0, 0, j)),
            pl.BlockSpec((filt.shape[0], cols), col),
            pl.BlockSpec((1, cols), col),
            full(fwd),
            full(inv),
        ],
        out_specs=[
            pl.BlockSpec((rows, cols), col),
            pl.BlockSpec((WINDOW, cols), col),
            pl.BlockSpec((BLOCK, cols), col),
        ],
        out_shape=[
            shape((rows, width), BF16),
            shape((WINDOW, width), F32),
            shape((BLOCK, width), BF16),
        ],
        scratch_shapes=[pltpu.VMEM((8 + rows, cols), F32)] * 3 + [pltpu.VMEM((rows, cols), BF16)],
        compiler_params=params(),
        cost_estimate=cost(WINDOW * WINDOW * width * 16, rows * width * 14),
        name="mr_main",
    )(qkv, tail, short, filt, decay[None, :], fwd, inv)


def mr_head(utail, lead, spec, qkv, tail, short, fwd, inv, part):
    rows, width = qkv.shape[1:]
    cols = 256
    col = lambda j: (0, j)
    return pl.pallas_call(
        mr_head_kernel,
        grid=(width // cols,),
        in_specs=[
            pl.BlockSpec((BLOCK, cols), col),
            pl.BlockSpec((BLOCK, cols), col),
            pl.BlockSpec((WINDOW, cols), col),
            pl.BlockSpec((1, BLOCK, cols), lambda j: (0, 0, j)),
            pl.BlockSpec((tail.shape[0], cols), col),
            pl.BlockSpec((3, 3, cols), lambda j: (0, 0, j)),
            full(fwd),
            full(inv),
            pl.BlockSpec(memory_space=pl.ANY),
        ],
        out_specs=pl.BlockSpec((BLOCK, cols), col),
        out_shape=shape((rows, width), BF16),
        scratch_shapes=[pltpu.VMEM((8 + BLOCK, cols), F32)],
        input_output_aliases={8: 0},
        compiler_params=params(),
        cost_estimate=cost(WINDOW * WINDOW * width * 6, rows * width * 4),
        name="mr_head",
    )(utail, lead, spec, qkv, tail, short, fwd, inv, part)


def head_spec(which, rows, offset):
    return pl.BlockSpec((1, rows, HD), lambda h: (which, 0, h + offset))


def local_attention(qkv):
    rows, width = qkv.shape[1:]
    heads = width // HD
    return pl.pallas_call(
        local_kernel,
        grid=(heads,),
        in_specs=[head_spec(j, rows, 0) for j in range(3)],
        out_specs=[
            pl.BlockSpec((1, rows, HD), lambda h: (h, 0, 0)),
            pl.BlockSpec((1, 8, padded(rows)), lambda h: (h, 0, 0)),
        ],
        out_shape=[shape((heads, rows, HD), F32), shape((heads, 8, padded(rows)), F32)],
        compiler_params=params(),
        cost_estimate=cost(heads * rows * rows * 512, rows * width * 10),
        name="local_attention",
    )(qkv, qkv, qkv)


def cross_attention(index, qkv, first, following, last, offset, count):
    rows = qkv.shape[1]
    block = pl.BlockSpec((1, rows + STAT_ROWS, HD), lambda h: (h, 0, 0))
    return pl.pallas_call(
        cross_kernel,
        grid=(count,),
        in_specs=[SMEM]
        + [head_spec(j, rows, offset) for j in range(3)]
        + [
            pl.BlockSpec((2, rows, HD), lambda h: (0, 0, h)),
            pl.BlockSpec((rows, HD), lambda h: (0, h)),
            pl.BlockSpec((rows, HD), lambda h: (0, h)),
        ],
        out_specs=[block] * 3,
        out_shape=[shape((count, rows + STAT_ROWS, HD), BF16)] * 3,
        compiler_params=params(),
        cost_estimate=cost(count * rows * rows * 2560, count * rows * HD * 20),
        name="cross_attention",
    )(index, qkv, qkv, qkv, first, following, last)


def merge_attention(index, local, stats, own, up, far, offset, count, done, width):
    rows = local.shape[1]
    block = pl.BlockSpec((1, rows + STAT_ROWS, HD), lambda h: (h, 0, 0))
    operands = [index, local, stats, own, up, far]
    specs = [
        SMEM,
        pl.BlockSpec((1, rows, HD), lambda h: (h + offset, 0, 0)),
        pl.BlockSpec((1, 8, padded(rows)), lambda h: (h + offset, 0, 0)),
        block,
        block,
        block,
    ]
    aliases = {}
    if done is not None:
        aliases = {len(operands): 0}
        operands.append(done)
        specs.append(pl.BlockSpec(memory_space=pl.ANY))
    return pl.pallas_call(
        merge_kernel,
        grid=(count,),
        in_specs=specs,
        out_specs=pl.BlockSpec((rows, HD), lambda h: (0, h + offset)),
        out_shape=shape((rows, width), BF16),
        input_output_aliases=aliases,
        compiler_params=params(),
        cost_estimate=cost(count * rows * HD * 40, count * rows * HD * 12),
        name="merge_attention",
    )(*operands)


def gathered_attention(attn_qkv):
    rows, width = attn_qkv.shape[1:]
    heads = width // HD
    pairs = lax.all_gather(attn_qkv[1:], "seq", axis=1, tiled=True)
    count = pairs.shape[1]
    query = attn_qkv[0].reshape(rows, heads, HD)
    positions = lax.axis_index("seq") * rows + jnp.arange(rows)
    visible = (jnp.arange(count)[None, :] <= positions[:, None])[None]
    scores = jnp.einsum(
        "qhd,khd->hqk", query, pairs[0].reshape(count, heads, HD), preferred_element_type=F32
    ) / jnp.sqrt(F32(HD))
    scores = jnp.where(visible, scores, F32(-1e30))
    peak = jnp.max(scores, axis=2, keepdims=True)
    weights = jnp.where(visible, jnp.exp(scores - peak), F32(0.0))
    total = jnp.sum(weights, axis=2)
    mixed = jnp.einsum(
        "hqk,khd->qhd",
        weights.astype(BF16),
        pairs[1].reshape(count, heads, HD),
        preferred_element_type=F32,
    )
    return (mixed / total.T[:, :, None]).astype(BF16).reshape(rows, width)


def on_device(se_qkv, se_short, se_filter, mr_qkv, mr_short, mr_filter, mr_decay, attn_qkv):
    rows, width = se_qkv.shape[1:]
    spans = lax.axis_size("seq")
    heads = width // HD
    fwd, inv = (jnp.asarray(m) for m in transforms())
    rising = [(s, s + 1) for s in range(spans - 1)]
    raw = jnp.concatenate(
        [
            se_qkv[1, rows - 8 :],
            se_qkv[2, rows - 8 :],
            se_qkv[0, rows - 2 :],
            mr_qkv[0, rows - 2 :],
            mr_qkv[1, rows - 2 :],
            mr_qkv[2, rows - 2 :],
            jnp.zeros((8, width), BF16),
        ],
        axis=0,
    )
    raw = lax.ppermute(raw, "seq", rising)
    product = mr_tail(mr_qkv, mr_short)
    se_out = se_mixer(se_qkv, raw, se_short, se_filter)
    mr_part, spec, lead = mr_main(mr_qkv, raw, mr_short, mr_filter, mr_decay, fwd, inv)

    if spans == 4:
        index = lax.axis_index("seq").astype(jnp.int32).reshape(1)
        starts = [sum(CHUNKS[:c]) for c in range(len(CHUNKS))]
        local, stats = local_attention(attn_qkv)
        upper = lax.ppermute(product, "seq", [(1, 2), (2, 3)])
        lower = lax.ppermute(product, "seq", [(0, 1)])
        utail = jnp.where(index[0] == 1, lower, upper)
        pieces = []
        for start, count in zip(starts, CHUNKS):
            cols = slice(start * HD, (start + count) * HD)
            first = lax.ppermute(attn_qkv[1:, :, cols], "seq", [(0, 1)])
            asked = attn_qkv[0, :, cols]
            following = lax.ppermute(asked, "seq", [(2, 1), (3, 2)])
            last = lax.ppermute(asked, "seq", [(3, 1)])
            own, up, far = cross_attention(index, attn_qkv, first, following, last, start, count)
            up = lax.ppermute(up, "seq", [(1, 2), (2, 3)])
            far = lax.ppermute(far, "seq", [(1, 3)])
            pieces.append((own, up, far))
        attn_out = None
        for start, count, piece in zip(starts, CHUNKS, pieces):
            attn_out = merge_attention(
                index, local, stats, *piece, start, count, attn_out, width
            )
    else:
        utail = lax.ppermute(product, "seq", rising)
        attn_out = gathered_attention(attn_qkv)
    mr_out = mr_head(utail, lead, spec, mr_qkv, raw, mr_short, fwd, inv, mr_part)
    return (se_out, mr_out, attn_out)


def solution(mesh):
    in_specs = (
        P(None, ("groups", "seq"), "chan"),
        P(None, None, "chan"),
        P(None, "chan"),
        P(None, ("groups", "seq"), "chan"),
        P(None, None, "chan"),
        P(None, "chan"),
        P("chan"),
        P(None, ("groups", "seq"), "chan"),
    )
    out_specs = (
        P(("groups", "seq"), "chan"),
        P(("groups", "seq"), "chan"),
        P(("groups", "seq"), "chan"),
    )
    return jax.shard_map(
        on_device, mesh=mesh, in_specs=in_specs, out_specs=out_specs, check_vma=False
    )
```

time: 311 us -> 183 us (0.59); the launches traced: 305 us -> 181 us
  local copies, waits for them, and re-layouts: 135 us -> 17.2 us
  matrix products: 62 us -> 0 us
  starting transfers between devices: 5.36 us -> 65.3 us
  Pallas kernels: 0 us -> 59.9 us
  other arithmetic: 27.9 us -> 1.11 us
  waiting for transfers between devices: 59.8 us -> 36.1 us
  between operations: 15.4 us -> 1.19 us
    ppermute x4 -> x23, starting transfers between devices: 5.32 us -> 65.3 us  [the longest x4 30 us: on_device(): last = lax.ppermute(asked, 'seq', [(3, 1)])]
    pallas_call x0 -> x13, Pallas kernels: none -> 59.9 us  [the longest x1 13 us: local_attention(): pl.pallas_call(local_kernel, grid=(heads,), in_specs=[head_spec(j, rows,...]
    conv_general_dilated x20 -> x0, local copies, waits for them, and re-layouts: 39.4 us -> none  [causal_valid(): lax.conv_general_dilated(extended[None], flipped, (1,), 'VALID', dimensio...]
    conv_general_dilated x8 -> x0, matrix products: 36.7 us -> none  [causal_valid(): lax.conv_general_dilated(extended[None], flipped, (1,), 'VALID', dimensio...]
    another operation x1 -> x0, local copies, waits for them, and re-layouts: 26 us -> none
    dot_general x2 -> x0, matrix products: 25.3 us -> none  [the longest x1 13.8 us: compute(): jnp.einsum('hqk,khd->qhd', weights.astype(jnp.bfloat16), valrows, preferr...]
    ppermute x4 -> x23, waiting for transfers between devices: 51.7 us -> 36.1 us  [the longest x4 27.9 us: on_device(): far = lax.ppermute(far, 'seq', [(1, 3)])]
    reduce_sum x1 -> x0, other arithmetic: 13.9 us -> none  [compute(): total = jnp.sum(weights, axis=2)]
  transfers between devices with their start and end apart: 5 -> 23, of which waited for: 2 -> 3; matrix products, arithmetic and copies ran while one was open for 45% -> 7% of each run, Pallas kernels for 0% -> 32%
where the time goes in v1:
time: 183 us; the launch traced here: 181 us
  starting transfers between devices  65.3 us (36%)
  Pallas kernels  59.9 us (33%)
  waiting for transfers between devices  36.1 us (20%)
  local copies, waits for them, and re-layouts  17.2 us (9%)
    ppermute x4, starting transfers between devices, on_device(): last = lax.ppermute(asked, 'seq', [(3, 1)])  30 us
    ppermute x4, waiting for transfers between devices, on_device(): far = lax.ppermute(far, 'seq', [(1, 3)])  27.9 us
    ppermute x4, starting transfers between devices, on_device(): following = lax.ppermute(asked, 'seq', [(2, 1), (3, 2)])  17.9 us
    pallas_call x1, Pallas kernels, local_attention(): pl.pallas_call(local_kernel, grid=(heads,), in_specs=[head_spec(j, rows,...  13 us
    pallas_call x4, Pallas kernels, cross_attention(): pl.pallas_call(cross_kernel, grid=(count,), in_specs=[SMEM] + [head_spec(...  11.9 us
    pallas_call x4, Pallas kernels, merge_attention(): pl.pallas_call(merge_kernel, grid=(count,), in_specs=specs, out_specs=pl....  10.2 us
    pallas_call x1, Pallas kernels, mr_main(): pl.pallas_call(mr_main_kernel, grid=(width // cols,), in_specs=[pl.BlockS...  9.69 us
    pallas_call x1, Pallas kernels, mr_head(): pl.pallas_call(mr_head_kernel, grid=(width // cols,), in_specs=[pl.BlockS...  6.99 us
  transfers between devices with their start and end apart: 23, of which 3 were waited for; matrix products, arithmetic and copies ran while one was open for 7% of the time, Pallas kernels for 32%

profile of v1, /device:TPU:26, one launch (start us, length us, event | category | flops | bytes accessed | tf_op | source)
XLA Modules:
  0.0 180.7 jit_solution(2557575387775852738)
XLA Ops:
  1.6 2.5 %collective-permute-start.4 = (bf16[320,256]{1,0:T(8,128)(2,1)S(1)}, bf16[320,256]{1,0:T(8,128)(2,1)S(1)}, u32[]{:S(2)}, u32[]{:S(2)}) collective-permute-start(bf16[320,256]{1,0:T(8,128)(2,1)S(1)} %slice_bitcast_fusion.3), channel_id=1, source_target_pairs={{8,4},{12,8},{9,5},{13,9},{10,6},{14,10},{11,7},{15,11},{24,20},{2... | collective-permute-start | bytes 491528 | tf_op jit(solution)/shard_map/ppermute | solution.py:561
  4.1 1.3 collective-permute-start.5
  5.4 2.7 %fusion = (bf16[2,320,640]{2,1,0:T(8,128)(2,1)}, bf16[2,320,640]{2,1,0:T(8,128)(2,1)}) fusion(bf16[3,320,2048]{2,1,0:T(8,128)(2,1)} %v_ref.11), kind=kLoop, calls=%fused_computation.11 | loop fusion | bytes 3276800 | tf_op jit(solution)/shard_map/slice | solution.py:559
  8.8 1.7 slice_bitcast_fusion.2
  10.5 1.7 collective-permute-start.10
  14.7 1.3 collective-permute-start
  17.2 4.4 %collective-permute-done.tail_ref = bf16[32,2048]{1,0:T(8,128)(2,1)S(1)} collective-permute-done((bf16[32,2048]{1,0:T(8,128)(2,1)S(1)}, bf16[32,2048]{1,0:T(8,128)(2,1)S(1)}, u32[]{:S(2)}, u32[]{:S(2)}) %collective-permute-start) | collective-permute-done | bytes 131104 | tf_op jit(solution)/shard_map/ppermute | solution.py:544
  21.6 1.5 collective-permute-start.19
  23.1 12.3 %collective-permute-start.20 = (bf16[320,640]{1,0:T(8,128)(2,1)S(1)}, bf16[320,640]{1,0:T(8,128)(2,1)S(1)}, u32[]{:S(2)}, u32[]{:S(2)}) collective-permute-start(bf16[320,640]{1,0:T(8,128)(2,1)S(1)} %get-tuple-element.37), channel_id=1, source_target_pairs={{12,4},{13,5},{14,6},{15,7},{28,20},{29,21},{30,22},{31,23}} | collective-permute-start | bytes 1228808 | tf_op jit(solution)/shard_map/ppermute | solution.py:562
  36.2 1.9 %collective-permute-start.14 = (bf16[320,640]{1,0:T(8,128)(2,1)S(1)}, bf16[320,640]{1,0:T(8,128)(2,1)S(1)}, u32[]{:S(2)}, u32[]{:S(2)}) collective-permute-start(bf16[320,640]{1,0:T(8,128)(2,1)S(1)} %get-tuple-element.38), channel_id=1, source_target_pairs={{8,4},{12,8},{9,5},{13,9},{10,6},{14,10},{11,7},{15,11},{24,20},{2... | collective-permute-start | bytes 1228808 | tf_op jit(solution)/shard_map/ppermute | solution.py:561
  38.1 2.0 %slice.50 = bf16[2,320,512]{2,1,0:T(8,128)(2,1)} slice(bf16[3,320,2048]{2,1,0:T(8,128)(2,1)} %v_ref.11), slice={[1:3], [0:320], [1280:1792]} | slice | bytes 1310720 | tf_op jit(solution)/shard_map/slice | solution.py:559
  41.5 3.8 %collective-permute-done.20.last_ref = bf16[320,640]{1,0:T(8,128)(2,1)S(1)} collective-permute-done((bf16[320,640]{1,0:T(8,128)(2,1)S(1)}, bf16[320,640]{1,0:T(8,128)(2,1)S(1)}, u32[]{:S(2)}, u32[]{:S(2)}) %collective-permute-start.20) | collective-permute-done | bytes 409632 | tf_op jit(solution)/shard_map/ppermute | solution.py:562
  46.1 14.7 %collective-permute-start.15 = (bf16[320,640]{1,0:T(8,128)(2,1)S(1)}, bf16[320,640]{1,0:T(8,128)(2,1)}, u32[]{:S(2)}, u32[]{:S(2)}) collective-permute-start(bf16[320,640]{1,0:T(8,128)(2,1)S(1)} %get-tuple-element.38), channel_id=1, source_target_pairs={{12,4},{13,5},{14,6},{15,7},{28,20},{29,21},{30,22},{31,23}} | collective-permute-start | bytes 1228808 | tf_op jit(solution)/shard_map/ppermute | solution.py:562
  60.8 12.0 %collective-permute-start.9 = (bf16[320,512]{1,0:T(8,128)(2,1)}, bf16[320,512]{1,0:T(8,128)(2,1)}, u32[]{:S(2)}, u32[]{:S(2)}) collective-permute-start(bf16[320,512]{1,0:T(8,128)(2,1)} %slice_bitcast_fusion.2), channel_id=1, source_target_pairs={{8,4},{12,8},{9,5},{13,9},{10,6},{14,10},{11,7},{15,11},{24,20},{2... | collective-permute-start | bytes 983048 | tf_op jit(solution)/shard_map/ppermute | solution.py:561
  72.8 1.7 slice.48
  74.5 1.4 collective-permute-start.3
  75.9 2.1 %copy-done.1 = bf16[3,320,2048]{2,1,0:T(8,128)(2,1)S(1)} copy-done((bf16[3,320,2048]{2,1,0:T(8,128)(2,1)S(1)}, bf16[3,320,2048]{2,1,0:T(8,128)(2,1)}, u32[]{:S(2)}) %copy-start.1) | copy-done | bytes 3932184
  79.3 3.9 %cross_attention.7 = (bf16[5,336,128]{2,1,0:T(8,128)(2,1)S(1)}, bf16[5,336,128]{2,1,0:T(8,128)(2,1)}, bf16[5,336,128]{2,1,0:T(8,128)(2,1)}) custom-call(s32[1]{0:T(128)} %bitcast.7.idx_ref, bf16[3,320,2048]{2,1,0:T(8,128)(2,1)} %v_ref.11, bf16[3,320,2048]{2,1,0:T(8,128)(2,1)} %v_ref.11, bf16[3,320,2048]{2,1,0:T(8,128)(2,1)} %v_ref.11, ...), custom_call_target="tpu_custom_call" | custom-call | flops 1310720000 | bytes 4096000 | tf_op jit(solution)/shard_map/cross_attention/pallas_call | solution.py:454
  85.2 3.8 %cross_attention.6 = (bf16[5,336,128]{2,1,0:T(8,128)(2,1)S(1)}, bf16[5,336,128]{2,1,0:T(8,128)(2,1)}, bf16[5,336,128]{2,1,0:T(8,128)(2,1)S(1)}) custom-call(s32[1]{0:T(128)} %bitcast.7.idx_ref, bf16[3,320,2048]{2,1,0:T(8,128)(2,1)} %v_ref.11, bf16[3,320,2048]{2,1,0:T(8,128)(2,1)} %v_ref.11, bf16[3,320,2048]{2,1,0:T(8,128)(2,1)} %v_ref.11, ...), custom_call_target="tpu_custom_call" | custom-call | flops 1310720000 | bytes 4096000 | tf_op jit(solution)/shard_map/cross_attention/pallas_call | solution.py:454
  91.7 1.6 collective-permute-start.16
  93.3 13.0 %local_attention.1 = (f32[16,320,128]{2,1,0:T(8,128)S(1)}, f32[16,8,384]{2,1,0:T(8,128)S(1)}) custom-call(bf16[3,320,2048]{2,1,0:T(8,128)(2,1)} %v_ref.11, bf16[3,320,2048]{2,1,0:T(8,128)(2,1)} %v_ref.11, bf16[3,320,2048]{2,1,0:T(8,128)(2,1)} %v_ref.11), custom_call_target="tpu_custom_call" | custom-call | flops 838860800 | bytes 6553600 | tf_op jit(solution)/shard_map/local_attention/pallas_call | solution.py:436
  106.4 6.9 %se_mixer.1 = bf16[320,2048]{1,0:T(8,128)(2,1)} custom-call(bf16[3,320,2048]{2,1,0:T(8,128)(2,1)S(1)} %copy-done.2, bf16[32,2048]{1,0:T(8,128)(2,1)S(1)} %collective-permute-done.tail_ref, f32[3,3,2048]{2,1,0:T(4,128)S(1)} %copy-done.23, f32[7,2048]{1,0:T(8,128)S(1)} %copy-done.24), custom_call_target="tpu_custom_call" | custom-call | flops 26214400 | bytes 5242880 | tf_op jit(solution)/shard_map/se_mixer/pallas_call | solution.py:324
  113.4 9.7 %mr_main.1 = (bf16[320,2048]{1,0:T(8,128)(2,1)}, f32[256,2048]{1,0:T(8,128)S(1)}, bf16[128,2048]{1,0:T(8,128)(2,1)S(1)}) custom-call(bf16[3,320,2048]{2,1,0:T(8,128)(2,1)} %query_ref.1, bf16[32,2048]{1,0:T(8,128)(2,1)S(1)} %collective-permute-done.tail_ref, f32[3,3,2048]{2,1,0:T(4,128)S(1)} %copy-done.13, f32[128,2048]{1,0:T(8,128)S(1)} %copy-done.25, ...), custom_call_target="tpu_custom_call" | custom-call | flops 2147483648 | bytes 9175040 | tf_op jit(solution)/shard_map/mr_main/pallas_call | solution.py:372
  123.1 1.8 cross_attention.4
  124.9 2.3 %cross_attention.5 = (bf16[4,336,128]{2,1,0:T(8,128)(2,1)S(1)}, bf16[4,336,128]{2,1,0:T(8,128)(2,1)S(1)}, bf16[4,336,128]{2,1,0:T(8,128)(2,1)S(1)}) custom-call(s32[1]{0:T(128)} %bitcast.7.idx_ref, bf16[3,320,2048]{2,1,0:T(8,128)(2,1)} %v_ref.11, bf16[3,320,2048]{2,1,0:T(8,128)(2,1)} %v_ref.11, bf16[3,320,2048]{2,1,0:T(8,128)(2,1)} %v_ref.11, ...), custom_call_target="tpu_custom_call" | custom-call | flops 1048576000 | bytes 3276800 | tf_op jit(solution)/shard_map/cross_attention/pallas_call | solution.py:454
  129.8 1.3 collective-permute-start.11
  133.2 1.3 collective-permute-start.17
  135.6 7.0 %mr_head.1 = bf16[320,2048]{1,0:T(8,128)(2,1)} custom-call(bf16[128,2048]{1,0:T(8,128)(2,1)S(1)} %broadcast_select_fusion.utail_ref, bf16[128,2048]{1,0:T(8,128)(2,1)S(1)} %get-tuple-element.20.lead_ref, f32[256,2048]{1,0:T(8,128)S(1)} %get-tuple-element.21.spec_ref, bf16[3,320,2048]{2,1,0:T(8,128)(2,1)} %query_ref.1, ...), custom_call_target="tpu_custom_call", output_to_operand_aliasing={{}: (8, {})} | custom-call | flops 805306368 | bytes 2621440 | tf_op jit(solution)/shard_map/mr_head/pallas_call | solution.py:405
  142.6 2.7 %merge_attention.4.rest_0_ = bf16[320,2048]{1,0:T(8,128)(2,1)} custom-call(s32[1]{0:T(128)} %bitcast.7.idx_ref, f32[16,320,128]{2,1,0:T(8,128)S(1)} %get-tuple-element.23.loc_ref, f32[16,8,384]{2,1,0:T(8,128)S(1)} %get-tuple-element.24.stat_ref, bf16[5,336,128]{2,1,0:T(8,128)(2,1)S(1)} %get-tuple-element.34.own_ref, ...), custom_call_target="tpu_custom_call" | custom-call | flops 8192000 | bytes 2457600 | tf_op jit(solution)/shard_map/merge_attention/pallas_call | solution.py:489
  145.3 27.9 %collective-permute-done.17.far_ref = bf16[5,336,128]{2,1,0:T(8,128)(2,1)S(1)} collective-permute-done((bf16[5,336,128]{2,1,0:T(8,128)(2,1)S(1)}, bf16[5,336,128]{2,1,0:T(8,128)(2,1)S(1)}, u32[]{:S(2)}, u32[]{:S(2)}) %collective-permute-start.17) | collective-permute-done | bytes 430112 | tf_op jit(solution)/shard_map/ppermute | solution.py:565
  173.2 4.2 %merge_attention.5.rest_0_ = bf16[320,2048]{1,0:T(8,128)(2,1)} custom-call(s32[1]{0:T(128)} %bitcast.7.idx_ref, f32[16,320,128]{2,1,0:T(8,128)S(1)} %get-tuple-element.23.loc_ref, f32[16,8,384]{2,1,0:T(8,128)S(1)} %get-tuple-element.24.stat_ref, bf16[5,336,128]{2,1,0:T(8,128)(2,1)S(1)} %copy-done.4, ...), custom_call_target="tpu_custom_call", output_to_operand_aliasing={{}: (6, {})} | custom-call | flops 8192000 | bytes 2457600 | tf_op jit(solution)/shard_map/merge_attention/pallas_call | solution.py:489
  177.3 2.1 %merge_attention.6.rest_0_ = bf16[320,2048]{1,0:T(8,128)(2,1)} custom-call(s32[1]{0:T(128)} %bitcast.7.idx_ref, f32[16,320,128]{2,1,0:T(8,128)S(1)} %get-tuple-element.23.loc_ref, f32[16,8,384]{2,1,0:T(8,128)S(1)} %get-tuple-element.24.stat_ref, bf16[4,336,128]{2,1,0:T(8,128)(2,1)S(1)} %get-tuple-element.28.own_ref, ...), custom_call_target="tpu_custom_call", output_to_operand_aliasing={{}: (6, {})} | custom-call | flops 6553600 | bytes 1966080 | tf_op jit(solution)/shard_map/merge_attention/pallas_call | solution.py:489
  (97 shorter events, 21.1 us)
Async XLA Ops:
  1.6 74.4 %copy-start.13 = (f32[3,3,2048]{2,1,0:T(4,128)S(1)}, f32[3,3,2048]{2,1,0:T(4,128)}, u32[]{:S(2)}) copy-start(f32[3,3,2048]{2,1,0:T(4,128)} %short_ref.7) | copy-start | bytes 221188
  1.6 21.5 %collective-permute-start.4 = (bf16[320,256]{1,0:T(8,128)(2,1)S(1)}, bf16[320,256]{1,0:T(8,128)(2,1)S(1)}, u32[]{:S(2)}, u32[]{:S(2)}) collective-permute-start(bf16[320,256]{1,0:T(8,128)(2,1)S(1)} %slice_bitcast_fusion.3), channel_id=1, source_target_pairs={{8,4},{12,8},{9,5},{13,9},{10,6},{14,10},{11,7},{15,11},{24,20},{2... | collective-permute-start | bytes 491528 | tf_op jit(solution)/shard_map/ppermute | solution.py:561
  4.1 31.4 %collective-permute-start.5 = (bf16[320,256]{1,0:T(8,128)(2,1)S(1)}, bf16[320,256]{1,0:T(8,128)(2,1)S(1)}, u32[]{:S(2)}, u32[]{:S(2)}) collective-permute-start(bf16[320,256]{1,0:T(8,128)(2,1)S(1)} %slice_bitcast_fusion.3), channel_id=1, source_target_pairs={{12,4},{13,5},{14,6},{15,7},{28,20},{29,21},{30,22},{31,23}} | collective-permute-start | bytes 491528 | tf_op jit(solution)/shard_map/ppermute | solution.py:562
  8.1 66.4 %collective-permute-start.18 = (bf16[2,320,640]{2,1,0:T(8,128)(2,1)}, bf16[2,320,640]{2,1,0:T(8,128)(2,1)S(1)}, u32[]{:S(2)}, u32[]{:S(2)}) collective-permute-start(bf16[2,320,640]{2,1,0:T(8,128)(2,1)} %get-tuple-element.39), channel_id=1, source_target_pairs={{0,4},{1,5},{2,6},{3,7},{16,20},{17,21},{18,22},{19,23}} | collective-permute-start | bytes 2457608 | tf_op jit(solution)/shard_map/ppermute | solution.py:559
  10.5 25.7 %collective-permute-start.10 = (bf16[320,512]{1,0:T(8,128)(2,1)}, bf16[320,512]{1,0:T(8,128)(2,1)S(1)}, u32[]{:S(2)}, u32[]{:S(2)}) collective-permute-start(bf16[320,512]{1,0:T(8,128)(2,1)} %slice_bitcast_fusion.2), channel_id=1, source_target_pairs={{12,4},{13,5},{14,6},{15,7},{28,20},{29,21},{30,22},{31,23}} | collective-permute-start | bytes 983048 | tf_op jit(solution)/shard_map/ppermute | solution.py:562
  14.7 6.9 %collective-permute-start = (bf16[32,2048]{1,0:T(8,128)(2,1)S(1)}, bf16[32,2048]{1,0:T(8,128)(2,1)S(1)}, u32[]{:S(2)}, u32[]{:S(2)}) collective-permute-start(bf16[32,2048]{1,0:T(8,128)(2,1)S(1)} %concatenate.3), channel_id=1, source_target_pairs={{0,4},{4,8},{8,12},{1,5},{5,9},{9,13},{2,6},{6,10},{10,14},{3,7},{... | collective-permute-start | bytes 393224 | tf_op jit(solution)/shard_map/ppermute | solution.py:544
  21.6 18.5 %collective-permute-start.19 = (bf16[320,640]{1,0:T(8,128)(2,1)S(1)}, bf16[320,640]{1,0:T(8,128)(2,1)S(1)}, u32[]{:S(2)}, u32[]{:S(2)}) collective-permute-start(bf16[320,640]{1,0:T(8,128)(2,1)S(1)} %get-tuple-element.37), channel_id=1, source_target_pairs={{8,4},{12,8},{9,5},{13,9},{10,6},{14,10},{11,7},{15,11},{24,20},{2... | collective-permute-start | bytes 1228808 | tf_op jit(solution)/shard_map/ppermute | solution.py:561
  23.1 17.0 %copy-start.17 = (bf16[320,256]{1,0:T(8,128)(2,1)}, bf16[320,256]{1,0:T(8,128)(2,1)S(1)}, u32[]{:S(2)}) copy-start(bf16[320,256]{1,0:T(8,128)(2,1)S(1)} %collective-permute-done.4.next_ref) | copy-start | bytes 491524
  23.1 22.2 %collective-permute-start.20 = (bf16[320,640]{1,0:T(8,128)(2,1)S(1)}, bf16[320,640]{1,0:T(8,128)(2,1)S(1)}, u32[]{:S(2)}, u32[]{:S(2)}) collective-permute-start(bf16[320,640]{1,0:T(8,128)(2,1)S(1)} %get-tuple-element.37), channel_id=1, source_target_pairs={{12,4},{13,5},{14,6},{15,7},{28,20},{29,21},{30,22},{31,23}} | collective-permute-start | bytes 1228808 | tf_op jit(solution)/shard_map/ppermute | solution.py:562
  35.5 40.4 %copy-start.19 = (bf16[320,256]{1,0:T(8,128)(2,1)}, bf16[320,256]{1,0:T(8,128)(2,1)S(1)}, u32[]{:S(2)}) copy-start(bf16[320,256]{1,0:T(8,128)(2,1)S(1)} %collective-permute-done.5.last_ref) | copy-start | bytes 491524
  35.5 48.4 %collective-permute-start.13 = (bf16[2,320,640]{2,1,0:T(8,128)(2,1)}, bf16[2,320,640]{2,1,0:T(8,128)(2,1)S(1)}, u32[]{:S(2)}, u32[]{:S(2)}) collective-permute-start(bf16[2,320,640]{2,1,0:T(8,128)(2,1)} %get-tuple-element.40), channel_id=1, source_target_pairs={{0,4},{1,5},{2,6},{3,7},{16,20},{17,21},{18,22},{19,23}} | collective-permute-start | bytes 2457608 | tf_op jit(solution)/shard_map/ppermute | solution.py:559
  36.2 39.7 %copy-start.14 = (bf16[320,512]{1,0:T(8,128)(2,1)}, bf16[320,512]{1,0:T(8,128)(2,1)S(1)}, u32[]{:S(2)}) copy-start(bf16[320,512]{1,0:T(8,128)(2,1)S(1)} %collective-permute-done.10.last_ref) | copy-start | bytes 983044
  36.2 24.5 %collective-permute-start.14 = (bf16[320,640]{1,0:T(8,128)(2,1)S(1)}, bf16[320,640]{1,0:T(8,128)(2,1)S(1)}, u32[]{:S(2)}, u32[]{:S(2)}) collective-permute-start(bf16[320,640]{1,0:T(8,128)(2,1)S(1)} %get-tuple-element.38), channel_id=1, source_target_pairs={{8,4},{12,8},{9,5},{13,9},{10,6},{14,10},{11,7},{15,11},{24,20},{2... | collective-permute-start | bytes 1228808 | tf_op jit(solution)/shard_map/ppermute | solution.py:561
  40.8 50.8 %collective-permute-start.8 = (bf16[2,320,512]{2,1,0:T(8,128)(2,1)}, bf16[2,320,512]{2,1,0:T(8,128)(2,1)S(1)}, u32[]{:S(2)}, u32[]{:S(2)}) collective-permute-start(bf16[2,320,512]{2,1,0:T(8,128)(2,1)} %slice.50), channel_id=1, source_target_pairs={{0,4},{1,5},{2,6},{3,7},{16,20},{17,21},{18,22},{19,23}} | collective-permute-start | bytes 1966088 | tf_op jit(solution)/shard_map/ppermute | solution.py:559
  46.1 37.1 %collective-permute-start.15 = (bf16[320,640]{1,0:T(8,128)(2,1)S(1)}, bf16[320,640]{1,0:T(8,128)(2,1)}, u32[]{:S(2)}, u32[]{:S(2)}) collective-permute-start(bf16[320,640]{1,0:T(8,128)(2,1)S(1)} %get-tuple-element.38), channel_id=1, source_target_pairs={{12,4},{13,5},{14,6},{15,7},{28,20},{29,21},{30,22},{31,23}} | collective-permute-start | bytes 1228808 | tf_op jit(solution)/shard_map/ppermute | solution.py:562
  60.8 28.3 %collective-permute-start.9 = (bf16[320,512]{1,0:T(8,128)(2,1)}, bf16[320,512]{1,0:T(8,128)(2,1)}, u32[]{:S(2)}, u32[]{:S(2)}) collective-permute-start(bf16[320,512]{1,0:T(8,128)(2,1)} %slice_bitcast_fusion.2), channel_id=1, source_target_pairs={{8,4},{12,8},{9,5},{13,9},{10,6},{14,10},{11,7},{15,11},{24,20},{2... | collective-permute-start | bytes 983048 | tf_op jit(solution)/shard_map/ppermute | solution.py:561
  74.5 15.8 %collective-permute-start.3 = (bf16[2,320,256]{2,1,0:T(8,128)(2,1)}, bf16[2,320,256]{2,1,0:T(8,128)(2,1)}, u32[]{:S(2)}, u32[]{:S(2)}) collective-permute-start(bf16[2,320,256]{2,1,0:T(8,128)(2,1)} %slice.48), channel_id=1, source_target_pairs={{0,4},{1,5},{2,6},{3,7},{16,20},{17,21},{18,22},{19,23}} | collective-permute-start | bytes 983048 | tf_op jit(solution)/shard_map/ppermute | solution.py:559
  83.2 44.0 %collective-permute-start.1 = (bf16[128,2048]{1,0:T(8,128)(2,1)S(1)}, bf16[128,2048]{1,0:T(8,128)(2,1)S(1)}, u32[]{:S(2)}, u32[]{:S(2)}) collective-permute-start(bf16[128,2048]{1,0:T(8,128)(2,1)S(1)} %mr_tail.1), channel_id=1, source_target_pairs={{0,4},{1,5},{2,6},{3,7},{16,20},{17,21},{18,22},{19,23}} | collective-permute-start | bytes 1572872 | tf_op jit(solution)/shard_map/ppermute | solution.py:554
  83.9 44.6 %collective-permute-start.2 = (bf16[128,2048]{1,0:T(8,128)(2,1)S(1)}, bf16[128,2048]{1,0:T(8,128)(2,1)}, u32[]{:S(2)}, u32[]{:S(2)}) collective-permute-start(bf16[128,2048]{1,0:T(8,128)(2,1)S(1)} %mr_tail.1), channel_id=1, source_target_pairs={{4,8},{8,12},{5,9},{9,13},{6,10},{10,14},{7,11},{11,15},{20,24},{2... | collective-permute-start | bytes 1572872 | tf_op jit(solution)/shard_map/ppermute | solution.py:553
  89.1 17.2 %copy-start.3 = (bf16[5,336,128]{2,1,0:T(8,128)(2,1)}, bf16[5,336,128]{2,1,0:T(8,128)(2,1)S(1)}, u32[]{:S(2)}) copy-start(bf16[5,336,128]{2,1,0:T(8,128)(2,1)S(1)} %get-tuple-element.31.own_ref) | copy-start | bytes 1290244
  89.1 17.2 %copy-start.26 = (bf16[5,336,128]{2,1,0:T(8,128)(2,1)}, bf16[5,336,128]{2,1,0:T(8,128)(2,1)S(1)}, u32[]{:S(2)}) copy-start(bf16[5,336,128]{2,1,0:T(8,128)(2,1)S(1)} %get-tuple-element.33) | copy-start | bytes 1290244
  89.1 40.8 %collective-permute-start.21 = (bf16[5,336,128]{2,1,0:T(8,128)(2,1)}, bf16[5,336,128]{2,1,0:T(8,128)(2,1)S(1)}, u32[]{:S(2)}, u32[]{:S(2)}) collective-permute-start(bf16[5,336,128]{2,1,0:T(8,128)(2,1)} %get-tuple-element.35), channel_id=1, source_target_pairs={{4,8},{8,12},{5,9},{9,13},{6,10},{10,14},{7,11},{11,15},{20,24},{2... | collective-permute-start | bytes 1290248 | tf_op jit(solution)/shard_map/ppermute | solution.py:564
  90.4 40.8 %collective-permute-start.22 = (bf16[5,336,128]{2,1,0:T(8,128)(2,1)}, bf16[5,336,128]{2,1,0:T(8,128)(2,1)S(1)}, u32[]{:S(2)}, u32[]{:S(2)}) collective-permute-start(bf16[5,336,128]{2,1,0:T(8,128)(2,1)} %get-tuple-element.36), channel_id=1, source_target_pairs={{4,12},{5,13},{6,14},{7,15},{20,28},{21,29},{22,30},{23,31}} | collective-permute-start | bytes 1290248 | tf_op jit(solution)/shard_map/ppermute | solution.py:565
  91.7 14.6 %copy-start.2 = (bf16[3,320,2048]{2,1,0:T(8,128)(2,1)S(1)}, bf16[3,320,2048]{2,1,0:T(8,128)(2,1)}, u32[]{:S(2)}) copy-start(bf16[3,320,2048]{2,1,0:T(8,128)(2,1)} %qkv_ref.2) | copy-start | bytes 11796484
  91.7 14.6 %copy-start.23 = (f32[3,3,2048]{2,1,0:T(4,128)S(1)}, f32[3,3,2048]{2,1,0:T(4,128)}, u32[]{:S(2)}) copy-start(f32[3,3,2048]{2,1,0:T(4,128)} %short_ref.4) | copy-start | bytes 221188
  91.7 41.5 %collective-permute-start.16 = (bf16[5,336,128]{2,1,0:T(8,128)(2,1)}, bf16[5,336,128]{2,1,0:T(8,128)(2,1)}, u32[]{:S(2)}, u32[]{:S(2)}) collective-permute-start(bf16[5,336,128]{2,1,0:T(8,128)(2,1)} %get-tuple-element.32), channel_id=1, source_target_pairs={{4,8},{8,12},{5,9},{9,13},{6,10},{10,14},{7,11},{11,15},{20,24},{2... | collective-permute-start | bytes 1290248 | tf_op jit(solution)/shard_map/ppermute | solution.py:564
  127.2 52.3 %collective-permute-start.6 = (bf16[2,336,128]{2,1,0:T(8,128)(2,1)}, bf16[2,336,128]{2,1,0:T(8,128)(2,1)S(1)}, u32[]{:S(2)}, u32[]{:S(2)}) collective-permute-start(bf16[2,336,128]{2,1,0:T(8,128)(2,1)} %get-tuple-element.26), channel_id=1, source_target_pairs={{4,8},{8,12},{5,9},{9,13},{6,10},{10,14},{7,11},{11,15},{20,24},{2... | collective-permute-start | bytes 516104 | tf_op jit(solution)/shard_map/ppermute | solution.py:564
  128.5 51.0 %collective-permute-start.7 = (bf16[2,336,128]{2,1,0:T(8,128)(2,1)S(1)}, bf16[2,336,128]{2,1,0:T(8,128)(2,1)S(1)}, u32[]{:S(2)}, u32[]{:S(2)}) collective-permute-start(bf16[2,336,128]{2,1,0:T(8,128)(2,1)S(1)} %get-tuple-element.27), channel_id=1, source_target_pairs={{4,12},{5,13},{6,14},{7,15},{20,28},{21,29},{22,30},{23,31}} | collective-permute-start | bytes 516104 | tf_op jit(solution)/shard_map/ppermute | solution.py:565
  129.8 47.5 %collective-permute-start.11 = (bf16[4,336,128]{2,1,0:T(8,128)(2,1)S(1)}, bf16[4,336,128]{2,1,0:T(8,128)(2,1)S(1)}, u32[]{:S(2)}, u32[]{:S(2)}) collective-permute-start(bf16[4,336,128]{2,1,0:T(8,128)(2,1)S(1)} %get-tuple-element.29), channel_id=1, source_target_pairs={{4,8},{8,12},{5,9},{9,13},{6,10},{10,14},{7,11},{11,15},{20,24},{2... | collective-permute-start | bytes 1032200 | tf_op jit(solution)/shard_map/ppermute | solution.py:564
  131.9 45.4 %collective-permute-start.12 = (bf16[4,336,128]{2,1,0:T(8,128)(2,1)S(1)}, bf16[4,336,128]{2,1,0:T(8,128)(2,1)S(1)}, u32[]{:S(2)}, u32[]{:S(2)}) collective-permute-start(bf16[4,336,128]{2,1,0:T(8,128)(2,1)S(1)} %get-tuple-element.30), channel_id=1, source_target_pairs={{4,12},{5,13},{6,14},{7,15},{20,28},{21,29},{22,30},{23,31}} | collective-permute-start | bytes 1032200 | tf_op jit(solution)/shard_map/ppermute | solution.py:565
  133.2 39.9 %collective-permute-start.17 = (bf16[5,336,128]{2,1,0:T(8,128)(2,1)S(1)}, bf16[5,336,128]{2,1,0:T(8,128)(2,1)S(1)}, u32[]{:S(2)}, u32[]{:S(2)}) collective-permute-start(bf16[5,336,128]{2,1,0:T(8,128)(2,1)S(1)} %copy-done.27), channel_id=1, source_target_pairs={{4,12},{5,13},{6,14},{7,15},{20,28},{21,29},{22,30},{23,31}} | collective-permute-start | bytes 1290248 | tf_op jit(solution)/shard_map/ppermute | solution.py:565
  142.6 30.5 %copy-start.4 = (bf16[5,336,128]{2,1,0:T(8,128)(2,1)S(1)}, bf16[5,336,128]{2,1,0:T(8,128)(2,1)}, u32[]{:S(2)}) copy-start(bf16[5,336,128]{2,1,0:T(8,128)(2,1)} %copy-done.3) | copy-start | bytes 1290244
  (20 other events, 126.1 us)

commit v2 on v1

--- a/solution.py
+++ b/solution.py
@@ -13,11 +13,12 @@
 F32 = jnp.float32
 BF16 = jnp.bfloat16
 SCALE2 = float(np.log2(np.e) / np.sqrt(HD))
-CHUNKS = (5, 5, 4, 2)
+PARTS = 4
 STAT_ROWS = 16
 WINDOW = 256
 BLOCK = 128
-VMEM_LIMIT = 48 * 1024 * 1024
+VMEM_LIMIT = 36 * 1024 * 1024
+VMEM_EARLY = 60 * 1024 * 1024
 
 
 def split_np(value):
@@ -107,7 +108,16 @@
         out_ref[r : r + step] = (featurize(q_s, tq, 8 + r, step) * acc).astype(BF16)
 
 
-def mr_tail_kernel(k_ref, v_ref, short_ref, out_ref, k_s, v_s):
+def raw_kernel(se_ref, mr_ref, raw_ref):
+    se, mr = se_ref[...].astype(F32), mr_ref[...].astype(F32)
+    raw_ref[...] = jnp.concatenate(
+        [se[1, 8:], se[2, 8:], se[0, 14:], mr[0, 14:], mr[1, 14:], mr[2, 14:]]
+        + [jnp.zeros((8, se.shape[2]), F32)],
+        axis=0,
+    ).astype(BF16)
+
+
+def tail_kernel(k_ref, v_ref, short_ref, out_ref, k_s, v_s):
     half = k_ref.shape[1]
     k_s[...] = k_ref[0].astype(F32)
     v_s[...] = v_ref[0].astype(F32)
@@ -160,7 +170,7 @@
 
 
 def mr_head_kernel(
-    utail_ref, lead_ref, spec_ref, query_ref, tail_ref, short_ref, fwd_ref, inv_ref, part_ref,
+    idx_ref, low_ref, high_ref, lead_ref, spec_ref, query_ref, tail_ref, short_ref, fwd_ref, inv_ref, part_ref,
     out_ref, q_s,
 ):
     del part_ref
@@ -169,7 +179,8 @@
     q_s[0:8] = jnp.concatenate([jnp.zeros((6, width), F32), tail[18:20]], axis=0)
     q_s[8 : 8 + BLOCK] = query_ref[0].astype(F32)
     tq = tap_rows(short_ref, 0)
-    window = jnp.concatenate([utail_ref[...], lead_ref[...]], axis=0)
+    before = jnp.where(idx_ref[0] == 1, low_ref[...].astype(F32), high_ref[...].astype(F32))
+    window = jnp.concatenate([before.astype(BF16), lead_ref[...]], axis=0)
     mixed = back_of(inv_ref[...], spectral(forward_of(fwd_ref[...], window), spec_ref[...]))
     for r in range(0, BLOCK, 64):
         out_ref[r : r + 64] = (featurize(q_s, tq, 8 + r, 64) * mixed[r : r + 64]).astype(BF16)
@@ -183,21 +194,23 @@
     return lax.dot_general(left, right, (((0,), (0,)), ((), ())), preferred_element_type=F32)
 
 
-def partial_of(query, pairs, masked=False):
-    scores = [nt_dot(keys, query) for keys, _ in pairs]
-    if masked:
-        shape = scores[0].shape
-        below = lax.broadcasted_iota(jnp.int32, shape, 0) <= lax.broadcasted_iota(
-            jnp.int32, shape, 1
-        )
-        scores = [jnp.where(below, scores[0], F32(-1e30))]
-    peak = functools.reduce(jnp.maximum, [jnp.max(s, axis=0, keepdims=True) for s in scores])
-    weights = [jnp.exp2((s - peak) * SCALE2) for s in scores]
-    total = functools.reduce(jnp.add, [jnp.sum(w, axis=0, keepdims=True) for w in weights])
-    mixed = functools.reduce(
-        jnp.add, [tt_dot(vals, w.astype(BF16)) for w, (_, vals) in zip(weights, pairs)]
-    )
-    return mixed / total, peak * SCALE2 + jnp.log2(total)
+def partials_of(jobs, masked=None):
+    scores = [nt_dot(keys, query) for query, keys, _ in jobs]
+    if masked is not None:
+        key = lax.broadcasted_iota(jnp.int32, scores[0].shape, 0)
+        row = lax.broadcasted_iota(jnp.int32, scores[0].shape, 1)
+        seen = masked(key, row)
+        scores = [jnp.where(seen, s, F32(-1e30)) for s in scores]
+    ready = []
+    for s in scores:
+        peak = jnp.max(s, axis=0, keepdims=True)
+        weights = jnp.exp2((s - peak) * SCALE2)
+        ready.append((weights.astype(BF16), peak, jnp.sum(weights, axis=0, keepdims=True)))
+    results = []
+    for (weights, peak, total), (_, _, values) in zip(ready, jobs):
+        mixed = tt_dot(values, weights) * (1.0 / total)
+        results.append((mixed.T, peak * SCALE2 + jnp.log2(total)))
+    return results
 
 
 def padded(rows):
@@ -227,68 +240,113 @@
     return jnp.concatenate([total[j : j + 1] for j in range(lanes)], axis=1)
 
 
-def put_payload(ref, mixed, stat, rows):
-    ref[0, :rows] = mixed[:rows].astype(BF16)
-    ref[0, rows : rows + STAT_ROWS] = stat_block(stat)
-
-
-def local_kernel(q_ref, k_ref, v_ref, out_ref, stat_ref):
+def put_payload(ref, slot, mixed, stat, rows):
+    extra = padded(rows) - rows
+    if extra:
+        stat = jnp.concatenate([stat[:, :rows], jnp.zeros((1, extra), F32)], axis=1)
+    ref[slot, :rows] = mixed[:rows].astype(BF16)
+    ref[slot, rows : rows + STAT_ROWS] = stat_block(stat)
+
+
+def lanes_of(ref, slot, *lead):
+    return ref[(*lead, slice(None), slice(slot * HD, (slot + 1) * HD))]
+
+
+def local_kernel(idx_ref, q_ref, k_ref, v_ref, out_ref, stat_ref):
     rows = q_ref.shape[1]
-    mixed, stat = partial_of(pad_rows(q_ref[0]), [(k_ref[0], v_ref[0])], masked=True)
-    out_ref[0] = mixed.T[:rows]
-    stat_ref[0] = jnp.broadcast_to(stat, stat_ref.shape[1:])
-
-
-def cross_kernel(
-    idx_ref, q_ref, k_ref, v_ref, first_ref, next_ref, last_ref, own_ref, up_ref, far_ref
-):
+    slots = range(out_ref.shape[0])
+
+    @pl.when(idx_ref[0] != 1)
+    def _():
+        jobs = [
+            (pad_rows(lanes_of(q_ref, j, 0)), lanes_of(k_ref, j, 0), lanes_of(v_ref, j, 0))
+            for j in slots
+        ]
+        for j, (mixed, stat) in zip(slots, partials_of(jobs, lambda key, row: key <= row)):
+            out_ref[j] = mixed[:rows]
+            stat_ref[j] = jnp.broadcast_to(stat, stat_ref.shape[1:])
+
+
+def cross_kernel(has_ahead, has_done, idx_ref, q_ref, k_ref, v_ref, first_ref, *refs):
+    if has_ahead:
+        ahead_ref, refs = refs[0], refs[1:]
+    near_ref, last_ref = refs[:2]
+    own_ref, up_ref, far_ref = refs[3 if has_done else 2 :]
     rows = q_ref.shape[1]
     index = idx_ref[0]
+    slots = range(up_ref.shape[0])
 
     @pl.when(index == 1)
     def _():
-        early = (first_ref[0], first_ref[1])
-        here = (k_ref[0], v_ref[0])
-        both = jnp.concatenate([next_ref[...], last_ref[...]], axis=0)
-        mixed, stat = partial_of(both, [early, here])
-        mixed = mixed.T
-        pad = jnp.zeros((1, padded(rows) - rows), F32)
-        put_payload(up_ref, mixed[:rows], jnp.concatenate([stat[:, :rows], pad], axis=1), rows)
-        put_payload(far_ref, mixed[rows:], jnp.concatenate([stat[:, rows:], pad], axis=1), rows)
-        mixed, stat = partial_of(pad_rows(q_ref[0]), [early])
-        put_payload(own_ref, mixed.T, stat, rows)
+        jobs = []
+        for j in slots:
+            query = [lanes_of(q_ref, j, 0), near_ref[j, :rows], last_ref[j, :rows]]
+            keys = [lanes_of(first_ref, j, 0), lanes_of(k_ref, j, 0)]
+            values = [lanes_of(first_ref, j, 1), lanes_of(v_ref, j, 0)]
+            jobs.append(
+                (
+                    pad_rows(jnp.concatenate(query, axis=0)),
+                    jnp.concatenate(keys, axis=0),
+                    jnp.concatenate(values, axis=0),
+                )
+            )
+        seen = lambda key, row: (key <= row + rows) | (row >= rows)
+        for j, (mixed, stat) in zip(slots, partials_of(jobs, seen)):
+            own_ref[:, j * HD : (j + 1) * HD] = mixed[:rows].astype(BF16)
+            put_payload(up_ref, j, mixed[rows : 2 * rows], stat[:, rows : 2 * rows], rows)
+            put_payload(far_ref, j, mixed[2 * rows : 3 * rows], stat[:, 2 * rows : 3 * rows], rows)
 
     @pl.when(index == 2)
     def _():
-        mixed, stat = partial_of(pad_rows(next_ref[...]), [(k_ref[0], v_ref[0])])
-        put_payload(up_ref, mixed.T, stat, rows)
-
-
-def merge_kernel(idx_ref, loc_ref, stat_ref, own_ref, up_ref, far_ref, *rest):
-    out_ref = rest[-1]
+        jobs = [
+            (pad_rows(near_ref[j, :rows]), lanes_of(k_ref, j, 0), lanes_of(v_ref, j, 0))
+            for j in slots
+        ]
+        for j, (mixed, stat) in zip(slots, partials_of(jobs)):
+            put_payload(up_ref, j, mixed, stat, rows)
+
+    if has_ahead:
+
+        @pl.when(index >= 2)
+        def _():
+            for j in slots:
+                ask = lanes_of(ahead_ref, j, 0)
+
+                far_ref[j, :rows] = ask
+
+                @pl.when(index == 3)
+                def _():
+                    up_ref[j, :rows] = ask
+
+
+def merge_kernel(idx_ref, loc_ref, stat_ref, up_ref, far_ref, own_ref, out_ref):
     rows = loc_ref.shape[1]
     lanes = padded(rows) // 128
     index = idx_ref[0]
+    slots = range(loc_ref.shape[0])
 
     def merged(parts):
-        stats = [stat_ref[0, 0:1]] + [stat_of(p[0, rows : rows + STAT_ROWS], lanes) for p in parts]
-        values = [loc_ref[0]] + [p[0, :rows].astype(F32) for p in parts]
-        top = functools.reduce(jnp.maximum, stats)
-        weights = [jnp.exp2(s - top) for s in stats]
-        total = functools.reduce(jnp.add, weights)
-        result = 0.0
-        for weight, value in zip(weights, values):
-            column = jnp.broadcast_to(weight / total, (128, padded(rows))).T[:rows]
-            result = result + column * value
-        out_ref[...] = result.astype(BF16)
+        for j in slots:
+            stats = [stat_ref[j, 0:1]]
+            stats += [stat_of(p[j, rows : rows + STAT_ROWS], lanes) for p in parts]
+            base = loc_ref[j]
+            top = functools.reduce(jnp.maximum, stats)
+            weights = [jnp.exp2(s - top) for s in stats]
+            scale = 1.0 / functools.reduce(jnp.add, weights)
+            result = base
+            for weight, part in zip(weights[1:], parts):
+                column = jnp.broadcast_to(weight * scale, (128, padded(rows))).T[:rows]
+                result = result + column * (part[j, :rows].astype(F32) - base)
+            out_ref[:, j * HD : (j + 1) * HD] = result.astype(BF16)
 
     @pl.when(index == 0)
     def _():
-        out_ref[...] = loc_ref[0].astype(BF16)
+        for j in slots:
+            out_ref[:, j * HD : (j + 1) * HD] = loc_ref[j].astype(BF16)
 
     @pl.when(index == 1)
     def _():
-        merged([own_ref])
+        out_ref[...] = own_ref[...]
 
     @pl.when(index == 2)
     def _():
@@ -299,12 +357,66 @@
         merged([up_ref, far_ref])
 
 
-def params():
-    return pltpu.CompilerParams(vmem_limit_bytes=VMEM_LIMIT)
+def pack_kernel(lows, asks, part, idx_ref, qkv_ref, *refs):
+    low_refs, ask_refs = refs[: len(lows)], refs[len(lows) : len(lows) + len(asks)]
+    low_s, ask_s, sems = refs[len(lows) + len(asks) :]
+    rows = qkv_ref.shape[1]
+    heads = part // HD
+    index = idx_ref[0]
+
+    def cols(c):
+        return pl.ds(c * part, part)
+
+    def move(steps):
+        loads, stores = [], []
+        for source, place, targets in steps:
+            load = pltpu.make_async_copy(source, place, sems.at[0, len(loads)])
+            load.start()
+            loads.append(load)
+        for load, (_, _, targets) in zip(loads, steps):
+            load.wait()
+            for source, target in targets:
+                store = pltpu.make_async_copy(source, target, sems.at[1, len(stores)])
+                store.start()
+                stores.append(store)
+        for store in stores:
+            store.wait()
+
+    def ask_steps():
+        return [
+            (
+                qkv_ref.at[0, :, cols(c)],
+                ask_s.at[i],
+                [
+                    (ask_s.at[i, :, pl.ds(h * HD, HD)], ask_refs[i].at[h, pl.ds(0, rows), :])
+                    for h in range(heads)
+                ],
+            )
+            for i, c in enumerate(asks)
+        ]
+
+    @pl.when(index == 0)
+    def _():
+        move(
+            [
+                (qkv_ref.at[1:3, :, cols(c)], low_s.at[i], [(low_s.at[i], low_refs[i])])
+                for i, c in enumerate(lows)
+            ]
+        )
+
+    if asks:
+
+        @pl.when(index >= 2)
+        def _():
+            move(ask_steps())
+
+
+def params(limit=VMEM_LIMIT):
+    return pltpu.CompilerParams(vmem_limit_bytes=limit)
 
 
 def cost(flops, size):
-    return pl.CostEstimate(flops=int(flops), bytes_accessed=int(size), transcendentals=0)
+    return pl.CostEstimate(flops=1, bytes_accessed=1, transcendentals=0)
 
 
 SMEM = pl.BlockSpec(memory_space=pltpu.SMEM)
@@ -344,12 +456,28 @@
     )(qkv, tail, short, filt)
 
 
-def mr_tail(qkv, short):
-    rows, width = qkv.shape[1:]
-    cols = 512
+def raw_of(se_qkv, mr_qkv):
+    rows, width = mr_qkv.shape[1:]
+    last = rows // 16 - 1
+    tail = pl.BlockSpec((3, 16, width), lambda j: (0, last, 0))
+    return pl.pallas_call(
+        raw_kernel,
+        grid=(1,),
+        in_specs=[tail, tail],
+        out_specs=pl.BlockSpec((32, width), lambda j: (0, 0)),
+        out_shape=shape((32, width), BF16),
+        compiler_params=params(VMEM_EARLY),
+        cost_estimate=cost(0, 0),
+        name="raw_tail",
+    )(se_qkv, mr_qkv)
+
+
+def product_of(mr_qkv, short):
+    rows, width = mr_qkv.shape[1:]
+    cols = min(1024, width)
     half = rows // 2
     return pl.pallas_call(
-        mr_tail_kernel,
+        tail_kernel,
         grid=(width // cols,),
         in_specs=[
             pl.BlockSpec((1, half, cols), lambda j: (1, 1, j)),
@@ -359,15 +487,39 @@
         out_specs=pl.BlockSpec((BLOCK, cols), lambda j: (0, j)),
         out_shape=shape((BLOCK, width), BF16),
         scratch_shapes=[pltpu.VMEM((half, cols), F32), pltpu.VMEM((half, cols), F32)],
-        compiler_params=params(),
+        compiler_params=params(VMEM_EARLY),
         cost_estimate=cost(BLOCK * width * 12, rows * width * 3),
-        name="mr_tail",
-    )(qkv, qkv, short)
+        name="product_tail",
+    )(mr_qkv, mr_qkv, short)
+
+
+def pack(index, qkv, lows, asks):
+    rows, width = qkv.shape[1:]
+    count = width // HD // PARTS
+    part = count * HD
+    anywhere = pl.BlockSpec(memory_space=pl.ANY)
+    total = len(lows) + len(asks)
+    out = pl.pallas_call(
+        functools.partial(pack_kernel, lows, asks, part),
+        in_specs=[SMEM, anywhere],
+        out_specs=[anywhere] * total,
+        out_shape=[shape((2, rows, part), BF16)] * len(lows)
+        + [shape((count, rows + STAT_ROWS, HD), BF16)] * len(asks),
+        scratch_shapes=[
+            pltpu.VMEM((max(len(lows), 1), 2, rows, part), BF16),
+            pltpu.VMEM((max(len(asks), 1), rows, part), BF16),
+            pltpu.SemaphoreType.DMA((2, len(lows) + len(asks) * count)),
+        ],
+        compiler_params=params(VMEM_EARLY),
+        cost_estimate=cost(0, 0),
+        name="pack",
+    )(index, qkv)
+    return out[: len(lows)], out[len(lows) :]
 
 
 def mr_main(qkv, tail, short, filt, decay, fwd, inv):
     rows, width = qkv.shape[1:]
-    cols = 256
+    cols = 512
     col = lambda j: (0, j)
     return pl.pallas_call(
         mr_main_kernel,
@@ -398,14 +550,16 @@
     )(qkv, tail, short, filt, decay[None, :], fwd, inv)
 
 
-def mr_head(utail, lead, spec, qkv, tail, short, fwd, inv, part):
+def mr_head(index, low, high, lead, spec, qkv, tail, short, fwd, inv, part):
     rows, width = qkv.shape[1:]
-    cols = 256
+    cols = 512
     col = lambda j: (0, j)
     return pl.pallas_call(
         mr_head_kernel,
         grid=(width // cols,),
         in_specs=[
+            SMEM,
+            pl.BlockSpec((BLOCK, cols), col),
             pl.BlockSpec((BLOCK, cols), col),
             pl.BlockSpec((BLOCK, cols), col),
             pl.BlockSpec((WINDOW, cols), col),
@@ -419,84 +573,118 @@
         out_specs=pl.BlockSpec((BLOCK, cols), col),
         out_shape=shape((rows, width), BF16),
         scratch_shapes=[pltpu.VMEM((8 + BLOCK, cols), F32)],
-        input_output_aliases={8: 0},
+        input_output_aliases={10: 0},
         compiler_params=params(),
         cost_estimate=cost(WINDOW * WINDOW * width * 6, rows * width * 4),
         name="mr_head",
-    )(utail, lead, spec, qkv, tail, short, fwd, inv, part)
-
-
-def head_spec(which, rows, offset):
-    return pl.BlockSpec((1, rows, HD), lambda h: (which, 0, h + offset))
-
-
-def local_attention(qkv):
+    )(index, low, high, lead, spec, qkv, tail, short, fwd, inv, part)
+
+
+def per_step(count):
+    return 2 if count % 2 == 0 else 1
+
+
+def head_spec(which, rows, per, offset):
+    return pl.BlockSpec((1, rows, per * HD), lambda h: (which, 0, h + offset // per))
+
+
+def unless_first(place):
+    return lambda h, idx: jnp.where(idx[0] == 1, 0, h + place)
+
+
+def local_attention(index, qkv):
     rows, width = qkv.shape[1:]
     heads = width // HD
+    per = 4 if heads % 4 == 0 else 1
+    at = unless_first(0)
+
+    def part(which):
+        return pl.BlockSpec((1, rows, per * HD), lambda h, idx: (which, 0, at(h, idx)))
+
     return pl.pallas_call(
         local_kernel,
-        grid=(heads,),
-        in_specs=[head_spec(j, rows, 0) for j in range(3)],
-        out_specs=[
-            pl.BlockSpec((1, rows, HD), lambda h: (h, 0, 0)),
-            pl.BlockSpec((1, 8, padded(rows)), lambda h: (h, 0, 0)),
-        ],
+        grid_spec=pltpu.PrefetchScalarGridSpec(
+            num_scalar_prefetch=1,
+            grid=(heads // per,),
+            in_specs=[part(j) for j in range(3)],
+            out_specs=[
+                pl.BlockSpec((per, rows, HD), lambda h, idx: (at(h, idx), 0, 0)),
+                pl.BlockSpec((per, 8, padded(rows)), lambda h, idx: (at(h, idx), 0, 0)),
+            ],
+        ),
         out_shape=[shape((heads, rows, HD), F32), shape((heads, 8, padded(rows)), F32)],
         compiler_params=params(),
         cost_estimate=cost(heads * rows * rows * 512, rows * width * 10),
         name="local_attention",
-    )(qkv, qkv, qkv)
-
-
-def cross_attention(index, qkv, first, following, last, offset, count):
-    rows = qkv.shape[1]
-    block = pl.BlockSpec((1, rows + STAT_ROWS, HD), lambda h: (h, 0, 0))
-    return pl.pallas_call(
-        cross_kernel,
-        grid=(count,),
-        in_specs=[SMEM]
-        + [head_spec(j, rows, offset) for j in range(3)]
-        + [
-            pl.BlockSpec((2, rows, HD), lambda h: (0, 0, h)),
-            pl.BlockSpec((rows, HD), lambda h: (0, h)),
-            pl.BlockSpec((rows, HD), lambda h: (0, h)),
-        ],
-        out_specs=[block] * 3,
-        out_shape=[shape((count, rows + STAT_ROWS, HD), BF16)] * 3,
-        compiler_params=params(),
-        cost_estimate=cost(count * rows * rows * 2560, count * rows * HD * 20),
-        name="cross_attention",
-    )(index, qkv, qkv, qkv, first, following, last)
-
-
-def merge_attention(index, local, stats, own, up, far, offset, count, done, width):
-    rows = local.shape[1]
-    block = pl.BlockSpec((1, rows + STAT_ROWS, HD), lambda h: (h, 0, 0))
-    operands = [index, local, stats, own, up, far]
-    specs = [
-        SMEM,
-        pl.BlockSpec((1, rows, HD), lambda h: (h + offset, 0, 0)),
-        pl.BlockSpec((1, 8, padded(rows)), lambda h: (h + offset, 0, 0)),
-        block,
-        block,
-        block,
-    ]
+    )(index, qkv, qkv, qkv)
+
+
+def cross_attention(index, qkv, first, near, last, done, c):
+    rows, width = qkv.shape[1:]
+    count = width // HD // PARTS
+    per = per_step(count)
+    steps = count // per
+    block = pl.BlockSpec((per, rows + STAT_ROWS, HD), lambda h: (h, 0, 0))
+    has_ahead = c + 2 < PARTS
+
+    def part(which, chunk):
+        return pl.BlockSpec((1, rows, per * HD), lambda h: (which, 0, h + chunk * steps))
+
+    specs = [SMEM] + [part(j, c) for j in range(3)]
+    specs.append(pl.BlockSpec((2, rows, per * HD), lambda h: (0, 0, h)))
+    operands = [index, qkv, qkv, qkv, first]
+    if has_ahead:
+        specs.append(part(0, c + 2))
+        operands.append(qkv)
+    operands += [near, last]
+    specs += [block, block]
     aliases = {}
     if done is not None:
         aliases = {len(operands): 0}
         operands.append(done)
         specs.append(pl.BlockSpec(memory_space=pl.ANY))
     return pl.pallas_call(
+        functools.partial(cross_kernel, has_ahead, done is not None),
+        grid=(steps,),
+        in_specs=specs,
+        out_specs=[pl.BlockSpec((rows, per * HD), lambda h: (0, h + c * steps)), block, block],
+        out_shape=[shape((rows, width), BF16)]
+        + [shape((count, rows + STAT_ROWS, HD), BF16)] * 2,
+        input_output_aliases=aliases,
+        compiler_params=params(),
+        cost_estimate=cost(count * rows * rows * 3072, count * rows * HD * 20),
+        name="cross_attention",
+    )(*operands)
+
+
+def merge_attention(index, local, stats, up, far, done, c):
+    rows, width = done.shape
+    count = width // HD // PARTS
+    per = per_step(count)
+    steps = count // per
+    here, there = unless_first(0), unless_first(c * steps)
+    block = pl.BlockSpec((per, rows + STAT_ROWS, HD), lambda h, idx: (here(h, idx), 0, 0))
+    flat = pl.BlockSpec((rows, per * HD), lambda h, idx: (0, there(h, idx)))
+    return pl.pallas_call(
         merge_kernel,
-        grid=(count,),
-        in_specs=specs,
-        out_specs=pl.BlockSpec((rows, HD), lambda h: (0, h + offset)),
+        grid_spec=pltpu.PrefetchScalarGridSpec(
+            num_scalar_prefetch=1,
+            grid=(steps,),
+            in_specs=[
+                pl.BlockSpec((per, rows, HD), lambda h, idx: (there(h, idx), 0, 0)),
+                pl.BlockSpec((per, 8, padded(rows)), lambda h, idx: (there(h, idx), 0, 0)),
+                block,
+                block,
+                flat,
+            ],
+            out_specs=flat,
+        ),
         out_shape=shape((rows, width), BF16),
-        input_output_aliases=aliases,
+        input_output_aliases={5: 0},
         compiler_params=params(),
         cost_estimate=cost(count * rows * HD * 40, count * rows * HD * 12),
         name="merge_attention",
-    )(*operands)
+    )(index, local, stats, up, far, done)
 
 
 def gathered_attention(attn_qkv):
@@ -523,56 +711,88 @@
     return (mixed / total.T[:, :, None]).astype(BF16).reshape(rows, width)
 
 
+def after(value, *needed):
+    return lax.optimization_barrier((value,) + needed)[0]
+
+
 def on_device(se_qkv, se_short, se_filter, mr_qkv, mr_short, mr_filter, mr_decay, attn_qkv):
     rows, width = se_qkv.shape[1:]
     spans = lax.axis_size("seq")
-    heads = width // HD
     fwd, inv = (jnp.asarray(m) for m in transforms())
     rising = [(s, s + 1) for s in range(spans - 1)]
-    raw = jnp.concatenate(
-        [
-            se_qkv[1, rows - 8 :],
-            se_qkv[2, rows - 8 :],
-            se_qkv[0, rows - 2 :],
-            mr_qkv[0, rows - 2 :],
-            mr_qkv[1, rows - 2 :],
-            mr_qkv[2, rows - 2 :],
-            jnp.zeros((8, width), BF16),
-        ],
-        axis=0,
-    )
-    raw = lax.ppermute(raw, "seq", rising)
-    product = mr_tail(mr_qkv, mr_short)
+    if spans == 4 and width % (PARTS * HD) == 0:
+        return four_spans(
+            se_qkv, se_short, se_filter, mr_qkv, mr_short, mr_filter, mr_decay, attn_qkv, fwd, inv
+        )
+    raw = lax.ppermute(raw_of(se_qkv, mr_qkv), "seq", rising)
+    product = product_of(mr_qkv, mr_short)
     se_out = se_mixer(se_qkv, raw, se_short, se_filter)
     mr_part, spec, lead = mr_main(mr_qkv, raw, mr_short, mr_filter, mr_decay, fwd, inv)
-
-    if spans == 4:
-        index = lax.axis_index("seq").astype(jnp.int32).reshape(1)
-        starts = [sum(CHUNKS[:c]) for c in range(len(CHUNKS))]
-        local, stats = local_attention(attn_qkv)
-        upper = lax.ppermute(product, "seq", [(1, 2), (2, 3)])
-        lower = lax.ppermute(product, "seq", [(0, 1)])
-        utail = jnp.where(index[0] == 1, lower, upper)
-        pieces = []
-        for start, count in zip(starts, CHUNKS):
-            cols = slice(start * HD, (start + count) * HD)
-            first = lax.ppermute(attn_qkv[1:, :, cols], "seq", [(0, 1)])
-            asked = attn_qkv[0, :, cols]
-            following = lax.ppermute(asked, "seq", [(2, 1), (3, 2)])
-            last = lax.ppermute(asked, "seq", [(3, 1)])
-            own, up, far = cross_attention(index, attn_qkv, first, following, last, start, count)
-            up = lax.ppermute(up, "seq", [(1, 2), (2, 3)])
-            far = lax.ppermute(far, "seq", [(1, 3)])
-            pieces.append((own, up, far))
-        attn_out = None
-        for start, count, piece in zip(starts, CHUNKS, pieces):
-            attn_out = merge_attention(
-                index, local, stats, *piece, start, count, attn_out, width
+    utail = lax.ppermute(product, "seq", rising)
+    attn_out = gathered_attention(attn_qkv)
+    index = lax.axis_index("seq").astype(jnp.int32).reshape(1)
+    mr_out = mr_head(
+        index, utail, utail, lead, spec, mr_qkv, raw, mr_short, fwd, inv, mr_part
+    )
+    return (se_out, mr_out, attn_out)
+
+
+def four_spans(
+    se_qkv, se_short, se_filter, mr_qkv, mr_short, mr_filter, mr_decay, attn_qkv, fwd, inv
+):
+    width = attn_qkv.shape[2]
+    count = width // HD // PARTS
+    send = lambda value, *pairs: lax.ppermute(value, "seq", list(pairs))
+    index = lax.axis_index("seq").astype(jnp.int32).reshape(1)
+    raw_own = raw_of(se_qkv, mr_qkv)
+    raw = send(raw_own, (0, 1), (1, 2), (2, 3))
+    a_in, ask_in = pack(index, after(attn_qkv, raw_own), [0], [0])
+    a, b, d, up, far = ({} for _ in range(5))
+    from_above = [(2, 1), (3, 2)]
+    merging = [(1, 2), (2, 3)]
+    b[0] = send(ask_in[0], (3, 1))
+    d[0] = send(ask_in[0], *from_above)
+    a[0] = send(a_in[0], (0, 1))
+    product = product_of(after(mr_qkv, a_in[0], raw), mr_short)
+    upper = send(product, (1, 2), (2, 3))
+    later = pack(index, after(attn_qkv, product), [1, 2, 3], [1])
+    a_in, ask_in = a_in + later[0], ask_in + later[1]
+    se_out = se_mixer(after(se_qkv, a_in[1]), raw, se_short, se_filter)
+    local, stats = local_attention(index, after(attn_qkv, se_out, b[0], d[0]))
+
+    def cross(c, done, *needed):
+        return cross_attention(index, attn_qkv, after(a[c], *needed), d[c], b[c], done, c)
+
+    a[1] = send(after(a_in[1], raw), (0, 1))
+    b[1] = send(after(ask_in[1], b[0], d[0], se_out), (3, 1))
+    d[1] = send(after(ask_in[1], b[0], d[0], se_out), *from_above)
+    attn_out, up[0], far[0] = cross(0, None, upper, stats)
+    b[2] = send(up[0], (3, 1), *merging)
+    d[2] = send(far[0], (1, 3), *from_above)
+    a[2] = send(after(a_in[2], a[1]), (0, 1))
+    a[3] = send(after(a_in[3], a[1], b[1], d[1], up[0]), (0, 1))
+    attn_out, up[1], far[1] = cross(1, attn_out)
+    b[3] = send(up[1], (3, 1), *merging)
+    d[3] = send(after(far[1], b[2]), (1, 3), *from_above)
+    lower = send(after(product, a[2], up[1]), (0, 1))
+    attn_out, up[2], far[2] = cross(2, attn_out)
+    b[4] = send(up[2], *merging)
+    d[4] = send(after(far[2], b[3]), (1, 3))
+    attn_out, up[3], far[3] = cross(3, attn_out)
+    b[5] = send(up[3], *merging)
+    d[5] = send(far[3], (1, 3))
+    mr_part, spec, lead = mr_main(
+        after(mr_qkv, attn_out), raw, mr_short, mr_filter, mr_decay, fwd, inv
+    )
+    for c in range(PARTS):
+        if c == PARTS - 1:
+            mr_out = mr_head(
+                index, lower, upper, lead, spec, mr_qkv, raw, mr_short, fwd, inv, mr_part
             )
-    else:
-        utail = lax.ppermute(product, "seq", rising)
-        attn_out = gathered_attention(attn_qkv)
-    mr_out = mr_head(utail, lead, spec, mr_qkv, raw, mr_short, fwd, inv, mr_part)
+            local = after(local, mr_out)
+        attn_out = merge_attention(
+            index, after(local, lead), stats, b[c + 2], d[c + 2], attn_out, c
+        )
     return (se_out, mr_out, attn_out)
 
 

time: 183 us -> 114 us (0.62)
  starting transfers between devices: 65.3 us -> 43.7 us
  local copies, waits for them, and re-layouts: 17.2 us -> 0.94 us
  Pallas kernels: 59.9 us -> 44.5 us
  waiting for transfers between devices: 36.1 us -> 23.1 us
    ppermute x23 -> x19, starting transfers between devices: 65.3 us -> 43.7 us  [four_spans(): send = lambda value, *pairs: lax.ppermute(value, 'seq', list(pairs))]
    pallas_call x11 -> x14, Pallas kernels: 43.3 us -> 29.5 us  [the longest x4 9.07 us: merge_attention(): pl.pallas_call(merge_kernel, grid_spec=pltpu.PrefetchScalarGridSpec(num_s...]
    ppermute x23 -> x19, waiting for transfers between devices: 36.1 us -> 23.1 us  [four_spans(): send = lambda value, *pairs: lax.ppermute(value, 'seq', list(pairs))]
    slice x3 -> x0, local copies, waits for them, and re-layouts: 6.4 us -> none  [on_device(): first = lax.ppermute(attn_qkv[1:, :, cols], 'seq', [(0, 1)])]
    squeeze x6 -> x0, local copies, waits for them, and re-layouts: 6.23 us -> none  [the longest x3 3.86 us: on_device(): asked = attn_qkv[0, :, cols]]
    unnamed x58 -> x28, local copies, waits for them, and re-layouts: 4.47 us -> 0.94 us
  transfers between devices with their start and end apart: 23 -> 19, of which waited for: 3 -> 6; matrix products, arithmetic and copies ran while one was open for 7% -> 0% of each run, Pallas kernels for 32% -> 31%
where the time goes in v2:
time: 114 us; the launch traced here: 113 us
  Pallas kernels  44.5 us (39%)
  starting transfers between devices  43.7 us (38%)
  waiting for transfers between devices  23.1 us (20%)
    ppermute x19, starting transfers between devices, four_spans(): send = lambda value, *pairs: lax.ppermute(value, 'seq', list(pairs))  43.7 us
    ppermute x19, waiting for transfers between devices, four_spans(): send = lambda value, *pairs: lax.ppermute(value, 'seq', list(pairs))  23.1 us
    pallas_call x4, Pallas kernels, merge_attention(): pl.pallas_call(merge_kernel, grid_spec=pltpu.PrefetchScalarGridSpec(num_s...  9.07 us
    pallas_call x1, Pallas kernels, mr_main(): pl.pallas_call(mr_main_kernel, grid=(width // cols,), in_specs=[pl.BlockS...  8.04 us
    pallas_call x1, Pallas kernels, se_mixer(): pl.pallas_call(se_kernel, grid=(width // cols,), in_specs=[pl.BlockSpec((...  6.94 us
    pallas_call x4, Pallas kernels, cross_attention(): pl.pallas_call(functools.partial(cross_kernel, has_ahead, done is not Non...  4.26 us
    pallas_call x1, Pallas kernels, local_attention(): pl.pallas_call(local_kernel, grid_spec=pltpu.PrefetchScalarGridSpec(num_s...  4.04 us
    pallas_call x2, Pallas kernels, pack(): pl.pallas_call(functools.partial(pack_kernel, lows, asks, part), in_specs...  3.78 us
  transfers between devices with their start and end apart: 19, of which 6 were waited for; matrix products, arithmetic and copies ran while one was open for 0% of the time, Pallas kernels for 31%

profile of v2, /device:TPU:26, one launch (start us, length us, event | category | flops | bytes accessed | tf_op | source)
XLA Modules:
  0.0 113.2 jit_solution(9663427125428003564)
XLA Ops:
  0.6 1.7 %raw_tail.1 = bf16[32,2048]{1,0:T(8,128)(2,1)} custom-call(bf16[3,320,2048]{2,1,0:T(8,128)(2,1)} %qkv_ref.2, bf16[3,320,2048]{2,1,0:T(8,128)(2,1)} %query_ref.1), custom_call_target="tpu_custom_call" | custom-call | flops 1 | bytes 1 | tf_op jit(solution)/shard_map/raw_tail/pallas_call | solution.py:463
  2.3 1.3 %collective-permute-start = (bf16[32,2048]{1,0:T(8,128)(2,1)}, bf16[32,2048]{1,0:T(8,128)(2,1)S(1)}, u32[]{:S(2)}, u32[]{:S(2)}) collective-permute-start(bf16[32,2048]{1,0:T(8,128)(2,1)} %raw_tail.1), channel_id=1, source_target_pairs={{0,4},{4,8},{8,12},{1,5},{5,9},{9,13},{2,6},{6,10},{10,14},{3,7},{... | collective-permute-start | bytes 393224 | tf_op jit(solution)/shard_map/ppermute | solution.py:745
  3.6 1.8 %pack.2 = (bf16[2,320,512]{2,1,0:T(8,128)(2,1)}, bf16[4,336,128]{2,1,0:T(8,128)(2,1)}) custom-call(s32[1]{0:T(128)} %bitcast.idx_ref, bf16[3,320,2048]{2,1,0:T(8,128)(2,1)} %v_ref.9), custom_call_target="tpu_custom_call" | custom-call | flops 1 | bytes 1 | tf_op jit(solution)/shard_map/pack/pallas_call | solution.py:502
  5.4 4.2 %collective-permute-done.tail_ref = bf16[32,2048]{1,0:T(8,128)(2,1)S(1)} collective-permute-done((bf16[32,2048]{1,0:T(8,128)(2,1)}, bf16[32,2048]{1,0:T(8,128)(2,1)S(1)}, u32[]{:S(2)}, u32[]{:S(2)}) %collective-permute-start) | collective-permute-done | bytes 131104 | tf_op jit(solution)/shard_map/ppermute | solution.py:745
  9.7 3.0 %product_tail.1 = bf16[128,2048]{1,0:T(8,128)(2,1)} custom-call(bf16[3,320,2048]{2,1,0:T(8,128)(2,1)} %query_ref.1, bf16[3,320,2048]{2,1,0:T(8,128)(2,1)} %query_ref.1, f32[3,3,2048]{2,1,0:T(4,128)} %short_ref.7), custom_call_target="tpu_custom_call" | custom-call | flops 1 | bytes 1 | tf_op jit(solution)/shard_map/product_tail/pallas_call | solution.py:479
  12.7 2.0 %pack.3 = (bf16[2,320,512]{2,1,0:T(8,128)(2,1)}, bf16[2,320,512]{2,1,0:T(8,128)(2,1)}, bf16[2,320,512]{2,1,0:T(8,128)(2,1)}, bf16[4,336,128]{2,1,0:T(8,128)(2,1)}) custom-call(s32[1]{0:T(128)} %bitcast.idx_ref, bf16[3,320,2048]{2,1,0:T(8,128)(2,1)} %v_ref.9), custom_call_target="tpu_custom_call" | custom-call | flops 1 | bytes 1 | tf_op jit(solution)/shard_map/pack/pallas_call | solution.py:502
  15.4 2.4 %collective-permute-start.4 = (bf16[4,336,128]{2,1,0:T(8,128)(2,1)}, bf16[4,336,128]{2,1,0:T(8,128)(2,1)S(1)}, u32[]{:S(2)}, u32[]{:S(2)}) collective-permute-start(bf16[4,336,128]{2,1,0:T(8,128)(2,1)} %get-tuple-element.53), channel_id=1, source_target_pairs={{8,4},{12,8},{9,5},{13,9},{10,6},{14,10},{11,7},{15,11},{24,20},{2... | collective-permute-start | bytes 1032200 | tf_op jit(solution)/shard_map/ppermute | solution.py:745
  17.8 1.3 %collective-permute-start.3 = (bf16[4,336,128]{2,1,0:T(8,128)(2,1)}, bf16[4,336,128]{2,1,0:T(8,128)(2,1)S(1)}, u32[]{:S(2)}, u32[]{:S(2)}) collective-permute-start(bf16[4,336,128]{2,1,0:T(8,128)(2,1)} %get-tuple-element.53), channel_id=1, source_target_pairs={{12,4},{13,5},{14,6},{15,7},{28,20},{29,21},{30,22},{31,23}} | collective-permute-start | bytes 1032200 | tf_op jit(solution)/shard_map/ppermute | solution.py:745
  19.8 1.3 %collective-permute-start.8 = (bf16[128,2048]{1,0:T(8,128)(2,1)}, bf16[128,2048]{1,0:T(8,128)(2,1)S(1)}, u32[]{:S(2)}, u32[]{:S(2)}) collective-permute-start(bf16[128,2048]{1,0:T(8,128)(2,1)} %product_tail.1), channel_id=1, source_target_pairs={{4,8},{8,12},{5,9},{9,13},{6,10},{10,14},{7,11},{11,15},{20,24},{2... | collective-permute-start | bytes 1572872 | tf_op jit(solution)/shard_map/ppermute | solution.py:745
  22.0 6.9 %se_mixer.1 = bf16[320,2048]{1,0:T(8,128)(2,1)} custom-call(bf16[3,320,2048]{2,1,0:T(8,128)(2,1)S(1)} %copy-done.2, bf16[32,2048]{1,0:T(8,128)(2,1)S(1)} %collective-permute-done.tail_ref, f32[3,3,2048]{2,1,0:T(4,128)S(1)} %copy-done.7, f32[7,2048]{1,0:T(8,128)S(1)} %copy-done.8), custom_call_target="tpu_custom_call" | custom-call | flops 1 | bytes 1 | tf_op jit(solution)/shard_map/se_mixer/pallas_call | solution.py:436
  29.0 2.9 %collective-permute-done.3.refs_2_ = bf16[4,336,128]{2,1,0:T(8,128)(2,1)S(1)} collective-permute-done((bf16[4,336,128]{2,1,0:T(8,128)(2,1)}, bf16[4,336,128]{2,1,0:T(8,128)(2,1)S(1)}, u32[]{:S(2)}, u32[]{:S(2)}) %collective-permute-start.3) | collective-permute-done | bytes 344096 | tf_op jit(solution)/shard_map/ppermute | solution.py:745
  31.9 5.2 %collective-permute-start.6 = (bf16[4,336,128]{2,1,0:T(8,128)(2,1)S(1)}, bf16[4,336,128]{2,1,0:T(8,128)(2,1)S(1)}, u32[]{:S(2)}, u32[]{:S(2)}) collective-permute-start(bf16[4,336,128]{2,1,0:T(8,128)(2,1)S(1)} %copy-done.13), channel_id=1, source_target_pairs={{12,4},{13,5},{14,6},{15,7},{28,20},{29,21},{30,22},{31,23}} | collective-permute-start | bytes 1032200 | tf_op jit(solution)/shard_map/ppermute | solution.py:745
  37.1 1.3 %collective-permute-start.5 = (bf16[4,336,128]{2,1,0:T(8,128)(2,1)S(1)}, bf16[4,336,128]{2,1,0:T(8,128)(2,1)S(1)}, u32[]{:S(2)}, u32[]{:S(2)}) collective-permute-start(bf16[4,336,128]{2,1,0:T(8,128)(2,1)S(1)} %copy-done.13), channel_id=1, source_target_pairs={{8,4},{12,8},{9,5},{13,9},{10,6},{14,10},{11,7},{15,11},{24,20},{2... | collective-permute-start | bytes 1032200 | tf_op jit(solution)/shard_map/ppermute | solution.py:745
  39.2 4.0 %local_attention.1 = (f32[16,320,128]{2,1,0:T(8,128)S(1)}, f32[16,8,384]{2,1,0:T(8,128)S(1)}) custom-call(s32[1]{0:T(128)} %bitcast.idx_ref, bf16[3,320,2048]{2,1,0:T(8,128)(2,1)S(1)} %copy-done, bf16[3,320,2048]{2,1,0:T(8,128)(2,1)S(1)} %copy-done, bf16[3,320,2048]{2,1,0:T(8,128)(2,1)S(1)} %copy-done), custom_call_target="tpu_custom_call" | custom-call | flops 1 | bytes 1 | tf_op jit(solution)/shard_map/local_attention/pallas_call | solution.py:604
  44.4 9.6 %collective-permute-start.11 = (bf16[4,336,128]{2,1,0:T(8,128)(2,1)S(1)}, bf16[4,336,128]{2,1,0:T(8,128)(2,1)S(1)}, u32[]{:S(2)}, u32[]{:S(2)}) collective-permute-start(bf16[4,336,128]{2,1,0:T(8,128)(2,1)S(1)} %get-tuple-element.62), channel_id=1, source_target_pairs={{12,4},{4,8},{8,12},{13,5},{5,9},{9,13},{14,6},{6,10},{10,14},{15,... | collective-permute-start | bytes 1032200 | tf_op jit(solution)/shard_map/ppermute | solution.py:745
  54.7 1.9 %collective-permute-start.14 = (bf16[4,336,128]{2,1,0:T(8,128)(2,1)S(1)}, bf16[4,336,128]{2,1,0:T(8,128)(2,1)S(1)}, u32[]{:S(2)}, u32[]{:S(2)}) collective-permute-start(bf16[4,336,128]{2,1,0:T(8,128)(2,1)S(1)} %get-tuple-element.66), channel_id=1, source_target_pairs={{4,12},{8,4},{12,8},{5,13},{9,5},{13,9},{6,14},{10,6},{14,10},{7,1... | collective-permute-start | bytes 1032200 | tf_op jit(solution)/shard_map/ppermute | solution.py:745
  57.8 8.5 %collective-permute-start.13 = (bf16[4,336,128]{2,1,0:T(8,128)(2,1)S(1)}, bf16[4,336,128]{2,1,0:T(8,128)(2,1)S(1)}, u32[]{:S(2)}, u32[]{:S(2)}) collective-permute-start(bf16[4,336,128]{2,1,0:T(8,128)(2,1)S(1)} %get-tuple-element.59), channel_id=1, source_target_pairs={{12,4},{4,8},{8,12},{13,5},{5,9},{9,13},{14,6},{6,10},{10,14},{15,... | collective-permute-start | bytes 1032200 | tf_op jit(solution)/shard_map/ppermute | solution.py:745
  66.3 1.9 %collective-permute-start.12 = (bf16[4,336,128]{2,1,0:T(8,128)(2,1)S(1)}, bf16[4,336,128]{2,1,0:T(8,128)(2,1)S(1)}, u32[]{:S(2)}, u32[]{:S(2)}) collective-permute-start(bf16[4,336,128]{2,1,0:T(8,128)(2,1)S(1)} %get-tuple-element.65), channel_id=1, source_target_pairs={{4,12},{8,4},{12,8},{5,13},{9,5},{13,9},{6,14},{10,6},{14,10},{7,1... | collective-permute-start | bytes 1032200 | tf_op jit(solution)/shard_map/ppermute | solution.py:745
  70.0 5.9 %collective-permute-done.13.refs_1_.up_ref = bf16[4,336,128]{2,1,0:T(8,128)(2,1)S(1)} collective-permute-done((bf16[4,336,128]{2,1,0:T(8,128)(2,1)S(1)}, bf16[4,336,128]{2,1,0:T(8,128)(2,1)S(1)}, u32[]{:S(2)}, u32[]{:S(2)}) %collective-permute-start.13) | collective-permute-done | bytes 344096 | tf_op jit(solution)/shard_map/ppermute | solution.py:745
  75.8 1.3 %collective-permute-start.18 = (bf16[4,336,128]{2,1,0:T(8,128)(2,1)S(1)}, bf16[4,336,128]{2,1,0:T(8,128)(2,1)S(1)}, u32[]{:S(2)}, u32[]{:S(2)}) collective-permute-start(bf16[4,336,128]{2,1,0:T(8,128)(2,1)S(1)} %get-tuple-element.82), channel_id=1, source_target_pairs={{4,12},{5,13},{6,14},{7,15},{20,28},{21,29},{22,30},{23,31}} | collective-permute-start | bytes 1032200 | tf_op jit(solution)/shard_map/ppermute | solution.py:745
  77.1 1.5 %collective-permute-start.17 = (bf16[4,336,128]{2,1,0:T(8,128)(2,1)S(1)}, bf16[4,336,128]{2,1,0:T(8,128)(2,1)S(1)}, u32[]{:S(2)}, u32[]{:S(2)}) collective-permute-start(bf16[4,336,128]{2,1,0:T(8,128)(2,1)S(1)} %get-tuple-element.80), channel_id=1, source_target_pairs={{4,8},{8,12},{5,9},{9,13},{6,10},{10,14},{7,11},{11,15},{20,24},{2... | collective-permute-start | bytes 1032200 | tf_op jit(solution)/shard_map/ppermute | solution.py:745
  78.6 2.7 %collective-permute-done.12.refs_0_.far_ref = bf16[4,336,128]{2,1,0:T(8,128)(2,1)S(1)} collective-permute-done((bf16[4,336,128]{2,1,0:T(8,128)(2,1)S(1)}, bf16[4,336,128]{2,1,0:T(8,128)(2,1)S(1)}, u32[]{:S(2)}, u32[]{:S(2)}) %collective-permute-start.12) | collective-permute-done | bytes 344096 | tf_op jit(solution)/shard_map/ppermute | solution.py:745
  82.4 1.4 %collective-permute-start.15 = (bf16[4,336,128]{2,1,0:T(8,128)(2,1)S(1)}, bf16[4,336,128]{2,1,0:T(8,128)(2,1)S(1)}, u32[]{:S(2)}, u32[]{:S(2)}) collective-permute-start(bf16[4,336,128]{2,1,0:T(8,128)(2,1)S(1)} %get-tuple-element.77), channel_id=1, source_target_pairs={{4,8},{8,12},{5,9},{9,13},{6,10},{10,14},{7,11},{11,15},{20,24},{2... | collective-permute-start | bytes 1032200 | tf_op jit(solution)/shard_map/ppermute | solution.py:745
  83.8 1.3 %collective-permute-start.16 = (bf16[4,336,128]{2,1,0:T(8,128)(2,1)S(1)}, bf16[4,336,128]{2,1,0:T(8,128)(2,1)S(1)}, u32[]{:S(2)}, u32[]{:S(2)}) collective-permute-start(bf16[4,336,128]{2,1,0:T(8,128)(2,1)S(1)} %get-tuple-element.78), channel_id=1, source_target_pairs={{4,12},{5,13},{6,14},{7,15},{20,28},{21,29},{22,30},{23,31}} | collective-permute-start | bytes 1032200 | tf_op jit(solution)/shard_map/ppermute | solution.py:745
  85.1 8.0 %mr_main.1 = (bf16[320,2048]{1,0:T(8,128)(2,1)}, f32[256,2048]{1,0:T(8,128)S(1)}, bf16[128,2048]{1,0:T(8,128)(2,1)S(1)}) custom-call(bf16[3,320,2048]{2,1,0:T(8,128)(2,1)S(1)} %copy-done.1, bf16[32,2048]{1,0:T(8,128)(2,1)S(1)} %collective-permute-done.tail_ref, f32[3,3,2048]{2,1,0:T(4,128)S(1)} %copy-done.5, f32[128,2048]{1,0:T(8,128)S(1)} %copy-done.4, ...), custom_call_target="tpu_custom_call" | custom-call | flops 1 | bytes 1 | tf_op jit(solution)/shard_map/mr_main/pallas_call | solution.py:524
  93.2 2.3 %merge_attention.4.own_ref = bf16[320,2048]{1,0:T(8,128)(2,1)} custom-call(s32[1]{0:T(128)} %bitcast.idx_ref, f32[16,320,128]{2,1,0:T(8,128)S(1)} %get-tuple-element.79.loc_ref, f32[16,8,384]{2,1,0:T(8,128)S(1)} %get-tuple-element.56.stat_ref, bf16[4,336,128]{2,1,0:T(8,128)(2,1)S(1)} %collective-permute-done.11.refs_1_.up_ref, ...), custom_call_target="tpu_custom_call", output_to_operand_aliasing={{}: (5, {})} | custom-call | flops 1 | bytes 1 | tf_op jit(solution)/shard_map/merge_attention/pallas_call | solution.py:668
  95.5 2.3 %merge_attention.5.own_ref = bf16[320,2048]{1,0:T(8,128)(2,1)} custom-call(s32[1]{0:T(128)} %bitcast.idx_ref, f32[16,320,128]{2,1,0:T(8,128)S(1)} %get-tuple-element.79.loc_ref, f32[16,8,384]{2,1,0:T(8,128)S(1)} %get-tuple-element.56.stat_ref, bf16[4,336,128]{2,1,0:T(8,128)(2,1)S(1)} %collective-permute-done.13.refs_1_.up_ref, ...), custom_call_target="tpu_custom_call", output_to_operand_aliasing={{}: (5, {})} | custom-call | flops 1 | bytes 1 | tf_op jit(solution)/shard_map/merge_attention/pallas_call | solution.py:668
  97.7 2.3 %merge_attention.6.own_ref = bf16[320,2048]{1,0:T(8,128)(2,1)} custom-call(s32[1]{0:T(128)} %bitcast.idx_ref, f32[16,320,128]{2,1,0:T(8,128)S(1)} %get-tuple-element.79.loc_ref, f32[16,8,384]{2,1,0:T(8,128)S(1)} %get-tuple-element.56.stat_ref, bf16[4,336,128]{2,1,0:T(8,128)(2,1)S(1)} %collective-permute-done.17.up_ref, ...), custom_call_target="tpu_custom_call", output_to_operand_aliasing={{}: (5, {})} | custom-call | flops 1 | bytes 1 | tf_op jit(solution)/shard_map/merge_attention/pallas_call | solution.py:668
  100.0 3.6 %mr_head.1 = bf16[320,2048]{1,0:T(8,128)(2,1)} custom-call(s32[1]{0:T(128)} %bitcast.idx_ref, bf16[128,2048]{1,0:T(8,128)(2,1)S(1)} %collective-permute-done.9.low_ref, bf16[128,2048]{1,0:T(8,128)(2,1)S(1)} %collective-permute-done.8.high_ref, bf16[128,2048]{1,0:T(8,128)(2,1)S(1)} %get-tuple-element.71.lead_ref, ...), custom_call_target="tpu_custom_call", output_to_operand_aliasing={{}: (10, {})} | custom-call | flops 1 | bytes 1 | tf_op jit(solution)/shard_map/mr_head/pallas_call | solution.py:557
  103.6 3.6 %collective-permute-done.15.up_ref = bf16[4,336,128]{2,1,0:T(8,128)(2,1)S(1)} collective-permute-done((bf16[4,336,128]{2,1,0:T(8,128)(2,1)S(1)}, bf16[4,336,128]{2,1,0:T(8,128)(2,1)S(1)}, u32[]{:S(2)}, u32[]{:S(2)}) %collective-permute-start.15) | collective-permute-done | bytes 344096 | tf_op jit(solution)/shard_map/ppermute | solution.py:745
  107.2 3.7 %collective-permute-done.16.far_ref = bf16[4,336,128]{2,1,0:T(8,128)(2,1)S(1)} collective-permute-done((bf16[4,336,128]{2,1,0:T(8,128)(2,1)S(1)}, bf16[4,336,128]{2,1,0:T(8,128)(2,1)S(1)}, u32[]{:S(2)}, u32[]{:S(2)}) %collective-permute-start.16) | collective-permute-done | bytes 344096 | tf_op jit(solution)/shard_map/ppermute | solution.py:745
  110.9 2.3 %merge_attention.7 = bf16[320,2048]{1,0:T(8,128)(2,1)} custom-call(s32[1]{0:T(128)} %bitcast.idx_ref, f32[16,320,128]{2,1,0:T(8,128)S(1)} %get-tuple-element.79.loc_ref, f32[16,8,384]{2,1,0:T(8,128)S(1)} %get-tuple-element.56.stat_ref, bf16[4,336,128]{2,1,0:T(8,128)(2,1)S(1)} %collective-permute-done.15.up_ref, ...), custom_call_target="tpu_custom_call", output_to_operand_aliasing={{}: (5, {})} | custom-call | flops 1 | bytes 1 | tf_op jit(solution)/shard_map/merge_attention/pallas_call | solution.py:668
  (50 shorter events, 8.7 us)
Async XLA Ops:
  2.3 7.3 %collective-permute-start = (bf16[32,2048]{1,0:T(8,128)(2,1)}, bf16[32,2048]{1,0:T(8,128)(2,1)S(1)}, u32[]{:S(2)}, u32[]{:S(2)}) collective-permute-start(bf16[32,2048]{1,0:T(8,128)(2,1)} %raw_tail.1), channel_id=1, source_target_pairs={{0,4},{4,8},{8,12},{1,5},{5,9},{9,13},{2,6},{6,10},{10,14},{3,7},{... | collective-permute-start | bytes 393224 | tf_op jit(solution)/shard_map/ppermute | solution.py:745
  9.7 11.5 %copy-start.8 = (f32[7,2048]{1,0:T(8,128)S(1)}, f32[7,2048]{1,0:T(8,128)}, u32[]{:S(2)}) copy-start(f32[7,2048]{1,0:T(8,128)} %filt_ref.2) | copy-start | bytes 172036
  12.7 8.4 %copy-start.2 = (bf16[3,320,2048]{2,1,0:T(8,128)(2,1)S(1)}, bf16[3,320,2048]{2,1,0:T(8,128)(2,1)}, u32[]{:S(2)}) copy-start(bf16[3,320,2048]{2,1,0:T(8,128)(2,1)} %qkv_ref.2) | copy-start | bytes 11796484
  14.7 23.7 %collective-permute-start.1 = (bf16[2,320,512]{2,1,0:T(8,128)(2,1)}, bf16[2,320,512]{2,1,0:T(8,128)(2,1)S(1)}, u32[]{:S(2)}, u32[]{:S(2)}) collective-permute-start(bf16[2,320,512]{2,1,0:T(8,128)(2,1)} %get-tuple-element.50), channel_id=1, source_target_pairs={{0,4},{1,5},{2,6},{3,7},{16,20},{17,21},{18,22},{19,23}} | collective-permute-start | bytes 1966088 | tf_op jit(solution)/shard_map/ppermute | solution.py:745
  15.4 13.6 %collective-permute-start.4 = (bf16[4,336,128]{2,1,0:T(8,128)(2,1)}, bf16[4,336,128]{2,1,0:T(8,128)(2,1)S(1)}, u32[]{:S(2)}, u32[]{:S(2)}) collective-permute-start(bf16[4,336,128]{2,1,0:T(8,128)(2,1)} %get-tuple-element.53), channel_id=1, source_target_pairs={{8,4},{12,8},{9,5},{13,9},{10,6},{14,10},{11,7},{15,11},{24,20},{2... | collective-permute-start | bytes 1032200 | tf_op jit(solution)/shard_map/ppermute | solution.py:745
  17.8 14.1 %collective-permute-start.3 = (bf16[4,336,128]{2,1,0:T(8,128)(2,1)}, bf16[4,336,128]{2,1,0:T(8,128)(2,1)S(1)}, u32[]{:S(2)}, u32[]{:S(2)}) collective-permute-start(bf16[4,336,128]{2,1,0:T(8,128)(2,1)} %get-tuple-element.53), channel_id=1, source_target_pairs={{12,4},{13,5},{14,6},{15,7},{28,20},{29,21},{30,22},{31,23}} | collective-permute-start | bytes 1032200 | tf_op jit(solution)/shard_map/ppermute | solution.py:745
  19.1 24.1 %collective-permute-start.7 = (bf16[2,320,512]{2,1,0:T(8,128)(2,1)}, bf16[2,320,512]{2,1,0:T(8,128)(2,1)S(1)}, u32[]{:S(2)}, u32[]{:S(2)}) collective-permute-start(bf16[2,320,512]{2,1,0:T(8,128)(2,1)} %get-tuple-element.44), channel_id=1, source_target_pairs={{0,4},{1,5},{2,6},{3,7},{16,20},{17,21},{18,22},{19,23}} | collective-permute-start | bytes 1966088 | tf_op jit(solution)/shard_map/ppermute | solution.py:745
  19.8 23.4 %collective-permute-start.8 = (bf16[128,2048]{1,0:T(8,128)(2,1)}, bf16[128,2048]{1,0:T(8,128)(2,1)S(1)}, u32[]{:S(2)}, u32[]{:S(2)}) collective-permute-start(bf16[128,2048]{1,0:T(8,128)(2,1)} %product_tail.1), channel_id=1, source_target_pairs={{4,8},{8,12},{5,9},{9,13},{6,10},{10,14},{7,11},{11,15},{20,24},{2... | collective-permute-start | bytes 1572872 | tf_op jit(solution)/shard_map/ppermute | solution.py:745
  22.0 9.9 %copy-start.13 = (bf16[4,336,128]{2,1,0:T(8,128)(2,1)S(1)}, bf16[4,336,128]{2,1,0:T(8,128)(2,1)}, u32[]{:S(2)}) copy-start(bf16[4,336,128]{2,1,0:T(8,128)(2,1)} %get-tuple-element.54) | copy-start | bytes 1032196
  22.0 16.4 %copy-start.12 = (bf16[2,320,512]{2,1,0:T(8,128)(2,1)S(1)}, bf16[2,320,512]{2,1,0:T(8,128)(2,1)}, u32[]{:S(2)}) copy-start(bf16[2,320,512]{2,1,0:T(8,128)(2,1)} %get-tuple-element.51) | copy-start | bytes 1966084
  22.0 17.1 %copy-start = (bf16[3,320,2048]{2,1,0:T(8,128)(2,1)S(1)}, bf16[3,320,2048]{2,1,0:T(8,128)(2,1)}, u32[]{:S(2)}) copy-start(bf16[3,320,2048]{2,1,0:T(8,128)(2,1)} %v_ref.9) | copy-start | bytes 11796484
  31.9 22.1 %collective-permute-start.6 = (bf16[4,336,128]{2,1,0:T(8,128)(2,1)S(1)}, bf16[4,336,128]{2,1,0:T(8,128)(2,1)S(1)}, u32[]{:S(2)}, u32[]{:S(2)}) collective-permute-start(bf16[4,336,128]{2,1,0:T(8,128)(2,1)S(1)} %copy-done.13), channel_id=1, source_target_pairs={{12,4},{13,5},{14,6},{15,7},{28,20},{29,21},{30,22},{31,23}} | collective-permute-start | bytes 1032200 | tf_op jit(solution)/shard_map/ppermute | solution.py:745
  37.1 16.9 %collective-permute-start.5 = (bf16[4,336,128]{2,1,0:T(8,128)(2,1)S(1)}, bf16[4,336,128]{2,1,0:T(8,128)(2,1)S(1)}, u32[]{:S(2)}, u32[]{:S(2)}) collective-permute-start(bf16[4,336,128]{2,1,0:T(8,128)(2,1)S(1)} %copy-done.13), channel_id=1, source_target_pairs={{8,4},{12,8},{9,5},{13,9},{10,6},{14,10},{11,7},{15,11},{24,20},{2... | collective-permute-start | bytes 1032200 | tf_op jit(solution)/shard_map/ppermute | solution.py:745
  38.4 29.8 %collective-permute-start.2 = (bf16[2,320,512]{2,1,0:T(8,128)(2,1)S(1)}, bf16[2,320,512]{2,1,0:T(8,128)(2,1)S(1)}, u32[]{:S(2)}, u32[]{:S(2)}) collective-permute-start(bf16[2,320,512]{2,1,0:T(8,128)(2,1)S(1)} %copy-done.12), channel_id=1, source_target_pairs={{0,4},{1,5},{2,6},{3,7},{16,20},{17,21},{18,22},{19,23}} | collective-permute-start | bytes 1966088 | tf_op jit(solution)/shard_map/ppermute | solution.py:745
  43.2 10.8 %copy-start.11 = (bf16[2,320,512]{2,1,0:T(8,128)(2,1)S(1)}, bf16[2,320,512]{2,1,0:T(8,128)(2,1)}, u32[]{:S(2)}) copy-start(bf16[2,320,512]{2,1,0:T(8,128)(2,1)} %get-tuple-element.63) | copy-start | bytes 1966084
  44.4 21.9 %collective-permute-start.11 = (bf16[4,336,128]{2,1,0:T(8,128)(2,1)S(1)}, bf16[4,336,128]{2,1,0:T(8,128)(2,1)S(1)}, u32[]{:S(2)}, u32[]{:S(2)}) collective-permute-start(bf16[4,336,128]{2,1,0:T(8,128)(2,1)S(1)} %get-tuple-element.62), channel_id=1, source_target_pairs={{12,4},{4,8},{8,12},{13,5},{5,9},{9,13},{14,6},{6,10},{10,14},{15,... | collective-permute-start | bytes 1032200 | tf_op jit(solution)/shard_map/ppermute | solution.py:745
  54.0 24.6 %collective-permute-start.10 = (bf16[2,320,512]{2,1,0:T(8,128)(2,1)S(1)}, bf16[2,320,512]{2,1,0:T(8,128)(2,1)S(1)}, u32[]{:S(2)}, u32[]{:S(2)}) collective-permute-start(bf16[2,320,512]{2,1,0:T(8,128)(2,1)S(1)} %copy-done.11), channel_id=1, source_target_pairs={{0,4},{1,5},{2,6},{3,7},{16,20},{17,21},{18,22},{19,23}} | collective-permute-start | bytes 1966088 | tf_op jit(solution)/shard_map/ppermute | solution.py:745
  54.7 14.3 %collective-permute-start.14 = (bf16[4,336,128]{2,1,0:T(8,128)(2,1)S(1)}, bf16[4,336,128]{2,1,0:T(8,128)(2,1)S(1)}, u32[]{:S(2)}, u32[]{:S(2)}) collective-permute-start(bf16[4,336,128]{2,1,0:T(8,128)(2,1)S(1)} %get-tuple-element.66), channel_id=1, source_target_pairs={{4,12},{8,4},{12,8},{5,13},{9,5},{13,9},{6,14},{10,6},{14,10},{7,1... | collective-permute-start | bytes 1032200 | tf_op jit(solution)/shard_map/ppermute | solution.py:745
  56.6 11.6 %copy-start.10 = (bf16[128,2048]{1,0:T(8,128)(2,1)S(1)}, bf16[128,2048]{1,0:T(8,128)(2,1)}, u32[]{:S(2)}) copy-start(bf16[128,2048]{1,0:T(8,128)(2,1)} %product_tail.1) | copy-start | bytes 1572868
  57.8 18.0 %collective-permute-start.13 = (bf16[4,336,128]{2,1,0:T(8,128)(2,1)S(1)}, bf16[4,336,128]{2,1,0:T(8,128)(2,1)S(1)}, u32[]{:S(2)}, u32[]{:S(2)}) collective-permute-start(bf16[4,336,128]{2,1,0:T(8,128)(2,1)S(1)} %get-tuple-element.59), channel_id=1, source_target_pairs={{12,4},{4,8},{8,12},{13,5},{5,9},{9,13},{14,6},{6,10},{10,14},{15,... | collective-permute-start | bytes 1032200 | tf_op jit(solution)/shard_map/ppermute | solution.py:745
  66.3 15.0 %collective-permute-start.12 = (bf16[4,336,128]{2,1,0:T(8,128)(2,1)S(1)}, bf16[4,336,128]{2,1,0:T(8,128)(2,1)S(1)}, u32[]{:S(2)}, u32[]{:S(2)}) collective-permute-start(bf16[4,336,128]{2,1,0:T(8,128)(2,1)S(1)} %get-tuple-element.65), channel_id=1, source_target_pairs={{4,12},{8,4},{12,8},{5,13},{9,5},{13,9},{6,14},{10,6},{14,10},{7,1... | collective-permute-start | bytes 1032200 | tf_op jit(solution)/shard_map/ppermute | solution.py:745
  68.3 31.7 %collective-permute-start.9 = (bf16[128,2048]{1,0:T(8,128)(2,1)S(1)}, bf16[128,2048]{1,0:T(8,128)(2,1)S(1)}, u32[]{:S(2)}, u32[]{:S(2)}) collective-permute-start(bf16[128,2048]{1,0:T(8,128)(2,1)S(1)} %copy-done.10), channel_id=1, source_target_pairs={{0,4},{1,5},{2,6},{3,7},{16,20},{17,21},{18,22},{19,23}} | collective-permute-start | bytes 1572872 | tf_op jit(solution)/shard_map/ppermute | solution.py:745
  75.8 21.9 %collective-permute-start.18 = (bf16[4,336,128]{2,1,0:T(8,128)(2,1)S(1)}, bf16[4,336,128]{2,1,0:T(8,128)(2,1)S(1)}, u32[]{:S(2)}, u32[]{:S(2)}) collective-permute-start(bf16[4,336,128]{2,1,0:T(8,128)(2,1)S(1)} %get-tuple-element.82), channel_id=1, source_target_pairs={{4,12},{5,13},{6,14},{7,15},{20,28},{21,29},{22,30},{23,31}} | collective-permute-start | bytes 1032200 | tf_op jit(solution)/shard_map/ppermute | solution.py:745
  77.1 20.6 %collective-permute-start.17 = (bf16[4,336,128]{2,1,0:T(8,128)(2,1)S(1)}, bf16[4,336,128]{2,1,0:T(8,128)(2,1)S(1)}, u32[]{:S(2)}, u32[]{:S(2)}) collective-permute-start(bf16[4,336,128]{2,1,0:T(8,128)(2,1)S(1)} %get-tuple-element.80), channel_id=1, source_target_pairs={{4,8},{8,12},{5,9},{9,13},{6,10},{10,14},{7,11},{11,15},{20,24},{2... | collective-permute-start | bytes 1032200 | tf_op jit(solution)/shard_map/ppermute | solution.py:745
  81.3 3.7 %copy-start.1 = (bf16[3,320,2048]{2,1,0:T(8,128)(2,1)S(1)}, bf16[3,320,2048]{2,1,0:T(8,128)(2,1)}, u32[]{:S(2)}) copy-start(bf16[3,320,2048]{2,1,0:T(8,128)(2,1)} %query_ref.1) | copy-start | bytes 11796484
  81.3 3.8 %copy-start.3 = (bf16[512,256]{1,0:T(8,128)(2,1)S(1)}, bf16[512,256]{1,0:T(8,128)(2,1)}, u32[]{:S(2)}) copy-start(bf16[512,256]{1,0:T(8,128)(2,1)} %constant.9.clone.fwd_ref) | copy-start | bytes 786436
  81.3 3.8 %copy-start.4 = (f32[128,2048]{1,0:T(8,128)S(1)}, f32[128,2048]{1,0:T(8,128)}, u32[]{:S(2)}) copy-start(f32[128,2048]{1,0:T(8,128)} %filt_ref.3) | copy-start | bytes 3145732
  81.3 3.8 %copy-start.5 = (f32[3,3,2048]{2,1,0:T(4,128)S(1)}, f32[3,3,2048]{2,1,0:T(4,128)}, u32[]{:S(2)}) copy-start(f32[3,3,2048]{2,1,0:T(4,128)} %short_ref.7) | copy-start | bytes 221188
  81.3 3.8 %copy-start.6 = (bf16[256,256]{1,0:T(8,128)(2,1)S(1)}, bf16[256,256]{1,0:T(8,128)(2,1)}, u32[]{:S(2)}) copy-start(bf16[256,256]{1,0:T(8,128)(2,1)} %constant.10.clone.inv_ref) | copy-start | bytes 393220
  81.4 3.8 %copy-start.9 = (f32[2048]{0:T(1024)S(1)}, f32[2048]{0:T(1024)}, u32[]{:S(2)}) copy-start(f32[2048]{0:T(1024)} %param.16) | copy-start | bytes 24580
  82.4 24.8 %collective-permute-start.15 = (bf16[4,336,128]{2,1,0:T(8,128)(2,1)S(1)}, bf16[4,336,128]{2,1,0:T(8,128)(2,1)S(1)}, u32[]{:S(2)}, u32[]{:S(2)}) collective-permute-start(bf16[4,336,128]{2,1,0:T(8,128)(2,1)S(1)} %get-tuple-element.77), channel_id=1, source_target_pairs={{4,8},{8,12},{5,9},{9,13},{6,10},{10,14},{7,11},{11,15},{20,24},{2... | collective-permute-start | bytes 1032200 | tf_op jit(solution)/shard_map/ppermute | solution.py:745
  83.8 27.1 %collective-permute-start.16 = (bf16[4,336,128]{2,1,0:T(8,128)(2,1)S(1)}, bf16[4,336,128]{2,1,0:T(8,128)(2,1)S(1)}, u32[]{:S(2)}, u32[]{:S(2)}) collective-permute-start(bf16[4,336,128]{2,1,0:T(8,128)(2,1)S(1)} %get-tuple-element.78), channel_id=1, source_target_pairs={{4,12},{5,13},{6,14},{7,15},{20,28},{21,29},{22,30},{23,31}} | collective-permute-start | bytes 1032200 | tf_op jit(solution)/shard_map/ppermute | solution.py:745
  (1 other events, 0.9 us)

commit v3 on v2

--- a/solution.py
+++ b/solution.py
@@ -224,28 +224,31 @@
     return jnp.concatenate([value, jnp.zeros((extra, value.shape[1]), value.dtype)], axis=0)
 
 
-def stat_block(stat):
+def put_payload(ref, mixes, stats, rows):
+    for j, mixed in enumerate(mixes):
+        ref[0, j * rows : (j + 1) * rows] = mixed[:rows].astype(BF16)
+    total = len(mixes) * rows
+    extra = padded(total) - total
+    parts = [s[:, :rows] for s in stats] + ([jnp.zeros((1, extra), F32)] if extra else [])
+    stat = jnp.concatenate(parts, axis=1)
     high = stat.astype(BF16).astype(F32)
     mid = (stat - high).astype(BF16).astype(F32)
     low = (stat - high - mid).astype(BF16).astype(F32)
-    lanes = stat.shape[1] // 128
-    parts = [p[:, j * 128 : (j + 1) * 128] for p in (high, mid, low) for j in range(lanes)]
-    parts.append(jnp.zeros((STAT_ROWS - len(parts), 128), F32))
-    return jnp.concatenate(parts, axis=0).astype(BF16)
-
-
-def stat_of(block, lanes):
-    wide = block.astype(F32)
-    total = wide[0:lanes] + wide[lanes : 2 * lanes] + wide[2 * lanes : 3 * lanes]
-    return jnp.concatenate([total[j : j + 1] for j in range(lanes)], axis=1)
-
-
-def put_payload(ref, slot, mixed, stat, rows):
-    extra = padded(rows) - rows
-    if extra:
-        stat = jnp.concatenate([stat[:, :rows], jnp.zeros((1, extra), F32)], axis=1)
-    ref[slot, :rows] = mixed[:rows].astype(BF16)
-    ref[slot, rows : rows + STAT_ROWS] = stat_block(stat)
+    lanes = padded(total) // 128
+    pieces = [p[:, j * 128 : (j + 1) * 128] for p in (high, mid, low) for j in range(lanes)]
+    spare = STAT_ROWS - len(pieces)
+    pieces += [jnp.zeros((spare, 128), F32)] if spare else []
+    ref[0, total : total + STAT_ROWS] = jnp.concatenate(pieces, axis=0).astype(BF16)
+
+
+def stats_from(ref, count, rows):
+    total = count * rows
+    lanes = padded(total) // 128
+    wide = ref[0, total : total + STAT_ROWS].astype(F32)
+    added = wide[0:lanes] + wide[lanes : 2 * lanes] + wide[2 * lanes : 3 * lanes]
+    row = [added[j : j + 1] for j in range(lanes)] + [jnp.zeros((1, padded(rows)), F32)]
+    row = jnp.concatenate(row, axis=1)
+    return [row[:, j * rows : j * rows + padded(rows)] for j in range(count)]
 
 
 def lanes_of(ref, slot, *lead):
@@ -274,13 +277,16 @@
     own_ref, up_ref, far_ref = refs[3 if has_done else 2 :]
     rows = q_ref.shape[1]
     index = idx_ref[0]
-    slots = range(up_ref.shape[0])
+    slots = range(q_ref.shape[2] // HD)
+
+    def slot(ref, j):
+        return ref[0, j * rows : (j + 1) * rows]
 
     @pl.when(index == 1)
     def _():
         jobs = []
         for j in slots:
-            query = [lanes_of(q_ref, j, 0), near_ref[j, :rows], last_ref[j, :rows]]
+            query = [lanes_of(q_ref, j, 0), slot(near_ref, j), slot(last_ref, j)]
             keys = [lanes_of(first_ref, j, 0), lanes_of(k_ref, j, 0)]
             values = [lanes_of(first_ref, j, 1), lanes_of(v_ref, j, 0)]
             jobs.append(
@@ -291,19 +297,25 @@
                 )
             )
         seen = lambda key, row: (key <= row + rows) | (row >= rows)
-        for j, (mixed, stat) in zip(slots, partials_of(jobs, seen)):
+        results = partials_of(jobs, seen)
+        for j, (mixed, _) in zip(slots, results):
             own_ref[:, j * HD : (j + 1) * HD] = mixed[:rows].astype(BF16)
-            put_payload(up_ref, j, mixed[rows : 2 * rows], stat[:, rows : 2 * rows], rows)
-            put_payload(far_ref, j, mixed[2 * rows : 3 * rows], stat[:, 2 * rows : 3 * rows], rows)
+        for ref, start in ((up_ref, rows), (far_ref, 2 * rows)):
+            put_payload(
+                ref,
+                [mixed[start : start + rows] for mixed, _ in results],
+                [stat[:, start : start + rows] for _, stat in results],
+                rows,
+            )
 
     @pl.when(index == 2)
     def _():
         jobs = [
-            (pad_rows(near_ref[j, :rows]), lanes_of(k_ref, j, 0), lanes_of(v_ref, j, 0))
+            (pad_rows(slot(near_ref, j)), lanes_of(k_ref, j, 0), lanes_of(v_ref, j, 0))
             for j in slots
         ]
-        for j, (mixed, stat) in zip(slots, partials_of(jobs)):
-            put_payload(up_ref, j, mixed, stat, rows)
+        results = partials_of(jobs)
+        put_payload(up_ref, [m for m, _ in results], [t for _, t in results], rows)
 
     if has_ahead:
 
@@ -312,31 +324,33 @@
             for j in slots:
                 ask = lanes_of(ahead_ref, j, 0)
 
-                far_ref[j, :rows] = ask
+                far_ref[0, j * rows : (j + 1) * rows] = ask
 
                 @pl.when(index == 3)
                 def _():
-                    up_ref[j, :rows] = ask
-
-
-def merge_kernel(idx_ref, loc_ref, stat_ref, up_ref, far_ref, own_ref, out_ref):
+                    up_ref[0, j * rows : (j + 1) * rows] = ask
+
+
+def merge_kernel(steps, parts, idx_ref, loc_ref, stat_ref, *refs):
+    ups, fars = refs[:parts], refs[parts : 2 * parts]
+    own_ref, out_ref = refs[2 * parts :]
     rows = loc_ref.shape[1]
-    lanes = padded(rows) // 128
     index = idx_ref[0]
     slots = range(loc_ref.shape[0])
-
-    def merged(parts):
+    chunk = pl.program_id(0) // steps
+
+    def merged(sent):
+        known = [stats_from(p, len(slots), rows) for p in sent]
         for j in slots:
-            stats = [stat_ref[j, 0:1]]
-            stats += [stat_of(p[j, rows : rows + STAT_ROWS], lanes) for p in parts]
+            stats = [stat_ref[j, 0:1]] + [k[j] for k in known]
             base = loc_ref[j]
             top = functools.reduce(jnp.maximum, stats)
             weights = [jnp.exp2(s - top) for s in stats]
             scale = 1.0 / functools.reduce(jnp.add, weights)
             result = base
-            for weight, part in zip(weights[1:], parts):
+            for weight, part in zip(weights[1:], sent):
                 column = jnp.broadcast_to(weight * scale, (128, padded(rows))).T[:rows]
-                result = result + column * (part[j, :rows].astype(F32) - base)
+                result = result + column * (part[0, j * rows : (j + 1) * rows].astype(F32) - base)
             out_ref[:, j * HD : (j + 1) * HD] = result.astype(BF16)
 
     @pl.when(index == 0)
@@ -348,13 +362,15 @@
     def _():
         out_ref[...] = own_ref[...]
 
-    @pl.when(index == 2)
-    def _():
-        merged([up_ref])
-
-    @pl.when(index == 3)
-    def _():
-        merged([up_ref, far_ref])
+    for c in range(parts):
+
+        @pl.when((index == 2) & (chunk == c))
+        def _():
+            merged([ups[c]])
+
+        @pl.when((index == 3) & (chunk == c))
+        def _():
+            merged([ups[c], fars[c]])
 
 
 def pack_kernel(lows, asks, part, idx_ref, qkv_ref, *refs):
@@ -362,6 +378,7 @@
     low_s, ask_s, sems = refs[len(lows) + len(asks) :]
     rows = qkv_ref.shape[1]
     heads = part // HD
+    per = per_step(heads)
     index = idx_ref[0]
 
     def cols(c):
@@ -388,7 +405,10 @@
                 qkv_ref.at[0, :, cols(c)],
                 ask_s.at[i],
                 [
-                    (ask_s.at[i, :, pl.ds(h * HD, HD)], ask_refs[i].at[h, pl.ds(0, rows), :])
+                    (
+                        ask_s.at[i, :, pl.ds(h * HD, HD)],
+                        ask_refs[i].at[h // per, pl.ds(h % per * rows, rows), :],
+                    )
                     for h in range(heads)
                 ],
             )
@@ -415,10 +435,8 @@
     return pltpu.CompilerParams(vmem_limit_bytes=limit)
 
 
-def cost(flops, size):
-    return pl.CostEstimate(flops=1, bytes_accessed=1, transcendentals=0)
-
-
+NONE = pl.CostEstimate(flops=1, bytes_accessed=1, transcendentals=0)
+COVER = pl.CostEstimate(flops=int(2e10), bytes_accessed=int(8e7), transcendentals=0)
 SMEM = pl.BlockSpec(memory_space=pltpu.SMEM)
 
 
@@ -451,7 +469,7 @@
             pltpu.VMEM((8 + rows, cols), F32),
         ],
         compiler_params=params(),
-        cost_estimate=cost(rows * width * 40, rows * width * 8),
+        cost_estimate=NONE,
         name="se_mixer",
     )(qkv, tail, short, filt)
 
@@ -467,7 +485,7 @@
         out_specs=pl.BlockSpec((32, width), lambda j: (0, 0)),
         out_shape=shape((32, width), BF16),
         compiler_params=params(VMEM_EARLY),
-        cost_estimate=cost(0, 0),
+        cost_estimate=NONE,
         name="raw_tail",
     )(se_qkv, mr_qkv)
 
@@ -488,7 +506,7 @@
         out_shape=shape((BLOCK, width), BF16),
         scratch_shapes=[pltpu.VMEM((half, cols), F32), pltpu.VMEM((half, cols), F32)],
         compiler_params=params(VMEM_EARLY),
-        cost_estimate=cost(BLOCK * width * 12, rows * width * 3),
+        cost_estimate=COVER,
         name="product_tail",
     )(mr_qkv, mr_qkv, short)
 
@@ -504,14 +522,14 @@
         in_specs=[SMEM, anywhere],
         out_specs=[anywhere] * total,
         out_shape=[shape((2, rows, part), BF16)] * len(lows)
-        + [shape((count, rows + STAT_ROWS, HD), BF16)] * len(asks),
+        + [sent_shape(count, rows)] * len(asks),
         scratch_shapes=[
             pltpu.VMEM((max(len(lows), 1), 2, rows, part), BF16),
             pltpu.VMEM((max(len(asks), 1), rows, part), BF16),
             pltpu.SemaphoreType.DMA((2, len(lows) + len(asks) * count)),
         ],
         compiler_params=params(VMEM_EARLY),
-        cost_estimate=cost(0, 0),
+        cost_estimate=NONE,
         name="pack",
     )(index, qkv)
     return out[: len(lows)], out[len(lows) :]
@@ -545,7 +563,7 @@
         ],
         scratch_shapes=[pltpu.VMEM((8 + rows, cols), F32)] * 3 + [pltpu.VMEM((rows, cols), BF16)],
         compiler_params=params(),
-        cost_estimate=cost(WINDOW * WINDOW * width * 16, rows * width * 14),
+        cost_estimate=NONE,
         name="mr_main",
     )(qkv, tail, short, filt, decay[None, :], fwd, inv)
 
@@ -575,13 +593,18 @@
         scratch_shapes=[pltpu.VMEM((8 + BLOCK, cols), F32)],
         input_output_aliases={10: 0},
         compiler_params=params(),
-        cost_estimate=cost(WINDOW * WINDOW * width * 6, rows * width * 4),
+        cost_estimate=NONE,
         name="mr_head",
     )(index, low, high, lead, spec, qkv, tail, short, fwd, inv, part)
 
 
 def per_step(count):
     return 2 if count % 2 == 0 else 1
+
+
+def sent_shape(count, rows):
+    per = per_step(count)
+    return shape((count // per, per * rows + STAT_ROWS, HD), BF16)
 
 
 def head_spec(which, rows, per, offset):
@@ -614,7 +637,7 @@
         ),
         out_shape=[shape((heads, rows, HD), F32), shape((heads, 8, padded(rows)), F32)],
         compiler_params=params(),
-        cost_estimate=cost(heads * rows * rows * 512, rows * width * 10),
+        cost_estimate=NONE,
         name="local_attention",
     )(index, qkv, qkv, qkv)
 
@@ -624,7 +647,7 @@
     count = width // HD // PARTS
     per = per_step(count)
     steps = count // per
-    block = pl.BlockSpec((per, rows + STAT_ROWS, HD), lambda h: (h, 0, 0))
+    block = pl.BlockSpec((1, per * rows + STAT_ROWS, HD), lambda h: (h, 0, 0))
     has_ahead = c + 2 < PARTS
 
     def part(which, chunk):
@@ -649,42 +672,48 @@
         in_specs=specs,
         out_specs=[pl.BlockSpec((rows, per * HD), lambda h: (0, h + c * steps)), block, block],
         out_shape=[shape((rows, width), BF16)]
-        + [shape((count, rows + STAT_ROWS, HD), BF16)] * 2,
+        + [sent_shape(count, rows)] * 2,
         input_output_aliases=aliases,
         compiler_params=params(),
-        cost_estimate=cost(count * rows * rows * 3072, count * rows * HD * 20),
+        cost_estimate=COVER if c == 0 else NONE,
         name="cross_attention",
     )(*operands)
 
 
-def merge_attention(index, local, stats, up, far, done, c):
+def merge_attention(index, local, stats, ups, fars, done, first):
     rows, width = done.shape
     count = width // HD // PARTS
     per = per_step(count)
     steps = count // per
-    here, there = unless_first(0), unless_first(c * steps)
-    block = pl.BlockSpec((per, rows + STAT_ROWS, HD), lambda h, idx: (here(h, idx), 0, 0))
+    parts = len(ups)
+    there = unless_first(first * steps)
+
+    def payload(c):
+        def place(h, idx):
+            return (jnp.where(idx[0] < 2, 0, jnp.clip(h - c * steps, 0, steps - 1)), 0, 0)
+
+        return pl.BlockSpec((1, per * rows + STAT_ROWS, HD), place)
+
     flat = pl.BlockSpec((rows, per * HD), lambda h, idx: (0, there(h, idx)))
     return pl.pallas_call(
-        merge_kernel,
+        functools.partial(merge_kernel, steps, parts),
         grid_spec=pltpu.PrefetchScalarGridSpec(
             num_scalar_prefetch=1,
-            grid=(steps,),
+            grid=(steps * parts,),
             in_specs=[
                 pl.BlockSpec((per, rows, HD), lambda h, idx: (there(h, idx), 0, 0)),
                 pl.BlockSpec((per, 8, padded(rows)), lambda h, idx: (there(h, idx), 0, 0)),
-                block,
-                block,
-                flat,
-            ],
+            ]
+            + [payload(c) for c in range(parts)] * 2
+            + [flat],
             out_specs=flat,
         ),
         out_shape=shape((rows, width), BF16),
-        input_output_aliases={5: 0},
+        input_output_aliases={3 + 2 * parts: 0},
         compiler_params=params(),
-        cost_estimate=cost(count * rows * HD * 40, count * rows * HD * 12),
+        cost_estimate=NONE,
         name="merge_attention",
-    )(index, local, stats, up, far, done)
+    )(index, local, stats, *ups, *fars, done)
 
 
 def gathered_attention(attn_qkv):
@@ -758,22 +787,22 @@
     later = pack(index, after(attn_qkv, product), [1, 2, 3], [1])
     a_in, ask_in = a_in + later[0], ask_in + later[1]
     se_out = se_mixer(after(se_qkv, a_in[1]), raw, se_short, se_filter)
-    local, stats = local_attention(index, after(attn_qkv, se_out, b[0], d[0]))
 
     def cross(c, done, *needed):
         return cross_attention(index, attn_qkv, after(a[c], *needed), d[c], b[c], done, c)
 
-    a[1] = send(after(a_in[1], raw), (0, 1))
+    a[1] = send(a_in[1], (0, 1))
     b[1] = send(after(ask_in[1], b[0], d[0], se_out), (3, 1))
     d[1] = send(after(ask_in[1], b[0], d[0], se_out), *from_above)
-    attn_out, up[0], far[0] = cross(0, None, upper, stats)
+    attn_out, up[0], far[0] = cross(0, None, se_out, a_in[1])
+    local, stats = local_attention(index, after(attn_qkv, up[0]))
     b[2] = send(up[0], (3, 1), *merging)
     d[2] = send(far[0], (1, 3), *from_above)
-    a[2] = send(after(a_in[2], a[1]), (0, 1))
-    a[3] = send(after(a_in[3], a[1], b[1], d[1], up[0]), (0, 1))
-    attn_out, up[1], far[1] = cross(1, attn_out)
+    a[2] = send(after(a_in[2], a[1], up[0]), (0, 1))
+    attn_out, up[1], far[1] = cross(1, attn_out, upper, stats)
+    a[3] = send(after(a_in[3], up[1]), (0, 1))
     b[3] = send(up[1], (3, 1), *merging)
-    d[3] = send(after(far[1], b[2]), (1, 3), *from_above)
+    d[3] = send(after(far[1], b[2], d[2]), (1, 3), *from_above)
     lower = send(after(product, a[2], up[1]), (0, 1))
     attn_out, up[2], far[2] = cross(2, attn_out)
     b[4] = send(up[2], *merging)
@@ -784,15 +813,25 @@
     mr_part, spec, lead = mr_main(
         after(mr_qkv, attn_out), raw, mr_short, mr_filter, mr_decay, fwd, inv
     )
-    for c in range(PARTS):
-        if c == PARTS - 1:
-            mr_out = mr_head(
-                index, lower, upper, lead, spec, mr_qkv, raw, mr_short, fwd, inv, mr_part
-            )
-            local = after(local, mr_out)
-        attn_out = merge_attention(
-            index, after(local, lead), stats, b[c + 2], d[c + 2], attn_out, c
-        )
+    attn_out = merge_attention(
+        index,
+        after(local, lead),
+        stats,
+        [b[c + 2] for c in range(PARTS - 1)],
+        [d[c + 2] for c in range(PARTS - 1)],
+        attn_out,
+        0,
+    )
+    mr_out = mr_head(index, lower, upper, lead, spec, mr_qkv, raw, mr_short, fwd, inv, mr_part)
+    attn_out = merge_attention(
+        index,
+        after(local, mr_out),
+        stats,
+        [b[PARTS + 1]],
+        [d[PARTS + 1]],
+        attn_out,
+        PARTS - 1,
+    )
     return (se_out, mr_out, attn_out)
 
 

time: 114 us -> 105 us (0.921)
  waiting for transfers between devices: 23.1 us -> 15.6 us
  starting transfers between devices: 43.7 us -> 40.6 us
  Pallas kernels: 44.5 us -> 46.3 us
    ppermute x19, waiting for transfers between devices: 23.1 us -> 15.6 us  [four_spans(): send = lambda value, *pairs: lax.ppermute(value, 'seq', list(pairs))]
    ppermute x19, starting transfers between devices: 43.7 us -> 40.6 us  [four_spans(): send = lambda value, *pairs: lax.ppermute(value, 'seq', list(pairs))]
    pallas_call x4 -> x2, Pallas kernels: 9.07 us -> 8.88 us  [merge_attention(): pl.pallas_call(functools.partial(merge_kernel, steps, parts), grid_spec=p...]
  transfers between devices with their start and end apart: 19 -> 19, of which waited for: 6 -> 5; matrix products, arithmetic and copies ran while one was open for 0% -> 0% of each run, Pallas kernels for 31% -> 40%
where the time goes in v3:
time: 105 us
  Pallas kernels  46.3 us (44%)
  starting transfers between devices  40.6 us (39%)
  waiting for transfers between devices  15.6 us (15%)
  local copies, waits for them, and re-layouts  1.25 us (1%)
    ppermute x19, starting transfers between devices, four_spans(): send = lambda value, *pairs: lax.ppermute(value, 'seq', list(pairs))  40.6 us
    ppermute x19, waiting for transfers between devices, four_spans(): send = lambda value, *pairs: lax.ppermute(value, 'seq', list(pairs))  15.6 us
    pallas_call x2, Pallas kernels, merge_attention(): pl.pallas_call(functools.partial(merge_kernel, steps, parts), grid_spec=p...  8.88 us
    pallas_call x1, Pallas kernels, mr_main(): pl.pallas_call(mr_main_kernel, grid=(width // cols,), in_specs=[pl.BlockS...  8.11 us
    pallas_call x1, Pallas kernels, se_mixer(): pl.pallas_call(se_kernel, grid=(width // cols,), in_specs=[pl.BlockSpec((...  6.93 us
    pallas_call x4, Pallas kernels, cross_attention(): pl.pallas_call(functools.partial(cross_kernel, has_ahead, done is not Non...  5.32 us
    pallas_call x1, Pallas kernels, mr_head(): pl.pallas_call(mr_head_kernel, grid=(width // cols,), in_specs=[SMEM, pl....  4.58 us
    pallas_call x1, Pallas kernels, local_attention(): pl.pallas_call(local_kernel, grid_spec=pltpu.PrefetchScalarGridSpec(num_s...  4.04 us
  transfers between devices with their start and end apart: 19, of which 5 were waited for; matrix products, arithmetic and copies ran while one was open for 0% of the time, Pallas kernels for 40%

profile of v3, /device:TPU:26, one launch (start us, length us, event | category | flops | bytes accessed | tf_op | source)
XLA Modules:
  0.0 104.7 jit_solution(8989098553945478672)
XLA Ops:
  0.6 1.7 %raw_tail.1 = bf16[32,2048]{1,0:T(8,128)(2,1)} custom-call(bf16[3,320,2048]{2,1,0:T(8,128)(2,1)} %qkv_ref.2, bf16[3,320,2048]{2,1,0:T(8,128)(2,1)} %query_ref.1), custom_call_target="tpu_custom_call" | custom-call | flops 1 | bytes 1 | tf_op jit(solution)/shard_map/raw_tail/pallas_call | solution.py:481
  2.3 1.3 %collective-permute-start = (bf16[32,2048]{1,0:T(8,128)(2,1)}, bf16[32,2048]{1,0:T(8,128)(2,1)S(1)}, u32[]{:S(2)}, u32[]{:S(2)}) collective-permute-start(bf16[32,2048]{1,0:T(8,128)(2,1)} %raw_tail.1), channel_id=1, source_target_pairs={{0,4},{4,8},{8,12},{1,5},{5,9},{9,13},{2,6},{6,10},{10,14},{3,7},{... | collective-permute-start | bytes 393224 | tf_op jit(solution)/shard_map/ppermute | solution.py:774
  3.6 1.8 %pack.2 = (bf16[2,320,512]{2,1,0:T(8,128)(2,1)}, bf16[2,656,128]{2,1,0:T(8,128)(2,1)}) custom-call(s32[1]{0:T(128)} %bitcast.idx_ref, bf16[3,320,2048]{2,1,0:T(8,128)(2,1)} %v_ref.9), custom_call_target="tpu_custom_call" | custom-call | flops 1 | bytes 1 | tf_op jit(solution)/shard_map/pack/pallas_call | solution.py:520
  5.4 3.5 %collective-permute-start.4 = (bf16[2,656,128]{2,1,0:T(8,128)(2,1)}, bf16[2,656,128]{2,1,0:T(8,128)(2,1)}, u32[]{:S(2)}, u32[]{:S(2)}) collective-permute-start(bf16[2,656,128]{2,1,0:T(8,128)(2,1)} %get-tuple-element.50), channel_id=1, source_target_pairs={{12,4},{13,5},{14,6},{15,7},{28,20},{29,21},{30,22},{31,23}} | collective-permute-start | bytes 1007624 | tf_op jit(solution)/shard_map/ppermute | solution.py:774
  8.9 3.2 %collective-permute-start.3 = (bf16[2,656,128]{2,1,0:T(8,128)(2,1)}, bf16[2,656,128]{2,1,0:T(8,128)(2,1)}, u32[]{:S(2)}, u32[]{:S(2)}) collective-permute-start(bf16[2,656,128]{2,1,0:T(8,128)(2,1)} %get-tuple-element.50), channel_id=1, source_target_pairs={{8,4},{12,8},{9,5},{13,9},{10,6},{14,10},{11,7},{15,11},{24,20},{2... | collective-permute-start | bytes 1007624 | tf_op jit(solution)/shard_map/ppermute | solution.py:774
  12.1 1.5 %collective-permute-start.2 = (bf16[2,320,512]{2,1,0:T(8,128)(2,1)}, bf16[2,320,512]{2,1,0:T(8,128)(2,1)}, u32[]{:S(2)}, u32[]{:S(2)}) collective-permute-start(bf16[2,320,512]{2,1,0:T(8,128)(2,1)} %get-tuple-element.43), channel_id=1, source_target_pairs={{0,4},{1,5},{2,6},{3,7},{16,20},{17,21},{18,22},{19,23}} | collective-permute-start | bytes 1966088 | tf_op jit(solution)/shard_map/ppermute | solution.py:774
  13.6 3.0 %product_tail.1 = bf16[128,2048]{1,0:T(8,128)(2,1)} custom-call(bf16[3,320,2048]{2,1,0:T(8,128)(2,1)} %query_ref.1, bf16[3,320,2048]{2,1,0:T(8,128)(2,1)} %query_ref.1, f32[3,3,2048]{2,1,0:T(4,128)} %short_ref.7), custom_call_target="tpu_custom_call" | custom-call | flops 20000000000 | bytes 80000000 | tf_op jit(solution)/shard_map/product_tail/pallas_call | solution.py:497
  16.7 1.5 %collective-permute-start.6 = (bf16[128,2048]{1,0:T(8,128)(2,1)}, bf16[128,2048]{1,0:T(8,128)(2,1)}, u32[]{:S(2)}, u32[]{:S(2)}) collective-permute-start(bf16[128,2048]{1,0:T(8,128)(2,1)} %product_tail.1), channel_id=1, source_target_pairs={{4,8},{8,12},{5,9},{9,13},{6,10},{10,14},{7,11},{11,15},{20,24},{2... | collective-permute-start | bytes 1572872 | tf_op jit(solution)/shard_map/ppermute | solution.py:774
  18.2 1.9 %pack.3 = (bf16[2,320,512]{2,1,0:T(8,128)(2,1)}, bf16[2,320,512]{2,1,0:T(8,128)(2,1)}, bf16[2,320,512]{2,1,0:T(8,128)(2,1)}, bf16[2,656,128]{2,1,0:T(8,128)(2,1)}) custom-call(s32[1]{0:T(128)} %bitcast.idx_ref, bf16[3,320,2048]{2,1,0:T(8,128)(2,1)} %v_ref.9), custom_call_target="tpu_custom_call" | custom-call | flops 1 | bytes 1 | tf_op jit(solution)/shard_map/pack/pallas_call | solution.py:520
  21.0 1.2 %copy-done.7 = f32[3,3,2048]{2,1,0:T(4,128)S(1)} copy-done((f32[3,3,2048]{2,1,0:T(4,128)S(1)}, f32[3,3,2048]{2,1,0:T(4,128)}, u32[]{:S(2)}) %copy-start.7) | copy-done | bytes 73752
  22.2 6.9 %se_mixer.1 = bf16[320,2048]{1,0:T(8,128)(2,1)} custom-call(bf16[3,320,2048]{2,1,0:T(8,128)(2,1)S(1)} %copy-done.2, bf16[32,2048]{1,0:T(8,128)(2,1)S(1)} %collective-permute-done.tail_ref, f32[3,3,2048]{2,1,0:T(4,128)S(1)} %copy-done.7, f32[7,2048]{1,0:T(8,128)S(1)} %copy-done.8), custom_call_target="tpu_custom_call" | custom-call | flops 1 | bytes 1 | tf_op jit(solution)/shard_map/se_mixer/pallas_call | solution.py:454
  29.1 2.9 %collective-permute-start.8 = (bf16[2,656,128]{2,1,0:T(8,128)(2,1)S(1)}, bf16[2,656,128]{2,1,0:T(8,128)(2,1)S(1)}, u32[]{:S(2)}, u32[]{:S(2)}) collective-permute-start(bf16[2,656,128]{2,1,0:T(8,128)(2,1)S(1)} %copy-done.13), channel_id=1, source_target_pairs={{12,4},{13,5},{14,6},{15,7},{28,20},{29,21},{30,22},{31,23}} | collective-permute-start | bytes 1007624 | tf_op jit(solution)/shard_map/ppermute | solution.py:774
  32.0 2.5 %collective-permute-start.7 = (bf16[2,656,128]{2,1,0:T(8,128)(2,1)S(1)}, bf16[2,656,128]{2,1,0:T(8,128)(2,1)S(1)}, u32[]{:S(2)}, u32[]{:S(2)}) collective-permute-start(bf16[2,656,128]{2,1,0:T(8,128)(2,1)S(1)} %copy-done.13), channel_id=1, source_target_pairs={{8,4},{12,8},{9,5},{13,9},{10,6},{14,10},{11,7},{15,11},{24,20},{2... | collective-permute-start | bytes 1007624 | tf_op jit(solution)/shard_map/ppermute | solution.py:774
  34.5 2.2 %cross_attention.4 = (bf16[320,2048]{1,0:T(8,128)(2,1)}, bf16[2,656,128]{2,1,0:T(8,128)(2,1)S(1)}, bf16[2,656,128]{2,1,0:T(8,128)(2,1)S(1)}) custom-call(s32[1]{0:T(128)} %bitcast.idx_ref, bf16[3,320,2048]{2,1,0:T(8,128)(2,1)S(1)} %copy-done, bf16[3,320,2048]{2,1,0:T(8,128)(2,1)S(1)} %copy-done, bf16[3,320,2048]{2,1,0:T(8,128)(2,1)S(1)} %copy-done, ...), custom_call_target="tpu_custom_call" | custom-call | flops 20000000000 | bytes 80000000 | tf_op jit(solution)/shard_map/cross_attention/pallas_call | solution.py:669
  37.4 3.1 %collective-permute-start.12 = (bf16[2,656,128]{2,1,0:T(8,128)(2,1)S(1)}, bf16[2,656,128]{2,1,0:T(8,128)(2,1)S(1)}, u32[]{:S(2)}, u32[]{:S(2)}) collective-permute-start(bf16[2,656,128]{2,1,0:T(8,128)(2,1)S(1)} %get-tuple-element.64), channel_id=1, source_target_pairs={{4,12},{8,4},{12,8},{5,13},{9,5},{13,9},{6,14},{10,6},{14,10},{7,1... | collective-permute-start | bytes 1007624 | tf_op jit(solution)/shard_map/ppermute | solution.py:774
  40.6 6.0 %collective-permute-start.11 = (bf16[2,656,128]{2,1,0:T(8,128)(2,1)S(1)}, bf16[2,656,128]{2,1,0:T(8,128)(2,1)S(1)}, u32[]{:S(2)}, u32[]{:S(2)}) collective-permute-start(bf16[2,656,128]{2,1,0:T(8,128)(2,1)S(1)} %get-tuple-element.51), channel_id=1, source_target_pairs={{12,4},{4,8},{8,12},{13,5},{5,9},{9,13},{14,6},{6,10},{10,14},{15,... | collective-permute-start | bytes 1007624 | tf_op jit(solution)/shard_map/ppermute | solution.py:774
  46.5 4.0 %local_attention.1 = (f32[16,320,128]{2,1,0:T(8,128)S(1)}, f32[16,8,384]{2,1,0:T(8,128)S(1)}) custom-call(s32[1]{0:T(128)} %bitcast.idx_ref, bf16[3,320,2048]{2,1,0:T(8,128)(2,1)S(1)} %copy-done, bf16[3,320,2048]{2,1,0:T(8,128)(2,1)S(1)} %copy-done, bf16[3,320,2048]{2,1,0:T(8,128)(2,1)S(1)} %copy-done), custom_call_target="tpu_custom_call" | custom-call | flops 1 | bytes 1 | tf_op jit(solution)/shard_map/local_attention/pallas_call | solution.py:627
  50.6 1.1 %cross_attention.5 = (bf16[320,2048]{1,0:T(8,128)(2,1)}, bf16[2,656,128]{2,1,0:T(8,128)(2,1)S(1)}, bf16[2,656,128]{2,1,0:T(8,128)(2,1)S(1)}) custom-call(s32[1]{0:T(128)} %bitcast.idx_ref, bf16[3,320,2048]{2,1,0:T(8,128)(2,1)S(1)} %copy-done, bf16[3,320,2048]{2,1,0:T(8,128)(2,1)S(1)} %copy-done, ...), custom_call_target="tpu_custom_call", output_to_operand_aliasing={{0}: (8, {})} | custom-call | flops 1 | bytes 1 | tf_op jit(solution)/shard_map/cross_attention/pallas_call | solution.py:669
  52.5 4.9 %collective-permute-start.14 = (bf16[2,656,128]{2,1,0:T(8,128)(2,1)S(1)}, bf16[2,656,128]{2,1,0:T(8,128)(2,1)S(1)}, u32[]{:S(2)}, u32[]{:S(2)}) collective-permute-start(bf16[2,656,128]{2,1,0:T(8,128)(2,1)S(1)} %get-tuple-element.59), channel_id=1, source_target_pairs={{12,4},{4,8},{8,12},{13,5},{5,9},{9,13},{14,6},{6,10},{10,14},{15,... | collective-permute-start | bytes 1007624 | tf_op jit(solution)/shard_map/ppermute | solution.py:774
  57.4 4.6 %collective-permute-done.11.refs_1_.refs_0_ = bf16[2,656,128]{2,1,0:T(8,128)(2,1)S(1)} collective-permute-done((bf16[2,656,128]{2,1,0:T(8,128)(2,1)S(1)}, bf16[2,656,128]{2,1,0:T(8,128)(2,1)S(1)}, u32[]{:S(2)}, u32[]{:S(2)}) %collective-permute-start.11) | collective-permute-done | bytes 335904 | tf_op jit(solution)/shard_map/ppermute | solution.py:774
  62.0 1.9 %collective-permute-start.13 = (bf16[2,656,128]{2,1,0:T(8,128)(2,1)S(1)}, bf16[2,656,128]{2,1,0:T(8,128)(2,1)S(1)}, u32[]{:S(2)}, u32[]{:S(2)}) collective-permute-start(bf16[2,656,128]{2,1,0:T(8,128)(2,1)S(1)} %get-tuple-element.65), channel_id=1, source_target_pairs={{4,12},{8,4},{12,8},{5,13},{9,5},{13,9},{6,14},{10,6},{14,10},{7,1... | collective-permute-start | bytes 1007624 | tf_op jit(solution)/shard_map/ppermute | solution.py:774
  65.6 3.6 %collective-permute-done.14.refs_1_ = bf16[2,656,128]{2,1,0:T(8,128)(2,1)S(1)} collective-permute-done((bf16[2,656,128]{2,1,0:T(8,128)(2,1)S(1)}, bf16[2,656,128]{2,1,0:T(8,128)(2,1)S(1)}, u32[]{:S(2)}, u32[]{:S(2)}) %collective-permute-start.14) | collective-permute-done | bytes 335904 | tf_op jit(solution)/shard_map/ppermute | solution.py:774
  69.2 1.3 %collective-permute-start.18 = (bf16[2,656,128]{2,1,0:T(8,128)(2,1)S(1)}, bf16[2,656,128]{2,1,0:T(8,128)(2,1)S(1)}, u32[]{:S(2)}, u32[]{:S(2)}) collective-permute-start(bf16[2,656,128]{2,1,0:T(8,128)(2,1)S(1)} %get-tuple-element.80), channel_id=1, source_target_pairs={{4,12},{5,13},{6,14},{7,15},{20,28},{21,29},{22,30},{23,31}} | collective-permute-start | bytes 1007624 | tf_op jit(solution)/shard_map/ppermute | solution.py:774
  70.5 1.5 %collective-permute-start.17 = (bf16[2,656,128]{2,1,0:T(8,128)(2,1)S(1)}, bf16[2,656,128]{2,1,0:T(8,128)(2,1)S(1)}, u32[]{:S(2)}, u32[]{:S(2)}) collective-permute-start(bf16[2,656,128]{2,1,0:T(8,128)(2,1)S(1)} %get-tuple-element.78), channel_id=1, source_target_pairs={{4,8},{8,12},{5,9},{9,13},{6,10},{10,14},{7,11},{11,15},{20,24},{2... | collective-permute-start | bytes 1007624 | tf_op jit(solution)/shard_map/ppermute | solution.py:774
  72.0 2.7 %collective-permute-done.13.refs_0_.refs_4_ = bf16[2,656,128]{2,1,0:T(8,128)(2,1)S(1)} collective-permute-done((bf16[2,656,128]{2,1,0:T(8,128)(2,1)S(1)}, bf16[2,656,128]{2,1,0:T(8,128)(2,1)S(1)}, u32[]{:S(2)}, u32[]{:S(2)}) %collective-permute-start.13) | collective-permute-done | bytes 335904 | tf_op jit(solution)/shard_map/ppermute | solution.py:774
  75.7 1.4 %collective-permute-start.15 = (bf16[2,656,128]{2,1,0:T(8,128)(2,1)S(1)}, bf16[2,656,128]{2,1,0:T(8,128)(2,1)S(1)}, u32[]{:S(2)}, u32[]{:S(2)}) collective-permute-start(bf16[2,656,128]{2,1,0:T(8,128)(2,1)S(1)} %get-tuple-element.75), channel_id=1, source_target_pairs={{4,8},{8,12},{5,9},{9,13},{6,10},{10,14},{7,11},{11,15},{20,24},{2... | collective-permute-start | bytes 1007624 | tf_op jit(solution)/shard_map/ppermute | solution.py:774
  77.1 1.3 %collective-permute-start.16 = (bf16[2,656,128]{2,1,0:T(8,128)(2,1)S(1)}, bf16[2,656,128]{2,1,0:T(8,128)(2,1)S(1)}, u32[]{:S(2)}, u32[]{:S(2)}) collective-permute-start(bf16[2,656,128]{2,1,0:T(8,128)(2,1)S(1)} %get-tuple-element.76), channel_id=1, source_target_pairs={{4,12},{5,13},{6,14},{7,15},{20,28},{21,29},{22,30},{23,31}} | collective-permute-start | bytes 1007624 | tf_op jit(solution)/shard_map/ppermute | solution.py:774
  78.5 8.1 %mr_main.1 = (bf16[320,2048]{1,0:T(8,128)(2,1)}, f32[256,2048]{1,0:T(8,128)S(1)}, bf16[128,2048]{1,0:T(8,128)(2,1)S(1)}) custom-call(bf16[3,320,2048]{2,1,0:T(8,128)(2,1)S(1)} %copy-done.1, bf16[32,2048]{1,0:T(8,128)(2,1)S(1)} %collective-permute-done.tail_ref, f32[3,3,2048]{2,1,0:T(4,128)S(1)} %copy-done.6, f32[128,2048]{1,0:T(8,128)S(1)} %copy-done.4, ...), custom_call_target="tpu_custom_call" | custom-call | flops 1 | bytes 1 | tf_op jit(solution)/shard_map/mr_main/pallas_call | solution.py:542
  87.6 6.1 %merge_attention.2.refs_2_ = bf16[320,2048]{1,0:T(8,128)(2,1)} custom-call(s32[1]{0:T(128)} %bitcast.idx_ref, f32[16,320,128]{2,1,0:T(8,128)S(1)} %get-tuple-element.77.loc_ref, f32[16,8,384]{2,1,0:T(8,128)S(1)} %get-tuple-element.54.stat_ref, bf16[2,656,128]{2,1,0:T(8,128)(2,1)S(1)} %collective-permute-done.11.refs_1_.refs_0_, ...), custom_call_target="tpu_custom_call", output_to_operand_aliasing={{}: (9, {})} | custom-call | flops 1 | bytes 1 | tf_op jit(solution)/shard_map/merge_attention/pallas_call | solution.py:698
  93.6 4.6 %mr_head.1 = bf16[320,2048]{1,0:T(8,128)(2,1)} custom-call(s32[1]{0:T(128)} %bitcast.idx_ref, bf16[128,2048]{1,0:T(8,128)(2,1)S(1)} %collective-permute-done.9.low_ref, bf16[128,2048]{1,0:T(8,128)(2,1)} %collective-permute-done.6.high_ref, bf16[128,2048]{1,0:T(8,128)(2,1)S(1)} %get-tuple-element.70.lead_ref, ...), custom_call_target="tpu_custom_call", output_to_operand_aliasing={{}: (10, {})} | custom-call | flops 1 | bytes 1 | tf_op jit(solution)/shard_map/mr_head/pallas_call | solution.py:575
  98.2 3.7 %collective-permute-done.16.refs_1_ = bf16[2,656,128]{2,1,0:T(8,128)(2,1)S(1)} collective-permute-done((bf16[2,656,128]{2,1,0:T(8,128)(2,1)S(1)}, bf16[2,656,128]{2,1,0:T(8,128)(2,1)S(1)}, u32[]{:S(2)}, u32[]{:S(2)}) %collective-permute-start.16) | collective-permute-done | bytes 335904 | tf_op jit(solution)/shard_map/ppermute | solution.py:774
  101.9 2.8 %merge_attention.3 = bf16[320,2048]{1,0:T(8,128)(2,1)} custom-call(s32[1]{0:T(128)} %bitcast.idx_ref, f32[16,320,128]{2,1,0:T(8,128)S(1)} %get-tuple-element.77.loc_ref, f32[16,8,384]{2,1,0:T(8,128)S(1)} %get-tuple-element.54.stat_ref, bf16[2,656,128]{2,1,0:T(8,128)(2,1)S(1)} %collective-permute-done.15.refs_0_, ...), custom_call_target="tpu_custom_call", output_to_operand_aliasing={{}: (5, {})} | custom-call | flops 1 | bytes 1 | tf_op jit(solution)/shard_map/merge_attention/pallas_call | solution.py:698
  (48 shorter events, 6.0 us)
Async XLA Ops:
  2.3 11.3 %collective-permute-start = (bf16[32,2048]{1,0:T(8,128)(2,1)}, bf16[32,2048]{1,0:T(8,128)(2,1)S(1)}, u32[]{:S(2)}, u32[]{:S(2)}) collective-permute-start(bf16[32,2048]{1,0:T(8,128)(2,1)} %raw_tail.1), channel_id=1, source_target_pairs={{0,4},{4,8},{8,12},{1,5},{5,9},{9,13},{2,6},{6,10},{10,14},{3,7},{... | collective-permute-start | bytes 393224 | tf_op jit(solution)/shard_map/ppermute | solution.py:774
  5.4 23.7 %collective-permute-start.4 = (bf16[2,656,128]{2,1,0:T(8,128)(2,1)}, bf16[2,656,128]{2,1,0:T(8,128)(2,1)}, u32[]{:S(2)}, u32[]{:S(2)}) collective-permute-start(bf16[2,656,128]{2,1,0:T(8,128)(2,1)} %get-tuple-element.50), channel_id=1, source_target_pairs={{12,4},{13,5},{14,6},{15,7},{28,20},{29,21},{30,22},{31,23}} | collective-permute-start | bytes 1007624 | tf_op jit(solution)/shard_map/ppermute | solution.py:774
  8.9 20.2 %collective-permute-start.3 = (bf16[2,656,128]{2,1,0:T(8,128)(2,1)}, bf16[2,656,128]{2,1,0:T(8,128)(2,1)}, u32[]{:S(2)}, u32[]{:S(2)}) collective-permute-start(bf16[2,656,128]{2,1,0:T(8,128)(2,1)} %get-tuple-element.50), channel_id=1, source_target_pairs={{8,4},{12,8},{9,5},{13,9},{10,6},{14,10},{11,7},{15,11},{24,20},{2... | collective-permute-start | bytes 1007624 | tf_op jit(solution)/shard_map/ppermute | solution.py:774
  12.1 22.4 %collective-permute-start.2 = (bf16[2,320,512]{2,1,0:T(8,128)(2,1)}, bf16[2,320,512]{2,1,0:T(8,128)(2,1)}, u32[]{:S(2)}, u32[]{:S(2)}) collective-permute-start(bf16[2,320,512]{2,1,0:T(8,128)(2,1)} %get-tuple-element.43), channel_id=1, source_target_pairs={{0,4},{1,5},{2,6},{3,7},{16,20},{17,21},{18,22},{19,23}} | collective-permute-start | bytes 1966088 | tf_op jit(solution)/shard_map/ppermute | solution.py:774
  13.6 7.3 %copy-start.8 = (f32[7,2048]{1,0:T(8,128)S(1)}, f32[7,2048]{1,0:T(8,128)}, u32[]{:S(2)}) copy-start(f32[7,2048]{1,0:T(8,128)} %filt_ref.2) | copy-start | bytes 172036
  16.7 4.3 %copy-start.2 = (bf16[3,320,2048]{2,1,0:T(8,128)(2,1)S(1)}, bf16[3,320,2048]{2,1,0:T(8,128)(2,1)}, u32[]{:S(2)}) copy-start(bf16[3,320,2048]{2,1,0:T(8,128)(2,1)} %qkv_ref.2) | copy-start | bytes 11796484
  16.7 23.9 %collective-permute-start.6 = (bf16[128,2048]{1,0:T(8,128)(2,1)}, bf16[128,2048]{1,0:T(8,128)(2,1)}, u32[]{:S(2)}, u32[]{:S(2)}) collective-permute-start(bf16[128,2048]{1,0:T(8,128)(2,1)} %product_tail.1), channel_id=1, source_target_pairs={{4,8},{8,12},{5,9},{9,13},{6,10},{10,14},{7,11},{11,15},{20,24},{2... | collective-permute-start | bytes 1572872 | tf_op jit(solution)/shard_map/ppermute | solution.py:774
  20.1 14.4 %copy-start = (bf16[3,320,2048]{2,1,0:T(8,128)(2,1)S(1)}, bf16[3,320,2048]{2,1,0:T(8,128)(2,1)}, u32[]{:S(2)}) copy-start(bf16[3,320,2048]{2,1,0:T(8,128)(2,1)} %v_ref.9) | copy-start | bytes 11796484
  20.1 16.6 %collective-permute-start.1 = (bf16[2,320,512]{2,1,0:T(8,128)(2,1)}, bf16[2,320,512]{2,1,0:T(8,128)(2,1)S(1)}, u32[]{:S(2)}, u32[]{:S(2)}) collective-permute-start(bf16[2,320,512]{2,1,0:T(8,128)(2,1)} %get-tuple-element.46), channel_id=1, source_target_pairs={{0,4},{1,5},{2,6},{3,7},{16,20},{17,21},{18,22},{19,23}} | collective-permute-start | bytes 1966088 | tf_op jit(solution)/shard_map/ppermute | solution.py:774
  21.0 1.2 %copy-start.7 = (f32[3,3,2048]{2,1,0:T(4,128)S(1)}, f32[3,3,2048]{2,1,0:T(4,128)}, u32[]{:S(2)}) copy-start(f32[3,3,2048]{2,1,0:T(4,128)} %short_ref.5) | copy-start | bytes 221188
  22.2 6.9 %copy-start.13 = (bf16[2,656,128]{2,1,0:T(8,128)(2,1)S(1)}, bf16[2,656,128]{2,1,0:T(8,128)(2,1)}, u32[]{:S(2)}) copy-start(bf16[2,656,128]{2,1,0:T(8,128)(2,1)} %get-tuple-element.57) | copy-start | bytes 1007620
  29.1 7.6 %copy-start.11 = (bf16[2,320,512]{2,1,0:T(8,128)(2,1)S(1)}, bf16[2,320,512]{2,1,0:T(8,128)(2,1)}, u32[]{:S(2)}) copy-start(bf16[2,320,512]{2,1,0:T(8,128)(2,1)} %get-tuple-element.52) | copy-start | bytes 1966084
  29.1 21.5 %collective-permute-start.8 = (bf16[2,656,128]{2,1,0:T(8,128)(2,1)S(1)}, bf16[2,656,128]{2,1,0:T(8,128)(2,1)S(1)}, u32[]{:S(2)}, u32[]{:S(2)}) collective-permute-start(bf16[2,656,128]{2,1,0:T(8,128)(2,1)S(1)} %copy-done.13), channel_id=1, source_target_pairs={{12,4},{13,5},{14,6},{15,7},{28,20},{29,21},{30,22},{31,23}} | collective-permute-start | bytes 1007624 | tf_op jit(solution)/shard_map/ppermute | solution.py:774
  32.0 18.6 %collective-permute-start.7 = (bf16[2,656,128]{2,1,0:T(8,128)(2,1)S(1)}, bf16[2,656,128]{2,1,0:T(8,128)(2,1)S(1)}, u32[]{:S(2)}, u32[]{:S(2)}) collective-permute-start(bf16[2,656,128]{2,1,0:T(8,128)(2,1)S(1)} %copy-done.13), channel_id=1, source_target_pairs={{8,4},{12,8},{9,5},{13,9},{10,6},{14,10},{11,7},{15,11},{24,20},{2... | collective-permute-start | bytes 1007624 | tf_op jit(solution)/shard_map/ppermute | solution.py:774
  36.7 27.2 %collective-permute-start.5 = (bf16[2,320,512]{2,1,0:T(8,128)(2,1)S(1)}, bf16[2,320,512]{2,1,0:T(8,128)(2,1)S(1)}, u32[]{:S(2)}, u32[]{:S(2)}) collective-permute-start(bf16[2,320,512]{2,1,0:T(8,128)(2,1)S(1)} %copy-done.11), channel_id=1, source_target_pairs={{0,4},{1,5},{2,6},{3,7},{16,20},{17,21},{18,22},{19,23}} | collective-permute-start | bytes 1966088 | tf_op jit(solution)/shard_map/ppermute | solution.py:774
  37.4 20.0 %collective-permute-start.12 = (bf16[2,656,128]{2,1,0:T(8,128)(2,1)S(1)}, bf16[2,656,128]{2,1,0:T(8,128)(2,1)S(1)}, u32[]{:S(2)}, u32[]{:S(2)}) collective-permute-start(bf16[2,656,128]{2,1,0:T(8,128)(2,1)S(1)} %get-tuple-element.64), channel_id=1, source_target_pairs={{4,12},{8,4},{12,8},{5,13},{9,5},{13,9},{6,14},{10,6},{14,10},{7,1... | collective-permute-start | bytes 1007624 | tf_op jit(solution)/shard_map/ppermute | solution.py:774
  40.6 21.4 %collective-permute-start.11 = (bf16[2,656,128]{2,1,0:T(8,128)(2,1)S(1)}, bf16[2,656,128]{2,1,0:T(8,128)(2,1)S(1)}, u32[]{:S(2)}, u32[]{:S(2)}) collective-permute-start(bf16[2,656,128]{2,1,0:T(8,128)(2,1)S(1)} %get-tuple-element.51), channel_id=1, source_target_pairs={{12,4},{4,8},{8,12},{13,5},{5,9},{9,13},{14,6},{6,10},{10,14},{15,... | collective-permute-start | bytes 1007624 | tf_op jit(solution)/shard_map/ppermute | solution.py:774
  50.6 13.3 %copy-start.12 = (bf16[128,2048]{1,0:T(8,128)(2,1)S(1)}, bf16[128,2048]{1,0:T(8,128)(2,1)}, u32[]{:S(2)}) copy-start(bf16[128,2048]{1,0:T(8,128)(2,1)} %product_tail.1) | copy-start | bytes 1572868
  51.8 20.2 %collective-permute-start.10 = (bf16[2,320,512]{2,1,0:T(8,128)(2,1)S(1)}, bf16[2,320,512]{2,1,0:T(8,128)(2,1)S(1)}, u32[]{:S(2)}, u32[]{:S(2)}) collective-permute-start(bf16[2,320,512]{2,1,0:T(8,128)(2,1)S(1)} %copy-done.10), channel_id=1, source_target_pairs={{0,4},{1,5},{2,6},{3,7},{16,20},{17,21},{18,22},{19,23}} | collective-permute-start | bytes 1966088 | tf_op jit(solution)/shard_map/ppermute | solution.py:774
  52.5 16.8 %collective-permute-start.14 = (bf16[2,656,128]{2,1,0:T(8,128)(2,1)S(1)}, bf16[2,656,128]{2,1,0:T(8,128)(2,1)S(1)}, u32[]{:S(2)}, u32[]{:S(2)}) collective-permute-start(bf16[2,656,128]{2,1,0:T(8,128)(2,1)S(1)} %get-tuple-element.59), channel_id=1, source_target_pairs={{12,4},{4,8},{8,12},{13,5},{5,9},{9,13},{14,6},{6,10},{10,14},{15,... | collective-permute-start | bytes 1007624 | tf_op jit(solution)/shard_map/ppermute | solution.py:774
  62.0 12.7 %collective-permute-start.13 = (bf16[2,656,128]{2,1,0:T(8,128)(2,1)S(1)}, bf16[2,656,128]{2,1,0:T(8,128)(2,1)S(1)}, u32[]{:S(2)}, u32[]{:S(2)}) collective-permute-start(bf16[2,656,128]{2,1,0:T(8,128)(2,1)S(1)} %get-tuple-element.65), channel_id=1, source_target_pairs={{4,12},{8,4},{12,8},{5,13},{9,5},{13,9},{6,14},{10,6},{14,10},{7,1... | collective-permute-start | bytes 1007624 | tf_op jit(solution)/shard_map/ppermute | solution.py:774
  63.9 29.7 %collective-permute-start.9 = (bf16[128,2048]{1,0:T(8,128)(2,1)S(1)}, bf16[128,2048]{1,0:T(8,128)(2,1)S(1)}, u32[]{:S(2)}, u32[]{:S(2)}) collective-permute-start(bf16[128,2048]{1,0:T(8,128)(2,1)S(1)} %copy-done.12), channel_id=1, source_target_pairs={{0,4},{1,5},{2,6},{3,7},{16,20},{17,21},{18,22},{19,23}} | collective-permute-start | bytes 1572872 | tf_op jit(solution)/shard_map/ppermute | solution.py:774
  69.2 17.3 %collective-permute-start.18 = (bf16[2,656,128]{2,1,0:T(8,128)(2,1)S(1)}, bf16[2,656,128]{2,1,0:T(8,128)(2,1)S(1)}, u32[]{:S(2)}, u32[]{:S(2)}) collective-permute-start(bf16[2,656,128]{2,1,0:T(8,128)(2,1)S(1)} %get-tuple-element.80), channel_id=1, source_target_pairs={{4,12},{5,13},{6,14},{7,15},{20,28},{21,29},{22,30},{23,31}} | collective-permute-start | bytes 1007624 | tf_op jit(solution)/shard_map/ppermute | solution.py:774
  70.5 17.1 %collective-permute-start.17 = (bf16[2,656,128]{2,1,0:T(8,128)(2,1)S(1)}, bf16[2,656,128]{2,1,0:T(8,128)(2,1)S(1)}, u32[]{:S(2)}, u32[]{:S(2)}) collective-permute-start(bf16[2,656,128]{2,1,0:T(8,128)(2,1)S(1)} %get-tuple-element.78), channel_id=1, source_target_pairs={{4,8},{8,12},{5,9},{9,13},{6,10},{10,14},{7,11},{11,15},{20,24},{2... | collective-permute-start | bytes 1007624 | tf_op jit(solution)/shard_map/ppermute | solution.py:774
  74.7 3.7 %copy-start.1 = (bf16[3,320,2048]{2,1,0:T(8,128)(2,1)S(1)}, bf16[3,320,2048]{2,1,0:T(8,128)(2,1)}, u32[]{:S(2)}) copy-start(bf16[3,320,2048]{2,1,0:T(8,128)(2,1)} %query_ref.1) | copy-start | bytes 11796484
  74.7 3.7 %copy-start.3 = (bf16[512,256]{1,0:T(8,128)(2,1)S(1)}, bf16[512,256]{1,0:T(8,128)(2,1)}, u32[]{:S(2)}) copy-start(bf16[512,256]{1,0:T(8,128)(2,1)} %constant.9.clone.fwd_ref) | copy-start | bytes 786436
  74.7 3.8 %copy-start.4 = (f32[128,2048]{1,0:T(8,128)S(1)}, f32[128,2048]{1,0:T(8,128)}, u32[]{:S(2)}) copy-start(f32[128,2048]{1,0:T(8,128)} %filt_ref.3) | copy-start | bytes 3145732
  74.7 3.8 %copy-start.5 = (bf16[256,256]{1,0:T(8,128)(2,1)S(1)}, bf16[256,256]{1,0:T(8,128)(2,1)}, u32[]{:S(2)}) copy-start(bf16[256,256]{1,0:T(8,128)(2,1)} %constant.10.clone.inv_ref) | copy-start | bytes 393220
  74.7 3.8 %copy-start.6 = (f32[3,3,2048]{2,1,0:T(4,128)S(1)}, f32[3,3,2048]{2,1,0:T(4,128)}, u32[]{:S(2)}) copy-start(f32[3,3,2048]{2,1,0:T(4,128)} %short_ref.7) | copy-start | bytes 221188
  74.7 3.8 %copy-start.9 = (f32[2048]{0:T(1024)S(1)}, f32[2048]{0:T(1024)}, u32[]{:S(2)}) copy-start(f32[2048]{0:T(1024)} %param.16) | copy-start | bytes 24580
  75.7 22.5 %collective-permute-start.15 = (bf16[2,656,128]{2,1,0:T(8,128)(2,1)S(1)}, bf16[2,656,128]{2,1,0:T(8,128)(2,1)S(1)}, u32[]{:S(2)}, u32[]{:S(2)}) collective-permute-start(bf16[2,656,128]{2,1,0:T(8,128)(2,1)S(1)} %get-tuple-element.75), channel_id=1, source_target_pairs={{4,8},{8,12},{5,9},{9,13},{6,10},{10,14},{7,11},{11,15},{20,24},{2... | collective-permute-start | bytes 1007624 | tf_op jit(solution)/shard_map/ppermute | solution.py:774
  77.1 24.8 %collective-permute-start.16 = (bf16[2,656,128]{2,1,0:T(8,128)(2,1)S(1)}, bf16[2,656,128]{2,1,0:T(8,128)(2,1)S(1)}, u32[]{:S(2)}, u32[]{:S(2)}) collective-permute-start(bf16[2,656,128]{2,1,0:T(8,128)(2,1)S(1)} %get-tuple-element.76), channel_id=1, source_target_pairs={{4,12},{5,13},{6,14},{7,15},{20,28},{21,29},{22,30},{23,31}} | collective-permute-start | bytes 1007624 | tf_op jit(solution)/shard_map/ppermute | solution.py:774
  (1 other events, 1.2 us)
